TPU v7x, 512 devices: a whole 4x4x16 slice. The times are simulated.
512 devices in a mesh: tok: 64 (over y_hi, z, core), feat: 8 (over x, y_lo).
Axes of the slice: x: 4, y: 4 (y_hi: 2, y_lo: 2; y = y_hi * 2 + y_lo), z: 16, core: 2. Of those that a mesh axis runs over, the one named last changes fastest.
Arguments:
- activations: bfloat16 [32768, 16384], P('tok', 'feat'), may hold values from -300 to 300
- down_proj: bfloat16 [16384, 1024], P('feat', 'tok'), may hold values from -0.00024414062 to 0.00024414062
- precond: bfloat16 [1024, 1024], replicated, may hold values from -1 to 2, as said below
- target: bfloat16 [32768, 256], P('tok'), may hold values from -8 to 8
Outputs:
- solution: float32 [1024, 256], P('feat')
- residual: float32 [32768, 256], P('tok')
Inputs may be any that keep to these rules, and one draw needn't show every extreme that they name: `precond`: upper triangular.
All inputs are finite; a program needn't handle non-finite values.
Results may differ from a plain program's by a relative error of at most 0.025.
Values may be sent and summed in bfloat16 or wider, within the bound.
No kernel may reach another device: no remote copies, remote signals or barrier semaphores. Data moves between devices by JAX's collectives and lax.ppermute only.
A program may use at most 64 MiB of HBM per device.

v0:
```python
import jax
import jax.numpy as jnp
from jax import lax
from jax.experimental import pallas as pl
from jax.experimental.pallas import tpu as pltpu
from jax.sharding import Mesh, PartitionSpec as P

AXES = ("yhi", "z", "core", "x", "ylo")
TOK = ("yhi", "z", "core")
FEAT = ("x", "ylo")
BLOCK = 64
bf16 = jnp.bfloat16
f32 = jnp.float32
precise = lax.Precision.HIGHEST


def dot(a, b, ca, cb, precision=None):
    return lax.dot_general(
        a, b, (((ca,), (cb,)), ((), ())), precision=precision, preferred_element_type=f32
    )


def invert_block(d):
    n = d.shape[0]
    rows = lax.broadcasted_iota(jnp.int32, (n, n), 0)
    lanes = lax.broadcasted_iota(jnp.int32, (n, n), 1)
    lane1 = lax.broadcasted_iota(jnp.int32, (1, n), 1)
    for j in range(n):
        col = jnp.broadcast_to(d[:, j : j + 1], (n, n))
        pivot = 1.0 / col[j : j + 1, :]
        row = jnp.where(lane1 == j, pivot, d[j : j + 1, :] * pivot)
        kept = jnp.where((rows == j) | (lanes == j), 0.0, d)
        d = kept - jnp.where(rows == j, -1.0, col) * row
    return d


def invert_kernel(matrix_ref, out_ref):
    n = matrix_ref.shape[0]
    rows = lax.broadcasted_iota(jnp.int32, (n, BLOCK), 0)
    out_ref[...] = matrix_ref[...]
    for k in range(n // BLOCK):
        lo, hi = k * BLOCK, (k + 1) * BLOCK
        whole = out_ref[...]
        inverse = invert_block(whole[lo:hi, lo:hi])
        panel = dot(inverse, whole[lo:hi, :], 1, 0, precise)
        left = whole[:, lo:hi]
        inside = (rows >= lo) & (rows < hi)
        zeroed = jnp.where(inside, 0.0, left)
        update = whole - dot(zeroed, panel, 1, 0, precise)
        out_ref[...] = update
        out_ref[lo:hi, :] = panel
        out_ref[:, lo:hi] = -dot(zeroed, inverse, 1, 0, precise)
        out_ref[lo:hi, lo:hi] = inverse


def invert(matrix):
    return pl.pallas_call(
        invert_kernel,
        out_shape=jax.ShapeDtypeStruct(matrix.shape, f32),
        in_specs=[pl.BlockSpec(memory_space=pltpu.VMEM)],
        out_specs=pl.BlockSpec(memory_space=pltpu.VMEM),
        compiler_params=pltpu.CompilerParams(vmem_limit_bytes=16 * 1024 * 1024),
    )(matrix)


def swap(value, axis):
    return lax.ppermute(value, axis, [(0, 1), (1, 0)])


def ordered(first, mine, other):
    return jnp.where(first, mine, other), jnp.where(first, other, mine)


def gather_columns(down_t):
    nz, z_core = lax.axis_size("z"), ("z", "core")
    narrow, features = down_t.shape
    core = lax.axis_index("core")
    pair = jnp.concatenate(ordered(core == 0, down_t, swap(down_t, "core")))
    block = jnp.concatenate(ordered(lax.axis_index("yhi") == 0, pair, swap(pair, "yhi")))
    size = 4 * narrow
    ring = [(2 * z, 2 * ((z + 1) % nz)) for z in range(nz)]
    ring += [(2 * z + 1, 2 * ((z - 1) % nz) + 1) for z in range(nz)]
    held = jnp.zeros((nz * size, features), down_t.dtype)
    held = lax.dynamic_update_slice(held, block, (0, 0))
    moving = block
    for k in range(1, nz // 2):
        moving = lax.ppermute(moving, z_core, ring)
        offset = jnp.where(core == 0, nz - k, k)
        held = lax.dynamic_update_slice(held, moving, (offset * size, 0))
    half = size // 2
    far = nz // 2 * size + jnp.where(core == 0, half, 0)
    last = jnp.where(core == 0, moving[half:], moving[:half])
    held = lax.dynamic_update_slice(held, lax.ppermute(last, z_core, ring), (far, 0))
    count = nz // 2 * size - half
    here = jnp.where(core == 0, size + count, size)
    there = jnp.where(core == 0, size, size + count)
    sent = lax.dynamic_slice_in_dim(held, here, count, 0)
    return lax.dynamic_update_slice(held, swap(sent, "core"), (there, 0))


def gather_by_exchange(value, axes):
    n = lax.axis_size(axes)
    spread = jnp.broadcast_to(value[None], (n,) + value.shape)
    return lax.all_to_all(spread, axes, 0, 0, tiled=True)


def sum_by_exchange(value, axes):
    n = lax.axis_size(axes)
    parts = value.astype(bf16).reshape(n, value.shape[0] // n, value.shape[1])
    return jnp.sum(lax.all_to_all(parts, axes, 0, 0, tiled=True).astype(f32), axis=0)


def on_device(activations, down_proj, precond, target):
    tokens, features = activations.shape
    rank = precond.shape[0]
    nf, nz = lax.axis_size(FEAT), lax.axis_size("z")
    feat = lax.axis_index(FEAT)
    core = lax.axis_index("core")
    share = rank // nf
    narrow = down_proj.shape[1]

    columns_t = gather_columns(down_proj.T)
    partial_map = dot(activations, columns_t, 1, 1)

    rows = precond.reshape(2, nz, 2 * narrow, rank).transpose(1, 0, 2, 3).reshape(rank, rank)

    share_rel = sum_by_exchange(partial_map, FEAT).astype(bf16)
    start = rank - lax.axis_index("z") * (rank // nz)
    joined_share = lax.dynamic_slice_in_dim(
        jnp.concatenate([share_rel, share_rel], axis=1), start, rank, 1
    )
    joined = gather_by_exchange(joined_share, FEAT).reshape(tokens, rank)

    joined_slice = lax.dynamic_slice_in_dim(joined, feat * share, share, 1)
    total = dot(joined_slice, jnp.concatenate([joined, target], axis=1), 0, 0)
    width = total.shape[1]
    summed = sum_by_exchange(sum_by_exchange(total, ("core", "yhi")), "z").astype(bf16)
    summed = gather_by_exchange(summed, "z").reshape(share // 4, width)
    summed = gather_by_exchange(summed, ("x", "ylo", "yhi")).reshape(nf, share // 2, width)
    low, high = ordered(core == 0, summed, swap(summed, "core"))
    summed = jnp.stack([low, high], axis=1).reshape(rank, width)
    gram = summed[:, :rank]
    back = summed[:, rank:]

    own_rows = lax.dynamic_slice_in_dim(precond, feat * share, share, 0)
    descent = dot(rows, back, 0, 0)
    gram_now = dot(descent, descent, 0, 0, precise)
    direction = descent.astype(bf16)
    lift = dot(rows, direction, 1, 0)
    lift_b = lift.astype(bf16)
    image_back = dot(gram, lift_b, 1, 0)
    curvature = dot(lift_b.astype(f32), image_back, 0, 0, precise)
    inverse = invert(curvature)
    step = dot(inverse, gram_now, 1, 0, precise)
    coefficients = dot(lift, step, 1, 0, precise)
    solution = dot(dot(own_rows, direction, 1, 0), step, 1, 0, precise)

    back_next = back.astype(f32) - dot(image_back, step, 1, 0, precise)
    descent_next = dot(rows, back_next.astype(bf16), 0, 0)
    gram_next = dot(descent_next, descent_next, 0, 0, precise)
    curved = dot(rows.astype(f32), image_back, 0, 0, precise)
    mixing = -dot(inverse, dot(curved, descent_next, 0, 0, precise), 1, 0, precise)
    direction = (descent_next + dot(descent, mixing, 1, 0, precise)).astype(bf16)
    lift = dot(rows, direction, 1, 0)
    lift_b = lift.astype(bf16)
    image_back = dot(gram, lift_b, 1, 0)
    curvature = dot(lift_b.astype(f32), image_back, 0, 0, precise)
    step = dot(invert(curvature), gram_next, 1, 0, precise)
    coefficients = coefficients + dot(lift, step, 1, 0, precise)
    solution = solution + dot(dot(own_rows, direction, 1, 0), step, 1, 0, precise)
    residual = target.astype(f32) - dot(joined, coefficients.astype(bf16), 1, 0)
    return solution, residual


def solution(mesh):
    ntok, nfeat = mesh.devices.shape
    fine = Mesh(mesh.devices.reshape(2, ntok // 4, 2, nfeat // 2, 2), AXES)
    return jax.shard_map(
        on_device,
        mesh=fine,
        in_specs=(P(TOK, FEAT), P(FEAT, TOK), P(), P(TOK, None)),
        out_specs=(P(FEAT, None), P(TOK, None)),
        check_vma=False,
    )
```

profile of v0, /device:TPU:1, one launch (start us, length us, event | category | flops | bytes accessed | tf_op | source)
XLA Modules:
  0.0 304.5 jit_solution(15488502572289043888)
XLA Ops:
  0.6 8.9 %collective-permute-start = (bf16[16,2048]{1,0:T(8,128)(2,1)}, bf16[16,2048]{1,0:T(8,128)(2,1)S(1)}, u32[]{:S(2)}, u32[]{:S(2)}) collective-permute-start(bf16[16,2048]{1,0:T(8,128)(2,1)} %bitcast.80), channel_id=1, source_target_pairs={{0,8},{8,0},{1,9},{9,1},{2,10},{10,2},{3,11},{11,3},{4,12},{12,4},... | collective-permute-start | bytes 196616 | tf_op jit(solution)/shard_map/ppermute | solution.py:67
  13.5 6.2 %collective-permute-done.1 = bf16[32,2048]{1,0:T(8,128)(2,1)S(1)} collective-permute-done((bf16[32,2048]{1,0:T(8,128)(2,1)S(1)}, bf16[32,2048]{1,0:T(8,128)(2,1)S(1)}, u32[]{:S(2)}, u32[]{:S(2)}) %collective-permute-start.1) | collective-permute-done | bytes 131104 | tf_op jit(solution)/shard_map/ppermute | solution.py:67
  19.7 5.7 %collective-permute-start.2 = (bf16[64,2048]{1,0:T(8,128)(2,1)S(1)}, bf16[64,2048]{1,0:T(8,128)(2,1)S(1)}, u32[]{:S(2)}, u32[]{:S(2)}) collective-permute-start(bf16[64,2048]{1,0:T(8,128)(2,1)S(1)} %pad_maximum_fusion.1), channel_id=1, source_target_pairs={{0,16},{16,32},{32,48},{48,64},{64,80},{80,96},{96,112},{112,128},... | collective-permute-start | bytes 786440 | tf_op jit(solution)/shard_map/ppermute | solution.py:87
  25.5 3.3 %collective-permute-done.2 = bf16[64,2048]{1,0:T(8,128)(2,1)S(1)} collective-permute-done((bf16[64,2048]{1,0:T(8,128)(2,1)S(1)}, bf16[64,2048]{1,0:T(8,128)(2,1)S(1)}, u32[]{:S(2)}, u32[]{:S(2)}) %collective-permute-start.2) | collective-permute-done | bytes 262176 | tf_op jit(solution)/shard_map/ppermute | solution.py:87
  28.8 5.0 %collective-permute-start.3 = (bf16[64,2048]{1,0:T(8,128)(2,1)S(1)}, bf16[64,2048]{1,0:T(8,128)(2,1)S(1)}, u32[]{:S(2)}, u32[]{:S(2)}) collective-permute-start(bf16[64,2048]{1,0:T(8,128)(2,1)S(1)} %collective-permute-done.2), channel_id=1, source_target_pairs={{0,16},{16,32},{32,48},{48,64},{64,80},{80,96},{96,112},{112,128},... | collective-permute-start | bytes 786440 | tf_op jit(solution)/shard_map/ppermute | solution.py:87
  33.8 3.3 %collective-permute-done.3 = bf16[64,2048]{1,0:T(8,128)(2,1)S(1)} collective-permute-done((bf16[64,2048]{1,0:T(8,128)(2,1)S(1)}, bf16[64,2048]{1,0:T(8,128)(2,1)S(1)}, u32[]{:S(2)}, u32[]{:S(2)}) %collective-permute-start.3) | collective-permute-done | bytes 262176 | tf_op jit(solution)/shard_map/ppermute | solution.py:87
  37.1 5.0 %collective-permute-start.4 = (bf16[64,2048]{1,0:T(8,128)(2,1)S(1)}, bf16[64,2048]{1,0:T(8,128)(2,1)S(1)}, u32[]{:S(2)}, u32[]{:S(2)}) collective-permute-start(bf16[64,2048]{1,0:T(8,128)(2,1)S(1)} %collective-permute-done.3), channel_id=1, source_target_pairs={{0,16},{16,32},{32,48},{48,64},{64,80},{80,96},{96,112},{112,128},... | collective-permute-start | bytes 786440 | tf_op jit(solution)/shard_map/ppermute | solution.py:87
  42.1 3.3 %collective-permute-done.4 = bf16[64,2048]{1,0:T(8,128)(2,1)S(1)} collective-permute-done((bf16[64,2048]{1,0:T(8,128)(2,1)S(1)}, bf16[64,2048]{1,0:T(8,128)(2,1)S(1)}, u32[]{:S(2)}, u32[]{:S(2)}) %collective-permute-start.4) | collective-permute-done | bytes 262176 | tf_op jit(solution)/shard_map/ppermute | solution.py:87
  45.4 5.0 %collective-permute-start.5 = (bf16[64,2048]{1,0:T(8,128)(2,1)S(1)}, bf16[64,2048]{1,0:T(8,128)(2,1)S(1)}, u32[]{:S(2)}, u32[]{:S(2)}) collective-permute-start(bf16[64,2048]{1,0:T(8,128)(2,1)S(1)} %collective-permute-done.4), channel_id=1, source_target_pairs={{0,16},{16,32},{32,48},{48,64},{64,80},{80,96},{96,112},{112,128},... | collective-permute-start | bytes 786440 | tf_op jit(solution)/shard_map/ppermute | solution.py:87
  51.0 2.8 collective-permute-done.5
  53.7 5.0 %collective-permute-start.6 = (bf16[64,2048]{1,0:T(8,128)(2,1)S(1)}, bf16[64,2048]{1,0:T(8,128)(2,1)S(1)}, u32[]{:S(2)}, u32[]{:S(2)}) collective-permute-start(bf16[64,2048]{1,0:T(8,128)(2,1)S(1)} %collective-permute-done.5), channel_id=1, source_target_pairs={{0,16},{16,32},{32,48},{48,64},{64,80},{80,96},{96,112},{112,128},... | collective-permute-start | bytes 786440 | tf_op jit(solution)/shard_map/ppermute | solution.py:87
  58.8 3.2 %collective-permute-done.6 = bf16[64,2048]{1,0:T(8,128)(2,1)S(1)} collective-permute-done((bf16[64,2048]{1,0:T(8,128)(2,1)S(1)}, bf16[64,2048]{1,0:T(8,128)(2,1)S(1)}, u32[]{:S(2)}, u32[]{:S(2)}) %collective-permute-start.6) | collective-permute-done | bytes 262176 | tf_op jit(solution)/shard_map/ppermute | solution.py:87
  62.1 5.0 %collective-permute-start.7 = (bf16[64,2048]{1,0:T(8,128)(2,1)S(1)}, bf16[64,2048]{1,0:T(8,128)(2,1)S(1)}, u32[]{:S(2)}, u32[]{:S(2)}) collective-permute-start(bf16[64,2048]{1,0:T(8,128)(2,1)S(1)} %collective-permute-done.6), channel_id=1, source_target_pairs={{0,16},{16,32},{32,48},{48,64},{64,80},{80,96},{96,112},{112,128},... | collective-permute-start | bytes 786440 | tf_op jit(solution)/shard_map/ppermute | solution.py:87
  67.1 3.2 %collective-permute-done.7 = bf16[64,2048]{1,0:T(8,128)(2,1)S(1)} collective-permute-done((bf16[64,2048]{1,0:T(8,128)(2,1)S(1)}, bf16[64,2048]{1,0:T(8,128)(2,1)S(1)}, u32[]{:S(2)}, u32[]{:S(2)}) %collective-permute-start.7) | collective-permute-done | bytes 262176 | tf_op jit(solution)/shard_map/ppermute | solution.py:87
  70.4 5.0 %collective-permute-start.8 = (bf16[64,2048]{1,0:T(8,128)(2,1)S(1)}, bf16[64,2048]{1,0:T(8,128)(2,1)S(1)}, u32[]{:S(2)}, u32[]{:S(2)}) collective-permute-start(bf16[64,2048]{1,0:T(8,128)(2,1)S(1)} %collective-permute-done.7), channel_id=1, source_target_pairs={{0,16},{16,32},{32,48},{48,64},{64,80},{80,96},{96,112},{112,128},... | collective-permute-start | bytes 786440 | tf_op jit(solution)/shard_map/ppermute | solution.py:87
  75.5 3.2 %collective-permute-done.8 = bf16[64,2048]{1,0:T(8,128)(2,1)S(1)} collective-permute-done((bf16[64,2048]{1,0:T(8,128)(2,1)S(1)}, bf16[64,2048]{1,0:T(8,128)(2,1)S(1)}, u32[]{:S(2)}, u32[]{:S(2)}) %collective-permute-start.8) | collective-permute-done | bytes 262176 | tf_op jit(solution)/shard_map/ppermute | solution.py:87
  78.7 5.0 %collective-permute-start.9 = (bf16[32,2048]{1,0:T(8,128)(2,1)S(1)}, bf16[32,2048]{1,0:T(8,128)(2,1)S(1)}, u32[]{:S(2)}, u32[]{:S(2)}) collective-permute-start(bf16[32,2048]{1,0:T(8,128)(2,1)S(1)} %slice_select_fusion), channel_id=1, source_target_pairs={{0,16},{16,32},{32,48},{48,64},{64,80},{80,96},{96,112},{112,128},... | collective-permute-start | bytes 393224 | tf_op jit(solution)/shard_map/ppermute | solution.py:93
  89.1 12.4 %collective-permute-start.10 = (bf16[480,2048]{1,0:T(8,128)(2,1)}, bf16[480,2048]{1,0:T(8,128)(2,1)}, u32[]{:S(2)}, u32[]{:S(2)}) collective-permute-start(bf16[480,2048]{1,0:T(8,128)(2,1)} %constant_dynamic-slice_fusion), channel_id=1, source_target_pairs={{0,8},{8,0},{1,9},{9,1},{2,10},{10,2},{3,11},{11,3},{4,12},{12,4},... | collective-permute-start | bytes 5898248 | tf_op jit(solution)/shard_map/ppermute | solution.py:67
  101.5 3.9 %collective-permute-done.10 = bf16[480,2048]{1,0:T(8,128)(2,1)} collective-permute-done((bf16[480,2048]{1,0:T(8,128)(2,1)}, bf16[480,2048]{1,0:T(8,128)(2,1)}, u32[]{:S(2)}, u32[]{:S(2)}) %collective-permute-start.10) | collective-permute-done | bytes 1966112 | tf_op jit(solution)/shard_map/ppermute | solution.py:67
  105.4 3.0 %constant_dynamic-update-slice_fusion = bf16[1024,2048]{1,0:T(8,128)(2,1)} fusion(bf16[1024,2048]{1,0:T(8,128)(2,1)} %copy-done.1, bf16[480,2048]{1,0:T(8,128)(2,1)} %collective-permute-done.10, s32[]{:T(128)S(6)} %select_n.133), kind=kLoop, calls=%fused_computation.49 | loop fusion | bytes 3932164 | tf_op jit(solution)/shard_map/dynamic_update_slice | solution.py:98
  108.5 5.5 %convolution_convert_fusion.1 = bf16[1024,512]{0,1:T(8,128)(2,1)} fusion(bf16[1024,2048]{1,0:T(8,128)(2,1)} %constant_dynamic-update-slice_fusion, bf16[512,2048]{1,0:T(8,128)(2,1)S(1)} %copy-done), kind=kOutput, calls=%fused_computation.6 | convolution fusion | flops 2148007936 | bytes 7340032 | tf_op jit(solution)/shard_map/dot_general | solution.py:18
  114.0 5.0 %all-to-all-start = ((bf16[8,64,1024]{2,1,0:T(8,128)(2,1)}), bf16[8,64,1024]{2,1,0:T(8,128)(2,1)S(1)}, u32[]{:S(2)}, u32[]{:S(2)}) async-start(bf16[8,64,1024]{2,1,0:T(8,128)(2,1)} %bitcast.78), calls=%async_computation | async-start | bytes 2097152 | tf_op jit(solution)/shard_map/all_to_all | solution.py:110
  119.0 15.7 %all-to-all-done = bf16[8,64,1024]{2,1,0:T(8,128)(2,1)S(1)} async-done(((bf16[8,64,1024]{2,1,0:T(8,128)(2,1)}), bf16[8,64,1024]{2,1,0:T(8,128)(2,1)S(1)}, u32[]{:S(2)}, u32[]{:S(2)}) %all-to-all-start) | async-done | bytes 1048608 | tf_op jit(solution)/shard_map/all_to_all | solution.py:110
  136.1 3.6 %all-to-all-start.1 = ((bf16[8,64,1024]{2,1,0:T(8,128)(2,1)}), bf16[8,64,1024]{2,1,0:T(8,128)(2,1)S(1)}, u32[]{:S(2)}, u32[]{:S(2)}) async-start(bf16[8,64,1024]{2,1,0:T(8,128)(2,1)} %broadcast_in_dim.8), calls=%async_computation.1 | async-start | bytes 2097152 | tf_op jit(solution)/shard_map/all_to_all | solution.py:104
  139.7 14.6 %all-to-all-done.1 = bf16[8,64,1024]{2,1,0:T(8,128)(2,1)S(1)} async-done(((bf16[8,64,1024]{2,1,0:T(8,128)(2,1)}), bf16[8,64,1024]{2,1,0:T(8,128)(2,1)S(1)}, u32[]{:S(2)}, u32[]{:S(2)}) %all-to-all-start.1) | async-done | bytes 1048608 | tf_op jit(solution)/shard_map/all_to_all | solution.py:104
  154.7 13.4 %all_to_all.30 = bf16[4,32,1280]{2,1,0:T(8,128)(2,1)S(1)} all-to-all(bf16[4,32,1280]{2,1,0:T(8,128)(2,1)S(1)} %bitcast.79), channel_id=1, replica_groups=mesh['yhi'=2,'z'=16,'core'=2,'x'=4,'ylo'=2] {'core','yhi'}, dimensions={0} | all-to-all | bytes 655360 | tf_op jit(solution)/shard_map/all_to_all | solution.py:110
  168.1 20.3 %all_to_all.31 = bf16[16,2,1280]{2,1,0:T(2,128)(2,1)S(1)} all-to-all(bf16[16,2,1280]{2,1,0:T(2,128)(2,1)S(1)} %reshape.34), channel_id=1, replica_groups=mesh['yhi'=2,'z'=16,'core'=2,'x'=4,'ylo'=2] {'z'}, dimensions={0} | all-to-all | bytes 163840 | tf_op jit(solution)/shard_map/all_to_all | solution.py:110
  188.5 15.8 %all_to_all.32 = bf16[16,2,1280]{2,1,0:T(2,128)(2,1)S(1)} all-to-all(bf16[16,2,1280]{2,1,0:T(2,128)(2,1)S(1)} %broadcast_in_dim.9), channel_id=1, replica_groups=mesh['yhi'=2,'z'=16,'core'=2,'x'=4,'ylo'=2] {'z'}, dimensions={0} | all-to-all | bytes 163840 | tf_op jit(solution)/shard_map/all_to_all | solution.py:104
  204.5 20.6 %all_to_all.33 = bf16[16,32,1280]{2,1,0:T(8,128)(2,1)S(1)} all-to-all(bf16[16,32,1280]{2,1,0:T(8,128)(2,1)S(1)} %broadcast_in_dim.11), channel_id=1, replica_groups=mesh['yhi'=2,'z'=16,'core'=2,'x'=4,'ylo'=2] {'x','ylo','yhi'}, dimensions={0} | all-to-all | bytes 2621440 | tf_op jit(solution)/shard_map/all_to_all | solution.py:104
  225.2 5.5 %collective-permute-start.11 = (bf16[8,64,1280]{2,1,0:T(8,128)(2,1)S(1)}, bf16[8,64,1280]{2,1,0:T(8,128)(2,1)S(1)}, u32[]{:S(2)}, u32[]{:S(2)}) collective-permute-start(bf16[8,64,1280]{2,1,0:T(8,128)(2,1)S(1)} %bitcast.69), channel_id=1, source_target_pairs={{0,8},{8,0},{1,9},{9,1},{2,10},{10,2},{3,11},{11,3},{4,12},{12,4},... | collective-permute-start | bytes 3932168 | tf_op jit(solution)/shard_map/ppermute | solution.py:67
  237.2 24.8 %shard_map.59 = f32[256,256]{1,0:T(8,128)S(1)} custom-call(f32[256,256]{1,0:T(8,128)S(1)} %fusion.15.matrix_ref), custom_call_target="tpu_custom_call" | custom-call | tf_op jit(solution)/shard_map/pallas_call | solution.py:57
  274.6 25.0 %shard_map.60 = f32[256,256]{1,0:T(8,128)S(1)} custom-call(f32[256,256]{1,0:T(8,128)S(1)} %fusion.12.matrix_ref), custom_call_target="tpu_custom_call" | custom-call | tf_op jit(solution)/shard_map/pallas_call | solution.py:57
  (66 shorter events, 35.8 us)
Async XLA Ops:
  0.6 107.8 %copy-start = (bf16[512,2048]{1,0:T(8,128)(2,1)S(1)}, bf16[512,2048]{1,0:T(8,128)(2,1)}, u32[]{:S(2)}) copy-start(bf16[512,2048]{1,0:T(8,128)(2,1)} %param.4) | copy-start | bytes 6291460
  0.6 10.0 %collective-permute-start = (bf16[16,2048]{1,0:T(8,128)(2,1)}, bf16[16,2048]{1,0:T(8,128)(2,1)S(1)}, u32[]{:S(2)}, u32[]{:S(2)}) collective-permute-start(bf16[16,2048]{1,0:T(8,128)(2,1)} %bitcast.80), channel_id=1, source_target_pairs={{0,8},{8,0},{1,9},{9,1},{2,10},{10,2},{3,11},{11,3},{4,12},{12,4},... | collective-permute-start | bytes 196616 | tf_op jit(solution)/shard_map/ppermute | solution.py:67
  11.5 8.1 %collective-permute-start.1 = (bf16[32,2048]{1,0:T(8,128)(2,1)S(1)}, bf16[32,2048]{1,0:T(8,128)(2,1)S(1)}, u32[]{:S(2)}, u32[]{:S(2)}) collective-permute-start(bf16[32,2048]{1,0:T(8,128)(2,1)S(1)} %pad_maximum_fusion.2), channel_id=1, source_target_pairs={{0,256},{256,0},{1,257},{257,1},{2,258},{258,2},{3,259},{259,3},{4... | collective-permute-start | bytes 393224 | tf_op jit(solution)/shard_map/ppermute | solution.py:67
  19.7 9.1 %collective-permute-start.2 = (bf16[64,2048]{1,0:T(8,128)(2,1)S(1)}, bf16[64,2048]{1,0:T(8,128)(2,1)S(1)}, u32[]{:S(2)}, u32[]{:S(2)}) collective-permute-start(bf16[64,2048]{1,0:T(8,128)(2,1)S(1)} %pad_maximum_fusion.1), channel_id=1, source_target_pairs={{0,16},{16,32},{32,48},{48,64},{64,80},{80,96},{96,112},{112,128},... | collective-permute-start | bytes 786440 | tf_op jit(solution)/shard_map/ppermute | solution.py:87
  28.8 8.3 %collective-permute-start.3 = (bf16[64,2048]{1,0:T(8,128)(2,1)S(1)}, bf16[64,2048]{1,0:T(8,128)(2,1)S(1)}, u32[]{:S(2)}, u32[]{:S(2)}) collective-permute-start(bf16[64,2048]{1,0:T(8,128)(2,1)S(1)} %collective-permute-done.2), channel_id=1, source_target_pairs={{0,16},{16,32},{32,48},{48,64},{64,80},{80,96},{96,112},{112,128},... | collective-permute-start | bytes 786440 | tf_op jit(solution)/shard_map/ppermute | solution.py:87
  37.1 8.3 %collective-permute-start.4 = (bf16[64,2048]{1,0:T(8,128)(2,1)S(1)}, bf16[64,2048]{1,0:T(8,128)(2,1)S(1)}, u32[]{:S(2)}, u32[]{:S(2)}) collective-permute-start(bf16[64,2048]{1,0:T(8,128)(2,1)S(1)} %collective-permute-done.3), channel_id=1, source_target_pairs={{0,16},{16,32},{32,48},{48,64},{64,80},{80,96},{96,112},{112,128},... | collective-permute-start | bytes 786440 | tf_op jit(solution)/shard_map/ppermute | solution.py:87
  45.4 8.3 %collective-permute-start.5 = (bf16[64,2048]{1,0:T(8,128)(2,1)S(1)}, bf16[64,2048]{1,0:T(8,128)(2,1)S(1)}, u32[]{:S(2)}, u32[]{:S(2)}) collective-permute-start(bf16[64,2048]{1,0:T(8,128)(2,1)S(1)} %collective-permute-done.4), channel_id=1, source_target_pairs={{0,16},{16,32},{32,48},{48,64},{64,80},{80,96},{96,112},{112,128},... | collective-permute-start | bytes 786440 | tf_op jit(solution)/shard_map/ppermute | solution.py:87
  53.7 8.3 %collective-permute-start.6 = (bf16[64,2048]{1,0:T(8,128)(2,1)S(1)}, bf16[64,2048]{1,0:T(8,128)(2,1)S(1)}, u32[]{:S(2)}, u32[]{:S(2)}) collective-permute-start(bf16[64,2048]{1,0:T(8,128)(2,1)S(1)} %collective-permute-done.5), channel_id=1, source_target_pairs={{0,16},{16,32},{32,48},{48,64},{64,80},{80,96},{96,112},{112,128},... | collective-permute-start | bytes 786440 | tf_op jit(solution)/shard_map/ppermute | solution.py:87
  62.1 8.3 %collective-permute-start.7 = (bf16[64,2048]{1,0:T(8,128)(2,1)S(1)}, bf16[64,2048]{1,0:T(8,128)(2,1)S(1)}, u32[]{:S(2)}, u32[]{:S(2)}) collective-permute-start(bf16[64,2048]{1,0:T(8,128)(2,1)S(1)} %collective-permute-done.6), channel_id=1, source_target_pairs={{0,16},{16,32},{32,48},{48,64},{64,80},{80,96},{96,112},{112,128},... | collective-permute-start | bytes 786440 | tf_op jit(solution)/shard_map/ppermute | solution.py:87
  70.4 8.3 %collective-permute-start.8 = (bf16[64,2048]{1,0:T(8,128)(2,1)S(1)}, bf16[64,2048]{1,0:T(8,128)(2,1)S(1)}, u32[]{:S(2)}, u32[]{:S(2)}) collective-permute-start(bf16[64,2048]{1,0:T(8,128)(2,1)S(1)} %collective-permute-done.7), channel_id=1, source_target_pairs={{0,16},{16,32},{32,48},{48,64},{64,80},{80,96},{96,112},{112,128},... | collective-permute-start | bytes 786440 | tf_op jit(solution)/shard_map/ppermute | solution.py:87
  78.7 7.0 %collective-permute-start.9 = (bf16[32,2048]{1,0:T(8,128)(2,1)S(1)}, bf16[32,2048]{1,0:T(8,128)(2,1)S(1)}, u32[]{:S(2)}, u32[]{:S(2)}) collective-permute-start(bf16[32,2048]{1,0:T(8,128)(2,1)S(1)} %slice_select_fusion), channel_id=1, source_target_pairs={{0,16},{16,32},{32,48},{48,64},{64,80},{80,96},{96,112},{112,128},... | collective-permute-start | bytes 393224 | tf_op jit(solution)/shard_map/ppermute | solution.py:93
  85.7 2.0 copy-start.1
  89.1 16.3 %collective-permute-start.10 = (bf16[480,2048]{1,0:T(8,128)(2,1)}, bf16[480,2048]{1,0:T(8,128)(2,1)}, u32[]{:S(2)}, u32[]{:S(2)}) collective-permute-start(bf16[480,2048]{1,0:T(8,128)(2,1)} %constant_dynamic-slice_fusion), channel_id=1, source_target_pairs={{0,8},{8,0},{1,9},{9,1},{2,10},{10,2},{3,11},{11,3},{4,12},{12,4},... | collective-permute-start | bytes 5898248 | tf_op jit(solution)/shard_map/ppermute | solution.py:67
  114.0 20.7 %all-to-all-start = ((bf16[8,64,1024]{2,1,0:T(8,128)(2,1)}), bf16[8,64,1024]{2,1,0:T(8,128)(2,1)S(1)}, u32[]{:S(2)}, u32[]{:S(2)}) async-start(bf16[8,64,1024]{2,1,0:T(8,128)(2,1)} %bitcast.78), calls=%async_computation | async-start | bytes 2097152 | tf_op jit(solution)/shard_map/all_to_all | solution.py:110
  119.0 35.3 %copy-start.3 = (bf16[512,256]{1,0:T(8,128)(2,1)S(1)}, bf16[512,256]{1,0:T(8,128)(2,1)}, u32[]{:S(2)}) copy-start(bf16[512,256]{1,0:T(8,128)(2,1)} %param.7) | copy-start | bytes 786436
  136.1 18.1 %all-to-all-start.1 = ((bf16[8,64,1024]{2,1,0:T(8,128)(2,1)}), bf16[8,64,1024]{2,1,0:T(8,128)(2,1)S(1)}, u32[]{:S(2)}, u32[]{:S(2)}) async-start(bf16[8,64,1024]{2,1,0:T(8,128)(2,1)} %broadcast_in_dim.8), calls=%async_computation.1 | async-start | bytes 2097152 | tf_op jit(solution)/shard_map/all_to_all | solution.py:104
  204.4 26.3 %copy-start.2 = (bf16[1024,1024]{1,0:T(8,128)(2,1)S(1)}, bf16[1024,1024]{1,0:T(8,128)(2,1)}, u32[]{:S(2)}) copy-start(bf16[1024,1024]{1,0:T(8,128)(2,1)} %param.6) | copy-start | bytes 6291460
  225.2 7.6 %collective-permute-start.11 = (bf16[8,64,1280]{2,1,0:T(8,128)(2,1)S(1)}, bf16[8,64,1280]{2,1,0:T(8,128)(2,1)S(1)}, u32[]{:S(2)}, u32[]{:S(2)}) collective-permute-start(bf16[8,64,1280]{2,1,0:T(8,128)(2,1)S(1)} %bitcast.69), channel_id=1, source_target_pairs={{0,8},{8,0},{1,9},{9,1},{2,10},{10,2},{3,11},{11,3},{4,12},{12,4},... | collective-permute-start | bytes 3932168 | tf_op jit(solution)/shard_map/ppermute | solution.py:67
  274.6 27.2 %copy-start.4 = (bf16[512,256]{1,0:T(8,128)(2,1)S(1)}, bf16[512,256]{1,0:T(8,128)(2,1)}, u32[]{:S(2)}) copy-start(bf16[512,256]{1,0:T(8,128)(2,1)} %param.7) | copy-start | bytes 786436
where the time goes:
time: 310 us; the launch traced here: 305 us
  starting transfers between devices  78.1 us (25%)
  blocking collectives  70.1 us (23%)
  waiting for transfers between devices  67.5 us (22%)
  Pallas kernels  49.8 us (16%)
  matrix products  27 us (9%)
  local copies, waits for them, and re-layouts  8.76 us (3%)
    pallas_call x2, Pallas kernels, invert(): pl.pallas_call(invert_kernel, out_shape=jax.ShapeDtypeStruct(matrix.shape...  49.8 us
    all_to_all x2, blocking collectives, gather_by_exchange(): return lax.all_to_all(spread, axes, 0, 0, tiled=True)  36.5 us
    ppermute x7, starting transfers between devices, gather_columns(): moving = lax.ppermute(moving, z_core, ring)  35.8 us
    all_to_all x2, blocking collectives, sum_by_exchange(): lax.all_to_all(parts, axes, 0, 0, tiled=True).astype(f32)  33.6 us
    ppermute x4, starting transfers between devices, swap(): return lax.ppermute(value, axis, [(0, 1), (1, 0)])  28.7 us
    dot_general x26, matrix products, dot(): lax.dot_general(a, b, (((ca,), (cb,)), ((), ())), precision=precision, pr...  27 us
    ppermute x7, waiting for transfers between devices, gather_columns(): moving = lax.ppermute(moving, z_core, ring)  22.3 us
    all_to_all x1, waiting for transfers between devices, sum_by_exchange(): lax.all_to_all(parts, axes, 0, 0, tiled=True).astype(f32)  15.7 us
  transfers between devices with their start and end apart: 14, of which 14 were waited for; matrix products, arithmetic and copies ran while one was open for 0% of the time, Pallas kernels for 0%

commit v1 on v0

v1 whole, which is shorter than its diff:
```python
import jax
import jax.numpy as jnp
from jax import lax
from jax.experimental import pallas as pl
from jax.experimental.pallas import tpu as pltpu
from jax.sharding import Mesh, PartitionSpec as P

AXES = ("yhi", "z", "core", "x", "ylo")
TOK = ("yhi", "z", "core")
FEAT = ("x", "ylo")
BLOCK = 128
bf16 = jnp.bfloat16
f32 = jnp.float32
precise = lax.Precision.HIGHEST
three = lax.Precision.HIGH


def dot(a, b, ca, cb, precision=None):
    return lax.dot_general(
        a, b, (((ca,), (cb,)), ((), ())), precision=precision, preferred_element_type=f32
    )


def invert_block(d):
    n = d.shape[0]
    lanes = lax.broadcasted_iota(jnp.int32, (8, n), 1)
    subs = lax.broadcasted_iota(jnp.int32, (8, n), 0)

    def lane(v, j):
        return jnp.broadcast_to(v[:, j : j + 1], (8, n))

    def row(v, j):
        return jnp.broadcast_to(v[j : j + 1, :], (8, n))

    tiles = [d[i : i + 8, :] for i in range(0, n, 8)]
    count = len(tiles)
    for p in range(count):
        lo = 8 * p
        pivots = [lane(tiles[p], lo + k) for k in range(8)]
        for j in range(8):
            at = subs == j
            scale = 1.0 / row(pivots[j], j)
            minus = -pivots[j]
            fresh = []
            for k in range(8):
                if k == j:
                    fresh.append(jnp.where(at, scale, minus * scale))
                else:
                    scaled = row(pivots[k], j) * scale
                    fresh.append(jnp.where(at, scaled, pivots[k] + minus * scaled))
            pivots = fresh
        inside = (lanes >= lo) & (lanes < lo + 8)
        panel = jnp.where(inside, jnp.where(lanes - lo == subs, 1.0, 0.0), tiles[p])
        scaled = pivots[0] * row(panel, 0)
        for k in range(1, 8):
            scaled = scaled + pivots[k] * row(panel, k)
        rows = [row(scaled, k) for k in range(8)]
        for i in [(p + 1 + i) % count for i in range(count - 1)]:
            even = lane(tiles[i], lo) * rows[0]
            odd = lane(tiles[i], lo + 1) * rows[1]
            for k in range(2, 8, 2):
                even = even + lane(tiles[i], lo + k) * rows[k]
                odd = odd + lane(tiles[i], lo + k + 1) * rows[k + 1]
            tiles[i] = jnp.where(inside, 0.0, tiles[i]) - (even + odd)
        tiles[p] = scaled
    return jnp.concatenate(tiles, axis=0)


def invert_kernel(matrix_ref, out_ref):
    n = matrix_ref.shape[0]
    rows = lax.broadcasted_iota(jnp.int32, (n, BLOCK), 0)
    out_ref[...] = matrix_ref[...]
    for k in range(n // BLOCK):
        lo, hi = k * BLOCK, (k + 1) * BLOCK
        inverse = invert_block(out_ref[lo:hi, lo:hi])
        left = out_ref[:, lo:hi]
        zeroed = jnp.where((rows >= lo) & (rows < hi), 0.0, left)
        out_ref[lo:hi, :] = dot(inverse, out_ref[lo:hi, :], 1, 0, precise)
        out_ref[lo:hi, lo:hi] = inverse
        panel = out_ref[lo:hi, :]
        out_ref[lo:hi, :] = jnp.zeros_like(panel)
        out_ref[:, lo:hi] = jnp.zeros_like(left)
        out_ref[...] = out_ref[...] - dot(zeroed, panel, 1, 0, precise)
        out_ref[lo:hi, :] = panel


def invert(matrix):
    return pl.pallas_call(
        invert_kernel,
        out_shape=jax.ShapeDtypeStruct(matrix.shape, f32),
        in_specs=[pl.BlockSpec(memory_space=pltpu.VMEM)],
        out_specs=pl.BlockSpec(memory_space=pltpu.VMEM),
        compiler_params=pltpu.CompilerParams(vmem_limit_bytes=16 * 1024 * 1024),
    )(matrix)


def swap(value, axis):
    return lax.ppermute(value, axis, [(0, 1), (1, 0)])


def ordered(first, mine, other):
    return jnp.where(first, mine, other), jnp.where(first, other, mine)


def shift(value, axis, by):
    n = lax.axis_size(axis)
    return lax.ppermute(value, axis, [(i, (i + by) % n) for i in range(n)])


def gather_columns(down_t):
    low, high = ordered(lax.axis_index("yhi") == 0, down_t, swap(down_t, "yhi"))
    block = jnp.concatenate([low, high])
    narrow = down_t.shape[0]
    up, down = block, block
    below, above = [], []
    for k in range(1, lax.axis_size("z") // 2):
        up, down = shift(up, "z", 1), shift(down, "z", -1)
        below.append(up)
        above.append(down)
    last = [shift(up[:narrow], "z", 1), shift(down[narrow:], "z", -1)]
    return jnp.concatenate([block] + above + last + below[::-1])


def gather_by_exchange(value, axes):
    n = lax.axis_size(axes)
    spread = jnp.broadcast_to(value[None], (n,) + value.shape)
    return lax.all_to_all(spread, axes, 0, 0, tiled=True)


def sum_by_exchange(value, axes):
    n = lax.axis_size(axes)
    parts = value.astype(bf16).reshape(n, value.shape[0] // n, value.shape[1])
    return jnp.sum(lax.all_to_all(parts, axes, 0, 0, tiled=True).astype(f32), axis=0)


def on_device(activations, down_proj, precond, target):
    tokens, features = activations.shape
    rank = precond.shape[0]
    nf, nz = lax.axis_size(FEAT), lax.axis_size("z")
    feat = lax.axis_index(FEAT)
    core = lax.axis_index("core")
    share = rank // nf
    narrow = down_proj.shape[1]

    mine = gather_columns(down_proj.T)
    other = swap(mine, "core")
    map_mine = dot(activations, mine, 1, 1).astype(bf16)
    map_other = dot(activations, other, 1, 1).astype(bf16)
    partial_map = jnp.concatenate(ordered(core == 0, map_mine, map_other), axis=1)

    rows = precond.reshape(2, nz, 2, narrow, rank).transpose(2, 1, 0, 3, 4).reshape(rank, rank)

    share_rel = sum_by_exchange(partial_map, FEAT).astype(bf16)
    half = rank // 2
    start = half - lax.axis_index("z") * (half // nz)
    joined_share = jnp.concatenate(
        [
            lax.dynamic_slice_in_dim(jnp.concatenate([part, part], axis=1), start, half, 1)
            for part in (share_rel[:, :half], share_rel[:, half:])
        ],
        axis=1,
    )
    joined = gather_by_exchange(joined_share, FEAT).reshape(tokens, rank)

    joined_slice = lax.dynamic_slice_in_dim(joined, feat * share, share, 1)
    total = dot(joined_slice, jnp.concatenate([joined, target], axis=1), 0, 0)
    width = total.shape[1]
    summed = sum_by_exchange(sum_by_exchange(total, ("core", "yhi")), "z").astype(bf16)
    summed = gather_by_exchange(summed, "z").reshape(share // 4, width)
    summed = gather_by_exchange(summed, ("x", "ylo", "yhi")).reshape(nf, share // 2, width)
    low, high = ordered(core == 0, summed, swap(summed, "core"))
    summed = jnp.stack([low, high], axis=1).reshape(rank, width)
    gram = summed[:, :rank]
    back = summed[:, rank:]

    descent = dot(rows, back, 0, 0)
    gram_now = dot(descent, descent, 0, 0, three)
    lift = dot(rows, descent.astype(bf16), 1, 0)
    lift_b = lift.astype(bf16)
    image_back = dot(gram, lift_b, 1, 0)
    curvature = dot(lift_b.astype(f32), image_back, 0, 0, three)
    inverse = invert(curvature)
    step = dot(inverse, gram_now, 1, 0, three)

    coarse = image_back.astype(bf16)
    fine = (image_back - coarse.astype(f32)).astype(bf16)
    curved = dot(rows, coarse, 0, 0) + dot(rows, fine, 0, 0)
    descent_next = descent - dot(curved, step, 1, 0, three)
    gram_next = dot(descent_next, descent_next, 0, 0, three)
    mixing = dot(inverse, dot(curved, descent_next, 0, 0, three), 1, 0, three)
    direction = descent_next - dot(descent, mixing, 1, 0, three)
    lift_next = dot(rows, direction.astype(bf16), 1, 0)
    lift_b = lift_next.astype(bf16)
    curvature = dot(lift_b.astype(f32), dot(gram, lift_b, 1, 0), 0, 0, three)
    step_next = dot(invert(curvature), gram_next, 1, 0, three)

    coefficients = dot(lift, step, 1, 0, three) + dot(lift_next, step_next, 1, 0, three)
    residual = target.astype(f32) - dot(joined, coefficients.astype(bf16), 1, 0)
    part = nz * 2 // nf
    kept = coefficients.reshape(2, nz, 2, narrow, -1).transpose(2, 1, 0, 3, 4)
    kept = kept.reshape(nf, part, 2, narrow, -1)
    solution = lax.dynamic_index_in_dim(kept, feat, 0, keepdims=False).reshape(share, -1)
    return solution, residual


def solution(mesh):
    ntok, nfeat = mesh.devices.shape
    fine = Mesh(mesh.devices.reshape(2, ntok // 4, 2, nfeat // 2, 2), AXES)
    return jax.shard_map(
        on_device,
        mesh=fine,
        in_specs=(P(TOK, FEAT), P(FEAT, TOK), P(), P(TOK, None)),
        out_specs=(P(FEAT, None), P(TOK, None)),
        check_vma=False,
    )
```

time: 310 us -> 263 us (0.85); the launches traced: 305 us -> 262 us
  Pallas kernels: 49.8 us -> 18.9 us
  waiting for transfers between devices: 67.5 us -> 37.3 us
  starting transfers between devices: 78.1 us -> 90.1 us
  local copies, waits for them, and re-layouts: 8.76 us -> 18.6 us
  matrix products: 27 us -> 19.8 us
  other arithmetic: 1.84 us -> 5.27 us
    pallas_call x2, Pallas kernels: 49.8 us -> 18.9 us  [invert(): pl.pallas_call(invert_kernel, out_shape=jax.ShapeDtypeStruct(matrix.shape...]
    ppermute x8 -> x16, waiting for transfers between devices: 24.2 us -> 1.08 us  [shift(): return lax.ppermute(value, axis, [(i, (i + by) % n) for i in range(n)])]
    ppermute x8 -> x16, starting transfers between devices: 40.8 us -> 59.3 us  [shift(): return lax.ppermute(value, axis, [(i, (i + by) % n) for i in range(n)])]
    unnamed x10 -> x27, local copies, waits for them, and re-layouts: 1.97 us -> 11.2 us
    dot_general x26 -> x23, matrix products: 27 us -> 19.8 us  [dot(): lax.dot_general(a, b, (((ca,), (cb,)), ((), ())), precision=precision, pr...]
    ppermute x4 -> x3, waiting for transfers between devices: 13.1 us -> 5.95 us  [swap(): return lax.ppermute(value, axis, [(0, 1), (1, 0)])]
    ppermute x4 -> x3, starting transfers between devices: 28.7 us -> 22.2 us  [swap(): return lax.ppermute(value, axis, [(0, 1), (1, 0)])]
    dynamic_update_slice x10 -> x0, local copies, waits for them, and re-layouts: 3.74 us -> none  [the longest x1 3.05 us: gather_columns(): return lax.dynamic_update_slice(held, swap(sent, 'core'), (there, 0))]
  transfers between devices with their start and end apart: 14 -> 21, of which waited for: 14 -> 6; matrix products, arithmetic and copies ran while one was open for 0% -> 3% of each run, Pallas kernels for 0% -> 0%
where the time goes in v1:
time: 263 us; the launch traced here: 262 us
  starting transfers between devices  90.1 us (34%)
  blocking collectives  70.8 us (27%)
  waiting for transfers between devices  37.3 us (14%)
  matrix products  19.8 us (8%)
  Pallas kernels  18.9 us (7%)
  local copies, waits for them, and re-layouts  18.6 us (7%)
  other arithmetic  5.27 us (2%)
    ppermute x16, starting transfers between devices, shift(): return lax.ppermute(value, axis, [(i, (i + by) % n) for i in range(n)])  59.3 us
    all_to_all x2, blocking collectives, gather_by_exchange(): return lax.all_to_all(spread, axes, 0, 0, tiled=True)  36.3 us
    all_to_all x2, blocking collectives, sum_by_exchange(): lax.all_to_all(parts, axes, 0, 0, tiled=True).astype(f32)  34.5 us
    ppermute x3, starting transfers between devices, swap(): return lax.ppermute(value, axis, [(0, 1), (1, 0)])  22.2 us
    dot_general x23, matrix products, dot(): lax.dot_general(a, b, (((ca,), (cb,)), ((), ())), precision=precision, pr...  19.8 us
    pallas_call x2, Pallas kernels, invert(): pl.pallas_call(invert_kernel, out_shape=jax.ShapeDtypeStruct(matrix.shape...  18.9 us
    all_to_all x1, waiting for transfers between devices, sum_by_exchange(): lax.all_to_all(parts, axes, 0, 0, tiled=True).astype(f32)  15.7 us
    all_to_all x1, waiting for transfers between devices, gather_by_exchange(): return lax.all_to_all(spread, axes, 0, 0, tiled=True)  14.6 us
  transfers between devices with their start and end apart: 21, of which 6 were waited for; matrix products, arithmetic and copies ran while one was open for 3% of the time, Pallas kernels for 0%

profile of v1, /device:TPU:1, one launch (start us, length us, event | category | flops | bytes accessed | tf_op | source)
XLA Modules:
  0.0 261.9 jit_solution(11910315764233796314)
XLA Ops:
  0.6 5.8 %collective-permute-start = (bf16[16,2048]{1,0:T(8,128)(2,1)}, bf16[16,2048]{1,0:T(8,128)(2,1)S(1)}, u32[]{:S(2)}, u32[]{:S(2)}) collective-permute-start(bf16[16,2048]{1,0:T(8,128)(2,1)} %bitcast.95), channel_id=1, source_target_pairs={{0,256},{256,0},{1,257},{257,1},{2,258},{258,2},{3,259},{259,3},{4... | collective-permute-start | bytes 196616 | tf_op jit(solution)/shard_map/ppermute | solution.py:98
  11.3 3.6 %collective-permute-start.8 = (bf16[32,2048]{1,0:T(8,128)(2,1)S(1)}, bf16[32,2048]{1,0:T(8,128)(2,1)S(1)}, u32[]{:S(2)}, u32[]{:S(2)}) collective-permute-start(bf16[32,2048]{1,0:T(8,128)(2,1)S(1)} %pad_maximum_fusion.2), channel_id=1, source_target_pairs={{0,16},{16,32},{32,48},{48,64},{64,80},{80,96},{96,112},{112,128},... | collective-permute-start | bytes 393224 | tf_op jit(solution)/shard_map/ppermute | solution.py:107
  14.9 9.5 %collective-permute-start.1 = (bf16[32,2048]{1,0:T(8,128)(2,1)S(1)}, bf16[32,2048]{1,0:T(8,128)(2,1)S(1)}, u32[]{:S(2)}, u32[]{:S(2)}) collective-permute-start(bf16[32,2048]{1,0:T(8,128)(2,1)S(1)} %pad_maximum_fusion.2), channel_id=1, source_target_pairs={{0,240},{16,0},{32,16},{48,32},{64,48},{80,64},{96,80},{112,96},{1... | collective-permute-start | bytes 393224 | tf_op jit(solution)/shard_map/ppermute | solution.py:107
  24.8 1.9 collective-permute-start.9
  26.7 4.6 %collective-permute-start.2 = (bf16[32,2048]{1,0:T(8,128)(2,1)S(1)}, bf16[32,2048]{1,0:T(8,128)(2,1)S(1)}, u32[]{:S(2)}, u32[]{:S(2)}) collective-permute-start(bf16[32,2048]{1,0:T(8,128)(2,1)S(1)} %collective-permute-done.1), channel_id=1, source_target_pairs={{0,240},{16,0},{32,16},{48,32},{64,48},{80,64},{96,80},{112,96},{1... | collective-permute-start | bytes 393224 | tf_op jit(solution)/shard_map/ppermute | solution.py:107
  32.0 1.9 collective-permute-start.10
  33.9 4.6 %collective-permute-start.3 = (bf16[32,2048]{1,0:T(8,128)(2,1)S(1)}, bf16[32,2048]{1,0:T(8,128)(2,1)S(1)}, u32[]{:S(2)}, u32[]{:S(2)}) collective-permute-start(bf16[32,2048]{1,0:T(8,128)(2,1)S(1)} %collective-permute-done.2), channel_id=1, source_target_pairs={{0,240},{16,0},{32,16},{48,32},{64,48},{80,64},{96,80},{112,96},{1... | collective-permute-start | bytes 393224 | tf_op jit(solution)/shard_map/ppermute | solution.py:107
  39.1 1.9 collective-permute-start.11
  41.0 4.6 %collective-permute-start.4 = (bf16[32,2048]{1,0:T(8,128)(2,1)S(1)}, bf16[32,2048]{1,0:T(8,128)(2,1)S(1)}, u32[]{:S(2)}, u32[]{:S(2)}) collective-permute-start(bf16[32,2048]{1,0:T(8,128)(2,1)S(1)} %collective-permute-done.3), channel_id=1, source_target_pairs={{0,240},{16,0},{32,16},{48,32},{64,48},{80,64},{96,80},{112,96},{1... | collective-permute-start | bytes 393224 | tf_op jit(solution)/shard_map/ppermute | solution.py:107
  46.3 1.9 collective-permute-start.12
  48.2 4.6 %collective-permute-start.5 = (bf16[32,2048]{1,0:T(8,128)(2,1)S(1)}, bf16[32,2048]{1,0:T(8,128)(2,1)S(1)}, u32[]{:S(2)}, u32[]{:S(2)}) collective-permute-start(bf16[32,2048]{1,0:T(8,128)(2,1)S(1)} %collective-permute-done.4), channel_id=1, source_target_pairs={{0,240},{16,0},{32,16},{48,32},{64,48},{80,64},{96,80},{112,96},{1... | collective-permute-start | bytes 393224 | tf_op jit(solution)/shard_map/ppermute | solution.py:107
  53.5 1.9 collective-permute-start.13
  55.4 4.6 %collective-permute-start.6 = (bf16[32,2048]{1,0:T(8,128)(2,1)S(1)}, bf16[32,2048]{1,0:T(8,128)(2,1)S(1)}, u32[]{:S(2)}, u32[]{:S(2)}) collective-permute-start(bf16[32,2048]{1,0:T(8,128)(2,1)S(1)} %collective-permute-done.5), channel_id=1, source_target_pairs={{0,240},{16,0},{32,16},{48,32},{64,48},{80,64},{96,80},{112,96},{1... | collective-permute-start | bytes 393224 | tf_op jit(solution)/shard_map/ppermute | solution.py:107
  60.6 1.9 collective-permute-start.14
  62.6 4.6 %collective-permute-start.7 = (bf16[32,2048]{1,0:T(8,128)(2,1)S(1)}, bf16[32,2048]{1,0:T(8,128)(2,1)S(1)}, u32[]{:S(2)}, u32[]{:S(2)}) collective-permute-start(bf16[32,2048]{1,0:T(8,128)(2,1)S(1)} %collective-permute-done.6), channel_id=1, source_target_pairs={{0,240},{16,0},{32,16},{48,32},{64,48},{80,64},{96,80},{112,96},{1... | collective-permute-start | bytes 393224 | tf_op jit(solution)/shard_map/ppermute | solution.py:107
  70.5 5.3 %collective-permute-start.16 = (bf16[16,2048]{1,0:T(8,128)(2,1)S(1)}, bf16[16,2048]{1,0:T(8,128)(2,1)S(1)}, u32[]{:S(2)}, u32[]{:S(2)}) collective-permute-start(bf16[16,2048]{1,0:T(8,128)(2,1)S(1)} %slice.25), channel_id=1, source_target_pairs={{0,240},{16,0},{32,16},{48,32},{64,48},{80,64},{96,80},{112,96},{1... | collective-permute-start | bytes 196616 | tf_op jit(solution)/shard_map/ppermute | solution.py:107
  82.4 11.3 %collective-permute-start.17 = (bf16[512,2048]{1,0:T(8,128)(2,1)}, bf16[512,2048]{1,0:T(8,128)(2,1)}, u32[]{:S(2)}, u32[]{:S(2)}) collective-permute-start(bf16[512,2048]{1,0:T(8,128)(2,1)} %constant_dynamic-update-slice_fusion), channel_id=1, source_target_pairs={{0,8},{8,0},{1,9},{9,1},{2,10},{10,2},{3,11},{11,3},{4,12},{12,4},... | collective-permute-start | bytes 6291464 | tf_op jit(solution)/shard_map/ppermute | solution.py:98
  93.6 4.1 %collective-permute-done.17 = bf16[512,2048]{1,0:T(8,128)(2,1)} collective-permute-done((bf16[512,2048]{1,0:T(8,128)(2,1)}, bf16[512,2048]{1,0:T(8,128)(2,1)}, u32[]{:S(2)}, u32[]{:S(2)}) %collective-permute-start.17) | collective-permute-done | bytes 2097184 | tf_op jit(solution)/shard_map/ppermute | solution.py:98
  97.7 2.9 %convolution_convert_fusion.1 = bf16[512,512]{1,0:T(8,128)(2,1)S(1)} fusion(bf16[512,2048]{1,0:T(8,128)(2,1)} %collective-permute-done.17, bf16[512,2048]{1,0:T(8,128)(2,1)S(1)} %copy-done), kind=kOutput, calls=%fused_computation.15 | convolution fusion | flops 1074003968 | bytes 4718592 | tf_op jit(solution)/shard_map/dot_general | solution.py:19
  100.6 2.9 %select_bitcast_fusion.3 = (bf16[512,512]{0,1:T(8,128)(2,1)S(1)}, bf16[512,512]{0,1:T(8,128)(2,1)S(1)}) fusion(bf16[512,512]{1,0:T(8,128)(2,1)S(1)} %convolution_convert_fusion.1, pred[]{:T(512)S(6)} %eq.7, bf16[512,2048]{1,0:T(8,128)(2,1)} %constant_dynamic-update-slice_fusion, bf16[512,2048]{1,0:T(8,128)(2,1)S(1)} %copy-done), kind=kOutput, calls=%fused_computation.27 | convolution fusion | flops 1074528256 | bytes 5767169 | tf_op jit(solution)/shard_map/dot_general | solution.py:19
  104.9 5.0 %all-to-all-start = ((bf16[8,64,1024]{2,1,0:T(8,128)(2,1)}), bf16[8,64,1024]{2,1,0:T(8,128)(2,1)S(1)}, u32[]{:S(2)}, u32[]{:S(2)}) async-start(bf16[8,64,1024]{2,1,0:T(8,128)(2,1)} %bitcast.86), calls=%async_computation | async-start | bytes 2097152 | tf_op jit(solution)/shard_map/all_to_all | solution.py:133
  109.9 15.7 %all-to-all-done = bf16[8,64,1024]{2,1,0:T(8,128)(2,1)S(1)} async-done(((bf16[8,64,1024]{2,1,0:T(8,128)(2,1)}), bf16[8,64,1024]{2,1,0:T(8,128)(2,1)S(1)}, u32[]{:S(2)}, u32[]{:S(2)}) %all-to-all-start) | async-done | bytes 1048608 | tf_op jit(solution)/shard_map/all_to_all | solution.py:133
  127.2 3.6 %all-to-all-start.1 = ((bf16[8,64,1024]{2,1,0:T(8,128)(2,1)}), bf16[8,64,1024]{2,1,0:T(8,128)(2,1)S(1)}, u32[]{:S(2)}, u32[]{:S(2)}) async-start(bf16[8,64,1024]{2,1,0:T(8,128)(2,1)} %broadcast_in_dim.8), calls=%async_computation.1 | async-start | bytes 2097152 | tf_op jit(solution)/shard_map/all_to_all | solution.py:127
  130.8 14.6 %all-to-all-done.1 = bf16[8,64,1024]{2,1,0:T(8,128)(2,1)S(1)} async-done(((bf16[8,64,1024]{2,1,0:T(8,128)(2,1)}), bf16[8,64,1024]{2,1,0:T(8,128)(2,1)S(1)}, u32[]{:S(2)}, u32[]{:S(2)}) %all-to-all-start.1) | async-done | bytes 1048608 | tf_op jit(solution)/shard_map/all_to_all | solution.py:127
  145.7 13.3 %all_to_all.30 = bf16[4,32,1280]{2,1,0:T(8,128)(2,1)S(1)} all-to-all(bf16[4,32,1280]{2,1,0:T(8,128)(2,1)S(1)} %bitcast.94), channel_id=1, replica_groups=mesh['yhi'=2,'z'=16,'core'=2,'x'=4,'ylo'=2] {'core','yhi'}, dimensions={0} | all-to-all | bytes 655360 | tf_op jit(solution)/shard_map/all_to_all | solution.py:133
  159.2 21.2 %all_to_all.31 = bf16[16,2,1280]{2,1,0:T(2,128)(2,1)S(1)} all-to-all(bf16[16,2,1280]{2,1,0:T(2,128)(2,1)S(1)} %reshape.44), channel_id=1, replica_groups=mesh['yhi'=2,'z'=16,'core'=2,'x'=4,'ylo'=2] {'z'}, dimensions={0} | all-to-all | bytes 163840 | tf_op jit(solution)/shard_map/all_to_all | solution.py:133
  180.4 15.8 %all_to_all.32 = bf16[16,2,1280]{2,1,0:T(2,128)(2,1)S(1)} all-to-all(bf16[16,2,1280]{2,1,0:T(2,128)(2,1)S(1)} %broadcast_in_dim.9), channel_id=1, replica_groups=mesh['yhi'=2,'z'=16,'core'=2,'x'=4,'ylo'=2] {'z'}, dimensions={0} | all-to-all | bytes 163840 | tf_op jit(solution)/shard_map/all_to_all | solution.py:127
  196.4 20.5 %all_to_all.33 = bf16[16,32,1280]{2,1,0:T(8,128)(2,1)S(1)} all-to-all(bf16[16,32,1280]{2,1,0:T(8,128)(2,1)S(1)} %broadcast_in_dim.22), channel_id=1, replica_groups=mesh['yhi'=2,'z'=16,'core'=2,'x'=4,'ylo'=2] {'x','ylo','yhi'}, dimensions={0} | all-to-all | bytes 2621440 | tf_op jit(solution)/shard_map/all_to_all | solution.py:127
  216.9 5.2 %collective-permute-start.18 = (bf16[8,64,1280]{2,1,0:T(8,128)(2,1)S(1)}, bf16[8,64,1280]{2,1,0:T(8,128)(2,1)}, u32[]{:S(2)}, u32[]{:S(2)}) collective-permute-start(bf16[8,64,1280]{2,1,0:T(8,128)(2,1)S(1)} %bitcast.84), channel_id=1, source_target_pairs={{0,8},{8,0},{1,9},{9,1},{2,10},{10,2},{3,11},{11,3},{4,12},{12,4},... | collective-permute-start | bytes 3932168 | tf_op jit(solution)/shard_map/ppermute | solution.py:98
  222.1 3.2 %copy.26 = bf16[2,16,2,16,1024]{4,3,2,1,0:T(8,128)(2,1)} copy(bf16[2,16,2,16,1024]{4,3,0,1,2:T(8,128)(2,1)} %bitcast.92) | data formatting | bytes 4194304 | tf_op jit(solution)/shard_map/transpose | solution.py:151
  232.6 9.3 %shard_map.59 = f32[256,256]{1,0:T(8,128)S(1)} custom-call(f32[256,256]{1,0:T(8,128)S(1)} %fusion.18.matrix_ref), custom_call_target="tpu_custom_call" | custom-call | tf_op jit(solution)/shard_map/pallas_call | solution.py:88
  249.0 9.6 %shard_map.60 = f32[256,256]{1,0:T(8,128)S(1)} custom-call(f32[256,256]{1,0:T(8,128)S(1)} %fusion.12.matrix_ref), custom_call_target="tpu_custom_call" | custom-call | tf_op jit(solution)/shard_map/pallas_call | solution.py:88
  (90 shorter events, 39.5 us)
Async XLA Ops:
  0.6 97.1 %copy-start = (bf16[512,2048]{1,0:T(8,128)(2,1)S(1)}, bf16[512,2048]{1,0:T(8,128)(2,1)}, u32[]{:S(2)}) copy-start(bf16[512,2048]{1,0:T(8,128)(2,1)} %param.4) | copy-start | bytes 6291460
  0.6 7.6 %collective-permute-start = (bf16[16,2048]{1,0:T(8,128)(2,1)}, bf16[16,2048]{1,0:T(8,128)(2,1)S(1)}, u32[]{:S(2)}, u32[]{:S(2)}) collective-permute-start(bf16[16,2048]{1,0:T(8,128)(2,1)} %bitcast.95), channel_id=1, source_target_pairs={{0,256},{256,0},{1,257},{257,1},{2,258},{258,2},{3,259},{259,3},{4... | collective-permute-start | bytes 196616 | tf_op jit(solution)/shard_map/ppermute | solution.py:98
  11.3 13.5 %collective-permute-start.8 = (bf16[32,2048]{1,0:T(8,128)(2,1)S(1)}, bf16[32,2048]{1,0:T(8,128)(2,1)S(1)}, u32[]{:S(2)}, u32[]{:S(2)}) collective-permute-start(bf16[32,2048]{1,0:T(8,128)(2,1)S(1)} %pad_maximum_fusion.2), channel_id=1, source_target_pairs={{0,16},{16,32},{32,48},{48,64},{64,80},{80,96},{96,112},{112,128},... | collective-permute-start | bytes 393224 | tf_op jit(solution)/shard_map/ppermute | solution.py:107
  14.9 11.8 %collective-permute-start.1 = (bf16[32,2048]{1,0:T(8,128)(2,1)S(1)}, bf16[32,2048]{1,0:T(8,128)(2,1)S(1)}, u32[]{:S(2)}, u32[]{:S(2)}) collective-permute-start(bf16[32,2048]{1,0:T(8,128)(2,1)S(1)} %pad_maximum_fusion.2), channel_id=1, source_target_pairs={{0,240},{16,0},{32,16},{48,32},{64,48},{80,64},{96,80},{112,96},{1... | collective-permute-start | bytes 393224 | tf_op jit(solution)/shard_map/ppermute | solution.py:107
  24.8 7.2 %collective-permute-start.9 = (bf16[32,2048]{1,0:T(8,128)(2,1)S(1)}, bf16[32,2048]{1,0:T(8,128)(2,1)S(1)}, u32[]{:S(2)}, u32[]{:S(2)}) collective-permute-start(bf16[32,2048]{1,0:T(8,128)(2,1)S(1)} %collective-permute-done.8), channel_id=1, source_target_pairs={{0,16},{16,32},{32,48},{48,64},{64,80},{80,96},{96,112},{112,128},... | collective-permute-start | bytes 393224 | tf_op jit(solution)/shard_map/ppermute | solution.py:107
  26.7 7.2 %collective-permute-start.2 = (bf16[32,2048]{1,0:T(8,128)(2,1)S(1)}, bf16[32,2048]{1,0:T(8,128)(2,1)S(1)}, u32[]{:S(2)}, u32[]{:S(2)}) collective-permute-start(bf16[32,2048]{1,0:T(8,128)(2,1)S(1)} %collective-permute-done.1), channel_id=1, source_target_pairs={{0,240},{16,0},{32,16},{48,32},{64,48},{80,64},{96,80},{112,96},{1... | collective-permute-start | bytes 393224 | tf_op jit(solution)/shard_map/ppermute | solution.py:107
  32.0 7.2 %collective-permute-start.10 = (bf16[32,2048]{1,0:T(8,128)(2,1)S(1)}, bf16[32,2048]{1,0:T(8,128)(2,1)S(1)}, u32[]{:S(2)}, u32[]{:S(2)}) collective-permute-start(bf16[32,2048]{1,0:T(8,128)(2,1)S(1)} %collective-permute-done.9), channel_id=1, source_target_pairs={{0,16},{16,32},{32,48},{48,64},{64,80},{80,96},{96,112},{112,128},... | collective-permute-start | bytes 393224 | tf_op jit(solution)/shard_map/ppermute | solution.py:107
  33.9 7.2 %collective-permute-start.3 = (bf16[32,2048]{1,0:T(8,128)(2,1)S(1)}, bf16[32,2048]{1,0:T(8,128)(2,1)S(1)}, u32[]{:S(2)}, u32[]{:S(2)}) collective-permute-start(bf16[32,2048]{1,0:T(8,128)(2,1)S(1)} %collective-permute-done.2), channel_id=1, source_target_pairs={{0,240},{16,0},{32,16},{48,32},{64,48},{80,64},{96,80},{112,96},{1... | collective-permute-start | bytes 393224 | tf_op jit(solution)/shard_map/ppermute | solution.py:107
  39.1 7.2 %collective-permute-start.11 = (bf16[32,2048]{1,0:T(8,128)(2,1)S(1)}, bf16[32,2048]{1,0:T(8,128)(2,1)S(1)}, u32[]{:S(2)}, u32[]{:S(2)}) collective-permute-start(bf16[32,2048]{1,0:T(8,128)(2,1)S(1)} %collective-permute-done.10), channel_id=1, source_target_pairs={{0,16},{16,32},{32,48},{48,64},{64,80},{80,96},{96,112},{112,128},... | collective-permute-start | bytes 393224 | tf_op jit(solution)/shard_map/ppermute | solution.py:107
  41.0 7.2 %collective-permute-start.4 = (bf16[32,2048]{1,0:T(8,128)(2,1)S(1)}, bf16[32,2048]{1,0:T(8,128)(2,1)S(1)}, u32[]{:S(2)}, u32[]{:S(2)}) collective-permute-start(bf16[32,2048]{1,0:T(8,128)(2,1)S(1)} %collective-permute-done.3), channel_id=1, source_target_pairs={{0,240},{16,0},{32,16},{48,32},{64,48},{80,64},{96,80},{112,96},{1... | collective-permute-start | bytes 393224 | tf_op jit(solution)/shard_map/ppermute | solution.py:107
  46.3 7.2 %collective-permute-start.12 = (bf16[32,2048]{1,0:T(8,128)(2,1)S(1)}, bf16[32,2048]{1,0:T(8,128)(2,1)S(1)}, u32[]{:S(2)}, u32[]{:S(2)}) collective-permute-start(bf16[32,2048]{1,0:T(8,128)(2,1)S(1)} %collective-permute-done.11), channel_id=1, source_target_pairs={{0,16},{16,32},{32,48},{48,64},{64,80},{80,96},{96,112},{112,128},... | collective-permute-start | bytes 393224 | tf_op jit(solution)/shard_map/ppermute | solution.py:107
  48.2 7.2 %collective-permute-start.5 = (bf16[32,2048]{1,0:T(8,128)(2,1)S(1)}, bf16[32,2048]{1,0:T(8,128)(2,1)S(1)}, u32[]{:S(2)}, u32[]{:S(2)}) collective-permute-start(bf16[32,2048]{1,0:T(8,128)(2,1)S(1)} %collective-permute-done.4), channel_id=1, source_target_pairs={{0,240},{16,0},{32,16},{48,32},{64,48},{80,64},{96,80},{112,96},{1... | collective-permute-start | bytes 393224 | tf_op jit(solution)/shard_map/ppermute | solution.py:107
  53.5 7.2 %collective-permute-start.13 = (bf16[32,2048]{1,0:T(8,128)(2,1)S(1)}, bf16[32,2048]{1,0:T(8,128)(2,1)S(1)}, u32[]{:S(2)}, u32[]{:S(2)}) collective-permute-start(bf16[32,2048]{1,0:T(8,128)(2,1)S(1)} %collective-permute-done.12), channel_id=1, source_target_pairs={{0,16},{16,32},{32,48},{48,64},{64,80},{80,96},{96,112},{112,128},... | collective-permute-start | bytes 393224 | tf_op jit(solution)/shard_map/ppermute | solution.py:107
  55.4 7.2 %collective-permute-start.6 = (bf16[32,2048]{1,0:T(8,128)(2,1)S(1)}, bf16[32,2048]{1,0:T(8,128)(2,1)S(1)}, u32[]{:S(2)}, u32[]{:S(2)}) collective-permute-start(bf16[32,2048]{1,0:T(8,128)(2,1)S(1)} %collective-permute-done.5), channel_id=1, source_target_pairs={{0,240},{16,0},{32,16},{48,32},{64,48},{80,64},{96,80},{112,96},{1... | collective-permute-start | bytes 393224 | tf_op jit(solution)/shard_map/ppermute | solution.py:107
  60.6 7.9 %collective-permute-start.14 = (bf16[32,2048]{1,0:T(8,128)(2,1)S(1)}, bf16[32,2048]{1,0:T(8,128)(2,1)S(1)}, u32[]{:S(2)}, u32[]{:S(2)}) collective-permute-start(bf16[32,2048]{1,0:T(8,128)(2,1)S(1)} %collective-permute-done.13), channel_id=1, source_target_pairs={{0,16},{16,32},{32,48},{48,64},{64,80},{80,96},{96,112},{112,128},... | collective-permute-start | bytes 393224 | tf_op jit(solution)/shard_map/ppermute | solution.py:107
  62.6 7.9 %collective-permute-start.7 = (bf16[32,2048]{1,0:T(8,128)(2,1)S(1)}, bf16[32,2048]{1,0:T(8,128)(2,1)S(1)}, u32[]{:S(2)}, u32[]{:S(2)}) collective-permute-start(bf16[32,2048]{1,0:T(8,128)(2,1)S(1)} %collective-permute-done.6), channel_id=1, source_target_pairs={{0,240},{16,0},{32,16},{48,32},{64,48},{80,64},{96,80},{112,96},{1... | collective-permute-start | bytes 393224 | tf_op jit(solution)/shard_map/ppermute | solution.py:107
  68.5 7.9 %collective-permute-start.15 = (bf16[16,2048]{1,0:T(8,128)(2,1)S(1)}, bf16[16,2048]{1,0:T(8,128)(2,1)S(1)}, u32[]{:S(2)}, u32[]{:S(2)}) collective-permute-start(bf16[16,2048]{1,0:T(8,128)(2,1)S(1)} %slice.24), channel_id=1, source_target_pairs={{0,16},{16,32},{32,48},{48,64},{64,80},{80,96},{96,112},{112,128},... | collective-permute-start | bytes 196616 | tf_op jit(solution)/shard_map/ppermute | solution.py:107
  70.5 6.6 %collective-permute-start.16 = (bf16[16,2048]{1,0:T(8,128)(2,1)S(1)}, bf16[16,2048]{1,0:T(8,128)(2,1)S(1)}, u32[]{:S(2)}, u32[]{:S(2)}) collective-permute-start(bf16[16,2048]{1,0:T(8,128)(2,1)S(1)} %slice.25), channel_id=1, source_target_pairs={{0,240},{16,0},{32,16},{48,32},{64,48},{80,64},{96,80},{112,96},{1... | collective-permute-start | bytes 196616 | tf_op jit(solution)/shard_map/ppermute | solution.py:107
  82.4 15.4 %collective-permute-start.17 = (bf16[512,2048]{1,0:T(8,128)(2,1)}, bf16[512,2048]{1,0:T(8,128)(2,1)}, u32[]{:S(2)}, u32[]{:S(2)}) collective-permute-start(bf16[512,2048]{1,0:T(8,128)(2,1)} %constant_dynamic-update-slice_fusion), channel_id=1, source_target_pairs={{0,8},{8,0},{1,9},{9,1},{2,10},{10,2},{3,11},{11,3},{4,12},{12,4},... | collective-permute-start | bytes 6291464 | tf_op jit(solution)/shard_map/ppermute | solution.py:98
  104.9 20.8 %all-to-all-start = ((bf16[8,64,1024]{2,1,0:T(8,128)(2,1)}), bf16[8,64,1024]{2,1,0:T(8,128)(2,1)S(1)}, u32[]{:S(2)}, u32[]{:S(2)}) async-start(bf16[8,64,1024]{2,1,0:T(8,128)(2,1)} %bitcast.86), calls=%async_computation | async-start | bytes 2097152 | tf_op jit(solution)/shard_map/all_to_all | solution.py:133
  125.8 19.5 %copy-start.4 = (bf16[512,256]{1,0:T(8,128)(2,1)S(1)}, bf16[512,256]{1,0:T(8,128)(2,1)}, u32[]{:S(2)}) copy-start(bf16[512,256]{1,0:T(8,128)(2,1)} %param.7) | copy-start | bytes 786436
  127.2 18.1 %all-to-all-start.1 = ((bf16[8,64,1024]{2,1,0:T(8,128)(2,1)}), bf16[8,64,1024]{2,1,0:T(8,128)(2,1)S(1)}, u32[]{:S(2)}, u32[]{:S(2)}) async-start(bf16[8,64,1024]{2,1,0:T(8,128)(2,1)} %broadcast_in_dim.8), calls=%async_computation.1 | async-start | bytes 2097152 | tf_op jit(solution)/shard_map/all_to_all | solution.py:127
  145.4 50.9 %copy-start.2 = (bf16[8,64,1024]{2,1,0:T(8,128)(2,1)}, bf16[8,64,1024]{2,1,0:T(8,128)(2,1)S(1)}, u32[]{:S(2)}) copy-start(bf16[8,64,1024]{2,1,0:T(8,128)(2,1)S(1)} %all-to-all-done.1) | copy-start | bytes 3145732
  216.9 8.4 %collective-permute-start.18 = (bf16[8,64,1280]{2,1,0:T(8,128)(2,1)S(1)}, bf16[8,64,1280]{2,1,0:T(8,128)(2,1)}, u32[]{:S(2)}, u32[]{:S(2)}) collective-permute-start(bf16[8,64,1280]{2,1,0:T(8,128)(2,1)S(1)} %bitcast.84), channel_id=1, source_target_pairs={{0,8},{8,0},{1,9},{9,1},{2,10},{10,2},{3,11},{11,3},{4,12},{12,4},... | collective-permute-start | bytes 3932168 | tf_op jit(solution)/shard_map/ppermute | solution.py:98
  226.9 1.6 copy-start.1
  258.6 1.3 copy-start.3
  258.6 1.3 copy-start.5

commit v2 on v1

--- a/solution.py
+++ b/solution.py
@@ -108,17 +108,15 @@
 
 
 def gather_columns(down_t):
-    low, high = ordered(lax.axis_index("yhi") == 0, down_t, swap(down_t, "yhi"))
-    block = jnp.concatenate([low, high])
-    narrow = down_t.shape[0]
-    up, down = block, block
+    half = down_t.shape[0] // 2
+    up, down = down_t, down_t
     below, above = [], []
     for k in range(1, lax.axis_size("z") // 2):
         up, down = shift(up, "z", 1), shift(down, "z", -1)
         below.append(up)
         above.append(down)
-    last = [shift(up[:narrow], "z", 1), shift(down[narrow:], "z", -1)]
-    return jnp.concatenate([block] + above + last + below[::-1])
+    last = [shift(up[:half], "z", 1), shift(down[half:], "z", -1)]
+    return jnp.concatenate([down_t] + above + last + below[::-1])
 
 
 def gather_by_exchange(value, axes):
@@ -142,32 +140,42 @@
     share = rank // nf
     narrow = down_proj.shape[1]
 
+    partner = swap(activations, "yhi")
     mine = gather_columns(down_proj.T)
-    other = swap(mine, "core")
-    map_mine = dot(activations, mine, 1, 1).astype(bf16)
-    map_other = dot(activations, other, 1, 1).astype(bf16)
-    partial_map = jnp.concatenate(ordered(core == 0, map_mine, map_other), axis=1)
-
-    rows = precond.reshape(2, nz, 2, narrow, rank).transpose(2, 1, 0, 3, 4).reshape(rank, rank)
-
-    share_rel = sum_by_exchange(partial_map, FEAT).astype(bf16)
-    half = rank // 2
-    start = half - lax.axis_index("z") * (half // nz)
-    joined_share = jnp.concatenate(
+    columns_t = jnp.concatenate([mine, swap(mine, "core")])
+    partial_map = jnp.stack(
         [
-            lax.dynamic_slice_in_dim(jnp.concatenate([part, part], axis=1), start, half, 1)
-            for part in (share_rel[:, :half], share_rel[:, half:])
+            dot(part, columns_t, 1, 1).astype(bf16).reshape(nf, tokens // nf, rank // 2)
+            for part in (activations, partner)
         ],
         axis=1,
     )
-    joined = gather_by_exchange(joined_share, FEAT).reshape(tokens, rank)
+    share_rel = sum_by_exchange(partial_map.reshape(2 * tokens, rank // 2), FEAT).astype(bf16)
+
+    quarter = rank // 4
+    start = quarter - lax.axis_index("z") * narrow
+    turned = [
+        lax.dynamic_slice_in_dim(jnp.concatenate([part, part], axis=1), start, quarter, 1)
+        for part in (share_rel[:, :quarter], share_rel[:, quarter:])
+    ]
+    turned = jnp.concatenate(ordered(core == 0, *turned), axis=1)
+    own, other = turned[: tokens // nf], turned[tokens // nf :]
+    spread = jnp.stack(ordered(lax.axis_index("yhi") == 0, own, other))
+    spread = jnp.broadcast_to(spread[None], (nf,) + spread.shape)
+    plane = ("x", "ylo", "yhi")
+    halves = lax.all_to_all(
+        spread.reshape(2 * nf, tokens // nf, rank // 2), plane, 0, 0, tiled=True
+    ).reshape(nf, 2, tokens // nf, rank // 2)
+    joined = jnp.concatenate([halves[:, 0], halves[:, 1]], axis=2).reshape(tokens, rank)
+
+    rows = precond.reshape(2, nz, 2, narrow, rank).transpose(0, 2, 1, 3, 4).reshape(rank, rank)
 
     joined_slice = lax.dynamic_slice_in_dim(joined, feat * share, share, 1)
     total = dot(joined_slice, jnp.concatenate([joined, target], axis=1), 0, 0)
     width = total.shape[1]
     summed = sum_by_exchange(sum_by_exchange(total, ("core", "yhi")), "z").astype(bf16)
     summed = gather_by_exchange(summed, "z").reshape(share // 4, width)
-    summed = gather_by_exchange(summed, ("x", "ylo", "yhi")).reshape(nf, share // 2, width)
+    summed = gather_by_exchange(summed, plane).reshape(nf, share // 2, width)
     low, high = ordered(core == 0, summed, swap(summed, "core"))
     summed = jnp.stack([low, high], axis=1).reshape(rank, width)
     gram = summed[:, :rank]
@@ -197,7 +205,7 @@
     coefficients = dot(lift, step, 1, 0, three) + dot(lift_next, step_next, 1, 0, three)
     residual = target.astype(f32) - dot(joined, coefficients.astype(bf16), 1, 0)
     part = nz * 2 // nf
-    kept = coefficients.reshape(2, nz, 2, narrow, -1).transpose(2, 1, 0, 3, 4)
+    kept = coefficients.reshape(2, 2, nz, narrow, -1).transpose(0, 2, 1, 3, 4)
     kept = kept.reshape(nf, part, 2, narrow, -1)
     solution = lax.dynamic_index_in_dim(kept, feat, 0, keepdims=False).reshape(share, -1)
     return solution, residual

time: 263 us -> 245 us (0.932)
  local copies, waits for them, and re-layouts: 18.6 us -> 5.86 us
  waiting for transfers between devices: 37.3 us -> 40.5 us
  matrix products: 19.8 us -> 16.6 us
    unnamed x27 -> x30, local copies, waits for them, and re-layouts: 11.2 us -> 1.81 us
    ppermute x16, waiting for transfers between devices: 1.08 us -> 5.55 us  [shift(): return lax.ppermute(value, axis, [(i, (i + by) % n) for i in range(n)])]
    dot_general x23, matrix products: 19.8 us -> 16.6 us  [dot(): lax.dot_general(a, b, (((ca,), (cb,)), ((), ())), precision=precision, pr...]
    unnamed x2 -> x0, other arithmetic: 2.97 us -> none
    ppermute x3, waiting for transfers between devices: 5.95 us -> 3.07 us  [swap(): return lax.ppermute(value, axis, [(0, 1), (1, 0)])]
  transfers between devices with their start and end apart: 21 -> 21, of which waited for: 6 -> 6; matrix products, arithmetic and copies ran while one was open for 3% -> 2% of each run, Pallas kernels for 0% -> 0%
where the time goes in v2:
time: 245 us; the launch traced here: 244 us
  starting transfers between devices  88 us (36%)
  blocking collectives  69.1 us (28%)
  waiting for transfers between devices  40.5 us (17%)
  Pallas kernels  18.9 us (8%)
  matrix products  16.6 us (7%)
  local copies, waits for them, and re-layouts  5.86 us (2%)
  other arithmetic  3.37 us (1%)
    ppermute x16, starting transfers between devices, shift(): return lax.ppermute(value, axis, [(i, (i + by) % n) for i in range(n)])  59.3 us
    all_to_all x2, blocking collectives, gather_by_exchange(): return lax.all_to_all(spread, axes, 0, 0, tiled=True)  37.2 us
    all_to_all x2, blocking collectives, sum_by_exchange(): lax.all_to_all(parts, axes, 0, 0, tiled=True).astype(f32)  31.9 us
    ppermute x3, starting transfers between devices, swap(): return lax.ppermute(value, axis, [(0, 1), (1, 0)])  20.5 us
    pallas_call x2, Pallas kernels, invert(): pl.pallas_call(invert_kernel, out_shape=jax.ShapeDtypeStruct(matrix.shape...  18.9 us
    dot_general x23, matrix products, dot(): lax.dot_general(a, b, (((ca,), (cb,)), ((), ())), precision=precision, pr...  16.6 us
    all_to_all x1, waiting for transfers between devices, on_device(): lax.all_to_all(spread.reshape(2 * nf, tokens // nf, rank // 2), plane, 0,...  16.2 us
    all_to_all x1, waiting for transfers between devices, sum_by_exchange(): lax.all_to_all(parts, axes, 0, 0, tiled=True).astype(f32)  15.7 us
  transfers between devices with their start and end apart: 21, of which 6 were waited for; matrix products, arithmetic and copies ran while one was open for 2% of the time, Pallas kernels for 0%

profile of v2, /device:TPU:1, one launch (start us, length us, event | category | flops | bytes accessed | tf_op | source)
XLA Modules:
  0.0 243.6 jit_solution(4093738792739712024)
XLA Ops:
  0.6 12.0 %collective-permute-start = (bf16[16,2048]{1,0:T(8,128)(2,1)}, bf16[16,2048]{1,0:T(8,128)(2,1)S(1)}, u32[]{:S(2)}, u32[]{:S(2)}) collective-permute-start(bf16[16,2048]{1,0:T(8,128)(2,1)} %bitcast.110), channel_id=1, source_target_pairs={{0,240},{16,0},{32,16},{48,32},{64,48},{80,64},{96,80},{112,96},{1... | collective-permute-start | bytes 196616 | tf_op jit(solution)/shard_map/ppermute | solution.py:107
  12.6 1.9 collective-permute-start.7
  14.5 4.8 %collective-permute-start.17 = (bf16[512,2048]{1,0:T(8,128)(2,1)}, bf16[512,2048]{1,0:T(8,128)(2,1)S(1)}, u32[]{:S(2)}, u32[]{:S(2)}) collective-permute-start(bf16[512,2048]{1,0:T(8,128)(2,1)} %param.4), channel_id=1, source_target_pairs={{0,256},{256,0},{1,257},{257,1},{2,258},{258,2},{3,259},{259,3},{4... | collective-permute-start | bytes 6291464 | tf_op jit(solution)/shard_map/ppermute | solution.py:98
  20.2 4.6 %collective-permute-start.1 = (bf16[16,2048]{1,0:T(8,128)(2,1)S(1)}, bf16[16,2048]{1,0:T(8,128)(2,1)S(1)}, u32[]{:S(2)}, u32[]{:S(2)}) collective-permute-start(bf16[16,2048]{1,0:T(8,128)(2,1)S(1)} %collective-permute-done), channel_id=1, source_target_pairs={{0,240},{16,0},{32,16},{48,32},{64,48},{80,64},{96,80},{112,96},{1... | collective-permute-start | bytes 196616 | tf_op jit(solution)/shard_map/ppermute | solution.py:107
  24.8 1.9 collective-permute-start.8
  26.8 4.6 %collective-permute-start.2 = (bf16[16,2048]{1,0:T(8,128)(2,1)S(1)}, bf16[16,2048]{1,0:T(8,128)(2,1)S(1)}, u32[]{:S(2)}, u32[]{:S(2)}) collective-permute-start(bf16[16,2048]{1,0:T(8,128)(2,1)S(1)} %collective-permute-done.1), channel_id=1, source_target_pairs={{0,240},{16,0},{32,16},{48,32},{64,48},{80,64},{96,80},{112,96},{1... | collective-permute-start | bytes 196616 | tf_op jit(solution)/shard_map/ppermute | solution.py:107
  31.4 1.9 collective-permute-start.9
  33.3 4.6 %collective-permute-start.3 = (bf16[16,2048]{1,0:T(8,128)(2,1)S(1)}, bf16[16,2048]{1,0:T(8,128)(2,1)S(1)}, u32[]{:S(2)}, u32[]{:S(2)}) collective-permute-start(bf16[16,2048]{1,0:T(8,128)(2,1)S(1)} %collective-permute-done.2), channel_id=1, source_target_pairs={{0,240},{16,0},{32,16},{48,32},{64,48},{80,64},{96,80},{112,96},{1... | collective-permute-start | bytes 196616 | tf_op jit(solution)/shard_map/ppermute | solution.py:107
  37.9 1.9 collective-permute-start.10
  39.9 4.6 %collective-permute-start.4 = (bf16[16,2048]{1,0:T(8,128)(2,1)S(1)}, bf16[16,2048]{1,0:T(8,128)(2,1)S(1)}, u32[]{:S(2)}, u32[]{:S(2)}) collective-permute-start(bf16[16,2048]{1,0:T(8,128)(2,1)S(1)} %collective-permute-done.3), channel_id=1, source_target_pairs={{0,240},{16,0},{32,16},{48,32},{64,48},{80,64},{96,80},{112,96},{1... | collective-permute-start | bytes 196616 | tf_op jit(solution)/shard_map/ppermute | solution.py:107
  44.5 1.9 collective-permute-start.11
  46.4 4.6 %collective-permute-start.5 = (bf16[16,2048]{1,0:T(8,128)(2,1)S(1)}, bf16[16,2048]{1,0:T(8,128)(2,1)S(1)}, u32[]{:S(2)}, u32[]{:S(2)}) collective-permute-start(bf16[16,2048]{1,0:T(8,128)(2,1)S(1)} %collective-permute-done.4), channel_id=1, source_target_pairs={{0,240},{16,0},{32,16},{48,32},{64,48},{80,64},{96,80},{112,96},{1... | collective-permute-start | bytes 196616 | tf_op jit(solution)/shard_map/ppermute | solution.py:107
  51.0 1.9 collective-permute-start.12
  53.0 4.6 %collective-permute-start.6 = (bf16[16,2048]{1,0:T(8,128)(2,1)S(1)}, bf16[16,2048]{1,0:T(8,128)(2,1)S(1)}, u32[]{:S(2)}, u32[]{:S(2)}) collective-permute-start(bf16[16,2048]{1,0:T(8,128)(2,1)S(1)} %collective-permute-done.5), channel_id=1, source_target_pairs={{0,240},{16,0},{32,16},{48,32},{64,48},{80,64},{96,80},{112,96},{1... | collective-permute-start | bytes 196616 | tf_op jit(solution)/shard_map/ppermute | solution.py:107
  57.6 1.9 collective-permute-start.13
  59.5 4.6 %collective-permute-done.13 = bf16[16,2048]{1,0:T(8,128)(2,1)S(1)} collective-permute-done((bf16[16,2048]{1,0:T(8,128)(2,1)S(1)}, bf16[16,2048]{1,0:T(8,128)(2,1)S(1)}, u32[]{:S(2)}, u32[]{:S(2)}) %collective-permute-start.13) | collective-permute-done | bytes 65568 | tf_op jit(solution)/shard_map/ppermute | solution.py:107
  64.1 1.9 collective-permute-start.14
  66.0 4.6 %collective-permute-start.15 = (bf16[8,2048]{1,0:T(8,128)(2,1)S(1)}, bf16[8,2048]{1,0:T(8,128)(2,1)S(1)}, u32[]{:S(2)}, u32[]{:S(2)}) collective-permute-start(bf16[8,2048]{1,0:T(8,128)(2,1)S(1)} %slice.41), channel_id=1, source_target_pairs={{0,240},{16,0},{32,16},{48,32},{64,48},{80,64},{96,80},{112,96},{1... | collective-permute-start | bytes 98312 | tf_op jit(solution)/shard_map/ppermute | solution.py:107
  71.7 10.1 %collective-permute-start.16 = (bf16[256,2048]{1,0:T(8,128)(2,1)S(1)}, bf16[256,2048]{1,0:T(8,128)(2,1)S(1)}, u32[]{:S(2)}, u32[]{:S(2)}) collective-permute-start(bf16[256,2048]{1,0:T(8,128)(2,1)S(1)} %get-tuple-element.12), channel_id=1, source_target_pairs={{0,8},{8,0},{1,9},{9,1},{2,10},{10,2},{3,11},{11,3},{4,12},{12,4},... | collective-permute-start | bytes 3145736 | tf_op jit(solution)/shard_map/ppermute | solution.py:98
  81.8 2.3 collective-permute-done.16
  87.8 4.1 %all-to-all-start = ((bf16[8,128,512]{2,1,0:T(8,128)(2,1)}), bf16[8,128,512]{2,1,0:T(8,128)(2,1)S(1)}, u32[]{:S(2)}, u32[]{:S(2)}) async-start(bf16[8,128,512]{2,1,0:T(8,128)(2,1)} %bitcast.7), calls=%async_computation | async-start | bytes 2097152 | tf_op jit(solution)/shard_map/all_to_all | solution.py:131
  92.0 15.7 %all-to-all-done = bf16[8,128,512]{2,1,0:T(8,128)(2,1)S(1)} async-done(((bf16[8,128,512]{2,1,0:T(8,128)(2,1)}), bf16[8,128,512]{2,1,0:T(8,128)(2,1)S(1)}, u32[]{:S(2)}, u32[]{:S(2)}) %all-to-all-start) | async-done | bytes 1048608 | tf_op jit(solution)/shard_map/all_to_all | solution.py:131
  109.2 4.1 %all-to-all-start.1 = ((bf16[16,64,512]{2,1,0:T(8,128)(2,1)}), bf16[16,64,512]{2,1,0:T(8,128)(2,1)S(1)}, u32[]{:S(2)}, u32[]{:S(2)}) async-start(bf16[16,64,512]{2,1,0:T(8,128)(2,1)} %bitcast.10), calls=%async_computation.1 | async-start | bytes 2097152 | tf_op jit(solution)/shard_map/all_to_all | solution.py:166
  113.3 16.2 %all-to-all-done.1 = bf16[16,64,512]{2,1,0:T(8,128)(2,1)S(1)} async-done(((bf16[16,64,512]{2,1,0:T(8,128)(2,1)}), bf16[16,64,512]{2,1,0:T(8,128)(2,1)S(1)}, u32[]{:S(2)}, u32[]{:S(2)}) %all-to-all-start.1) | async-done | bytes 1048608 | tf_op jit(solution)/shard_map/all_to_all | solution.py:166
  130.8 12.7 %all_to_all.30 = bf16[4,32,1280]{2,1,0:T(8,128)(2,1)S(1)} all-to-all(bf16[4,32,1280]{2,1,0:T(8,128)(2,1)S(1)} %bitcast.108), channel_id=1, replica_groups=mesh['yhi'=2,'z'=16,'core'=2,'x'=4,'ylo'=2] {'core','yhi'}, dimensions={0} | all-to-all | bytes 655360 | tf_op jit(solution)/shard_map/all_to_all | solution.py:131
  143.6 19.2 %all_to_all.31 = bf16[16,2,1280]{2,1,0:T(2,128)(2,1)S(1)} all-to-all(bf16[16,2,1280]{2,1,0:T(2,128)(2,1)S(1)} %reshape.49), channel_id=1, replica_groups=mesh['yhi'=2,'z'=16,'core'=2,'x'=4,'ylo'=2] {'z'}, dimensions={0} | all-to-all | bytes 163840 | tf_op jit(solution)/shard_map/all_to_all | solution.py:131
  162.9 15.8 %all_to_all.32 = bf16[16,2,1280]{2,1,0:T(2,128)(2,1)S(1)} all-to-all(bf16[16,2,1280]{2,1,0:T(2,128)(2,1)S(1)} %broadcast_in_dim.9), channel_id=1, replica_groups=mesh['yhi'=2,'z'=16,'core'=2,'x'=4,'ylo'=2] {'z'}, dimensions={0} | all-to-all | bytes 163840 | tf_op jit(solution)/shard_map/all_to_all | solution.py:125
  178.9 21.4 %all_to_all.33 = bf16[16,32,1280]{2,1,0:T(8,128)(2,1)S(1)} all-to-all(bf16[16,32,1280]{2,1,0:T(8,128)(2,1)S(1)} %broadcast_in_dim.22), channel_id=1, replica_groups=mesh['yhi'=2,'z'=16,'core'=2,'x'=4,'ylo'=2] {'x','ylo','yhi'}, dimensions={0} | all-to-all | bytes 2621440 | tf_op jit(solution)/shard_map/all_to_all | solution.py:125
  200.2 5.6 %collective-permute-start.18 = (bf16[8,64,1280]{2,1,0:T(8,128)(2,1)S(1)}, bf16[8,64,1280]{2,1,0:T(8,128)(2,1)}, u32[]{:S(2)}, u32[]{:S(2)}) collective-permute-start(bf16[8,64,1280]{2,1,0:T(8,128)(2,1)S(1)} %bitcast.94), channel_id=1, source_target_pairs={{0,8},{8,0},{1,9},{9,1},{2,10},{10,2},{3,11},{11,3},{4,12},{12,4},... | collective-permute-start | bytes 3932168 | tf_op jit(solution)/shard_map/ppermute | solution.py:98
  205.8 1.8 copy.30
  214.3 9.3 %shard_map.59 = f32[256,256]{1,0:T(8,128)S(1)} custom-call(f32[256,256]{1,0:T(8,128)S(1)} %fusion.20.matrix_ref), custom_call_target="tpu_custom_call" | custom-call | tf_op jit(solution)/shard_map/pallas_call | solution.py:88
  230.7 9.6 %shard_map.60 = f32[256,256]{1,0:T(8,128)S(1)} custom-call(f32[256,256]{1,0:T(8,128)S(1)} %fusion.14.matrix_ref), custom_call_target="tpu_custom_call" | custom-call | tf_op jit(solution)/shard_map/pallas_call | solution.py:88
  (92 shorter events, 25.9 us)
Async XLA Ops:
  0.6 19.6 %collective-permute-start = (bf16[16,2048]{1,0:T(8,128)(2,1)}, bf16[16,2048]{1,0:T(8,128)(2,1)S(1)}, u32[]{:S(2)}, u32[]{:S(2)}) collective-permute-start(bf16[16,2048]{1,0:T(8,128)(2,1)} %bitcast.110), channel_id=1, source_target_pairs={{0,240},{16,0},{32,16},{48,32},{64,48},{80,64},{96,80},{112,96},{1... | collective-permute-start | bytes 196616 | tf_op jit(solution)/shard_map/ppermute | solution.py:107
  12.6 12.2 %collective-permute-start.7 = (bf16[16,2048]{1,0:T(8,128)(2,1)}, bf16[16,2048]{1,0:T(8,128)(2,1)S(1)}, u32[]{:S(2)}, u32[]{:S(2)}) collective-permute-start(bf16[16,2048]{1,0:T(8,128)(2,1)} %bitcast.111), channel_id=1, source_target_pairs={{0,16},{16,32},{32,48},{48,64},{64,80},{80,96},{96,112},{112,128},... | collective-permute-start | bytes 196616 | tf_op jit(solution)/shard_map/ppermute | solution.py:107
  14.5 71.0 %collective-permute-start.17 = (bf16[512,2048]{1,0:T(8,128)(2,1)}, bf16[512,2048]{1,0:T(8,128)(2,1)S(1)}, u32[]{:S(2)}, u32[]{:S(2)}) collective-permute-start(bf16[512,2048]{1,0:T(8,128)(2,1)} %param.4), channel_id=1, source_target_pairs={{0,256},{256,0},{1,257},{257,1},{2,258},{258,2},{3,259},{259,3},{4... | collective-permute-start | bytes 6291464 | tf_op jit(solution)/shard_map/ppermute | solution.py:98
  20.2 6.5 %collective-permute-start.1 = (bf16[16,2048]{1,0:T(8,128)(2,1)S(1)}, bf16[16,2048]{1,0:T(8,128)(2,1)S(1)}, u32[]{:S(2)}, u32[]{:S(2)}) collective-permute-start(bf16[16,2048]{1,0:T(8,128)(2,1)S(1)} %collective-permute-done), channel_id=1, source_target_pairs={{0,240},{16,0},{32,16},{48,32},{64,48},{80,64},{96,80},{112,96},{1... | collective-permute-start | bytes 196616 | tf_op jit(solution)/shard_map/ppermute | solution.py:107
  24.8 6.5 %collective-permute-start.8 = (bf16[16,2048]{1,0:T(8,128)(2,1)S(1)}, bf16[16,2048]{1,0:T(8,128)(2,1)S(1)}, u32[]{:S(2)}, u32[]{:S(2)}) collective-permute-start(bf16[16,2048]{1,0:T(8,128)(2,1)S(1)} %collective-permute-done.7), channel_id=1, source_target_pairs={{0,16},{16,32},{32,48},{48,64},{64,80},{80,96},{96,112},{112,128},... | collective-permute-start | bytes 196616 | tf_op jit(solution)/shard_map/ppermute | solution.py:107
  26.8 6.5 %collective-permute-start.2 = (bf16[16,2048]{1,0:T(8,128)(2,1)S(1)}, bf16[16,2048]{1,0:T(8,128)(2,1)S(1)}, u32[]{:S(2)}, u32[]{:S(2)}) collective-permute-start(bf16[16,2048]{1,0:T(8,128)(2,1)S(1)} %collective-permute-done.1), channel_id=1, source_target_pairs={{0,240},{16,0},{32,16},{48,32},{64,48},{80,64},{96,80},{112,96},{1... | collective-permute-start | bytes 196616 | tf_op jit(solution)/shard_map/ppermute | solution.py:107
  31.4 6.5 %collective-permute-start.9 = (bf16[16,2048]{1,0:T(8,128)(2,1)S(1)}, bf16[16,2048]{1,0:T(8,128)(2,1)S(1)}, u32[]{:S(2)}, u32[]{:S(2)}) collective-permute-start(bf16[16,2048]{1,0:T(8,128)(2,1)S(1)} %collective-permute-done.8), channel_id=1, source_target_pairs={{0,16},{16,32},{32,48},{48,64},{64,80},{80,96},{96,112},{112,128},... | collective-permute-start | bytes 196616 | tf_op jit(solution)/shard_map/ppermute | solution.py:107
  33.3 6.5 %collective-permute-start.3 = (bf16[16,2048]{1,0:T(8,128)(2,1)S(1)}, bf16[16,2048]{1,0:T(8,128)(2,1)S(1)}, u32[]{:S(2)}, u32[]{:S(2)}) collective-permute-start(bf16[16,2048]{1,0:T(8,128)(2,1)S(1)} %collective-permute-done.2), channel_id=1, source_target_pairs={{0,240},{16,0},{32,16},{48,32},{64,48},{80,64},{96,80},{112,96},{1... | collective-permute-start | bytes 196616 | tf_op jit(solution)/shard_map/ppermute | solution.py:107
  37.9 6.5 %collective-permute-start.10 = (bf16[16,2048]{1,0:T(8,128)(2,1)S(1)}, bf16[16,2048]{1,0:T(8,128)(2,1)S(1)}, u32[]{:S(2)}, u32[]{:S(2)}) collective-permute-start(bf16[16,2048]{1,0:T(8,128)(2,1)S(1)} %collective-permute-done.9), channel_id=1, source_target_pairs={{0,16},{16,32},{32,48},{48,64},{64,80},{80,96},{96,112},{112,128},... | collective-permute-start | bytes 196616 | tf_op jit(solution)/shard_map/ppermute | solution.py:107
  39.9 6.5 %collective-permute-start.4 = (bf16[16,2048]{1,0:T(8,128)(2,1)S(1)}, bf16[16,2048]{1,0:T(8,128)(2,1)S(1)}, u32[]{:S(2)}, u32[]{:S(2)}) collective-permute-start(bf16[16,2048]{1,0:T(8,128)(2,1)S(1)} %collective-permute-done.3), channel_id=1, source_target_pairs={{0,240},{16,0},{32,16},{48,32},{64,48},{80,64},{96,80},{112,96},{1... | collective-permute-start | bytes 196616 | tf_op jit(solution)/shard_map/ppermute | solution.py:107
  44.5 6.5 %collective-permute-start.11 = (bf16[16,2048]{1,0:T(8,128)(2,1)S(1)}, bf16[16,2048]{1,0:T(8,128)(2,1)S(1)}, u32[]{:S(2)}, u32[]{:S(2)}) collective-permute-start(bf16[16,2048]{1,0:T(8,128)(2,1)S(1)} %collective-permute-done.10), channel_id=1, source_target_pairs={{0,16},{16,32},{32,48},{48,64},{64,80},{80,96},{96,112},{112,128},... | collective-permute-start | bytes 196616 | tf_op jit(solution)/shard_map/ppermute | solution.py:107
  46.4 6.5 %collective-permute-start.5 = (bf16[16,2048]{1,0:T(8,128)(2,1)S(1)}, bf16[16,2048]{1,0:T(8,128)(2,1)S(1)}, u32[]{:S(2)}, u32[]{:S(2)}) collective-permute-start(bf16[16,2048]{1,0:T(8,128)(2,1)S(1)} %collective-permute-done.4), channel_id=1, source_target_pairs={{0,240},{16,0},{32,16},{48,32},{64,48},{80,64},{96,80},{112,96},{1... | collective-permute-start | bytes 196616 | tf_op jit(solution)/shard_map/ppermute | solution.py:107
  51.0 6.5 %collective-permute-start.12 = (bf16[16,2048]{1,0:T(8,128)(2,1)S(1)}, bf16[16,2048]{1,0:T(8,128)(2,1)S(1)}, u32[]{:S(2)}, u32[]{:S(2)}) collective-permute-start(bf16[16,2048]{1,0:T(8,128)(2,1)S(1)} %collective-permute-done.11), channel_id=1, source_target_pairs={{0,16},{16,32},{32,48},{48,64},{64,80},{80,96},{96,112},{112,128},... | collective-permute-start | bytes 196616 | tf_op jit(solution)/shard_map/ppermute | solution.py:107
  53.0 13.0 %collective-permute-start.6 = (bf16[16,2048]{1,0:T(8,128)(2,1)S(1)}, bf16[16,2048]{1,0:T(8,128)(2,1)S(1)}, u32[]{:S(2)}, u32[]{:S(2)}) collective-permute-start(bf16[16,2048]{1,0:T(8,128)(2,1)S(1)} %collective-permute-done.5), channel_id=1, source_target_pairs={{0,240},{16,0},{32,16},{48,32},{64,48},{80,64},{96,80},{112,96},{1... | collective-permute-start | bytes 196616 | tf_op jit(solution)/shard_map/ppermute | solution.py:107
  57.6 6.5 %collective-permute-start.13 = (bf16[16,2048]{1,0:T(8,128)(2,1)S(1)}, bf16[16,2048]{1,0:T(8,128)(2,1)S(1)}, u32[]{:S(2)}, u32[]{:S(2)}) collective-permute-start(bf16[16,2048]{1,0:T(8,128)(2,1)S(1)} %collective-permute-done.12), channel_id=1, source_target_pairs={{0,16},{16,32},{32,48},{48,64},{64,80},{80,96},{96,112},{112,128},... | collective-permute-start | bytes 196616 | tf_op jit(solution)/shard_map/ppermute | solution.py:107
  59.5 24.7 %copy-start.6 = (bf16[512,2048]{1,0:T(8,128)(2,1)S(1)}, bf16[512,2048]{1,0:T(8,128)(2,1)}, u32[]{:S(2)}) copy-start(bf16[512,2048]{1,0:T(8,128)(2,1)} %param.4) | copy-start | bytes 6291460
  64.1 6.5 %collective-permute-start.14 = (bf16[8,2048]{1,0:T(8,128)(2,1)S(1)}, bf16[8,2048]{1,0:T(8,128)(2,1)S(1)}, u32[]{:S(2)}, u32[]{:S(2)}) collective-permute-start(bf16[8,2048]{1,0:T(8,128)(2,1)S(1)} %slice.40), channel_id=1, source_target_pairs={{0,16},{16,32},{32,48},{48,64},{64,80},{80,96},{96,112},{112,128},... | collective-permute-start | bytes 98312 | tf_op jit(solution)/shard_map/ppermute | solution.py:107
  66.0 5.6 %collective-permute-start.15 = (bf16[8,2048]{1,0:T(8,128)(2,1)S(1)}, bf16[8,2048]{1,0:T(8,128)(2,1)S(1)}, u32[]{:S(2)}, u32[]{:S(2)}) collective-permute-start(bf16[8,2048]{1,0:T(8,128)(2,1)S(1)} %slice.41), channel_id=1, source_target_pairs={{0,240},{16,0},{32,16},{48,32},{64,48},{80,64},{96,80},{112,96},{1... | collective-permute-start | bytes 98312 | tf_op jit(solution)/shard_map/ppermute | solution.py:107
  71.7 12.4 %collective-permute-start.16 = (bf16[256,2048]{1,0:T(8,128)(2,1)S(1)}, bf16[256,2048]{1,0:T(8,128)(2,1)S(1)}, u32[]{:S(2)}, u32[]{:S(2)}) collective-permute-start(bf16[256,2048]{1,0:T(8,128)(2,1)S(1)} %get-tuple-element.12), channel_id=1, source_target_pairs={{0,8},{8,0},{1,9},{9,1},{2,10},{10,2},{3,11},{11,3},{4,12},{12,4},... | collective-permute-start | bytes 3145736 | tf_op jit(solution)/shard_map/ppermute | solution.py:98
  87.8 19.8 %all-to-all-start = ((bf16[8,128,512]{2,1,0:T(8,128)(2,1)}), bf16[8,128,512]{2,1,0:T(8,128)(2,1)S(1)}, u32[]{:S(2)}, u32[]{:S(2)}) async-start(bf16[8,128,512]{2,1,0:T(8,128)(2,1)} %bitcast.7), calls=%async_computation | async-start | bytes 2097152 | tf_op jit(solution)/shard_map/all_to_all | solution.py:131
  109.2 21.1 %copy-start.4 = (bf16[512,256]{1,0:T(8,128)(2,1)S(1)}, bf16[512,256]{1,0:T(8,128)(2,1)}, u32[]{:S(2)}) copy-start(bf16[512,256]{1,0:T(8,128)(2,1)} %param.7) | copy-start | bytes 786436
  109.2 20.3 %all-to-all-start.1 = ((bf16[16,64,512]{2,1,0:T(8,128)(2,1)}), bf16[16,64,512]{2,1,0:T(8,128)(2,1)S(1)}, u32[]{:S(2)}, u32[]{:S(2)}) async-start(bf16[16,64,512]{2,1,0:T(8,128)(2,1)} %bitcast.10), calls=%async_computation.1 | async-start | bytes 2097152 | tf_op jit(solution)/shard_map/all_to_all | solution.py:166
  129.6 0.8 copy-start
  129.6 1.2 copy-start.2
  200.2 8.2 %collective-permute-start.18 = (bf16[8,64,1280]{2,1,0:T(8,128)(2,1)S(1)}, bf16[8,64,1280]{2,1,0:T(8,128)(2,1)}, u32[]{:S(2)}, u32[]{:S(2)}) collective-permute-start(bf16[8,64,1280]{2,1,0:T(8,128)(2,1)S(1)} %bitcast.94), channel_id=1, source_target_pairs={{0,8},{8,0},{1,9},{9,1},{2,10},{10,2},{3,11},{11,3},{4,12},{12,4},... | collective-permute-start | bytes 3932168 | tf_op jit(solution)/shard_map/ppermute | solution.py:98
  240.3 1.3 copy-start.1
  240.3 1.3 copy-start.3
  240.3 1.3 copy-start.5

commit v3 on v2

--- a/solution.py
+++ b/solution.py
@@ -8,7 +8,6 @@
 AXES = ("yhi", "z", "core", "x", "ylo")
 TOK = ("yhi", "z", "core")
 FEAT = ("x", "ylo")
-BLOCK = 128
 bf16 = jnp.bfloat16
 f32 = jnp.float32
 precise = lax.Precision.HIGHEST
@@ -67,21 +66,16 @@
 
 
 def invert_kernel(matrix_ref, out_ref):
-    n = matrix_ref.shape[0]
-    rows = lax.broadcasted_iota(jnp.int32, (n, BLOCK), 0)
-    out_ref[...] = matrix_ref[...]
-    for k in range(n // BLOCK):
-        lo, hi = k * BLOCK, (k + 1) * BLOCK
-        inverse = invert_block(out_ref[lo:hi, lo:hi])
-        left = out_ref[:, lo:hi]
-        zeroed = jnp.where((rows >= lo) & (rows < hi), 0.0, left)
-        out_ref[lo:hi, :] = dot(inverse, out_ref[lo:hi, :], 1, 0, precise)
-        out_ref[lo:hi, lo:hi] = inverse
-        panel = out_ref[lo:hi, :]
-        out_ref[lo:hi, :] = jnp.zeros_like(panel)
-        out_ref[:, lo:hi] = jnp.zeros_like(left)
-        out_ref[...] = out_ref[...] - dot(zeroed, panel, 1, 0, precise)
-        out_ref[lo:hi, :] = panel
+    half = matrix_ref.shape[0] // 2
+    first = invert_block(matrix_ref[:half, :half])
+    corner = matrix_ref[:half, half:]
+    right = dot(first, corner, 1, 0, precise)
+    last = invert_block(matrix_ref[half:, half:] - dot(corner, right, 0, 0, precise))
+    cross = dot(right, last, 1, 0, precise)
+    out_ref[:half, :half] = first + dot(cross, right, 1, 1, precise)
+    out_ref[:half, half:] = -cross
+    out_ref[half:, :half] = -cross.T
+    out_ref[half:, half:] = last
 
 
 def invert(matrix):
@@ -108,15 +102,32 @@
 
 
 def gather_columns(down_t):
-    half = down_t.shape[0] // 2
-    up, down = down_t, down_t
-    below, above = [], []
-    for k in range(1, lax.axis_size("z") // 2):
-        up, down = shift(up, "z", 1), shift(down, "z", -1)
-        below.append(up)
-        above.append(down)
-    last = [shift(up[:half], "z", 1), shift(down[half:], "z", -1)]
-    return jnp.concatenate([down_t] + above + last + below[::-1])
+    n = down_t.shape[0]
+    half = n // 2
+    nz = lax.axis_size("z")
+    if nz != 16:
+        up, down = down_t, down_t
+        below, above = [], []
+        for k in range(1, nz // 2):
+            up, down = shift(up, "z", 1), shift(down, "z", -1)
+            below.append(up)
+            above.append(down)
+        last = [shift(up[:half], "z", 1), shift(down[half:], "z", -1)]
+        return jnp.concatenate([down_t] + above + last + below[::-1])
+    below_1, above_1 = shift(down_t, "z", 1), shift(down_t, "z", -1)
+    below_2 = shift(jnp.concatenate([down_t, below_1]), "z", 2)
+    above_2 = shift(jnp.concatenate([down_t, above_1]), "z", -2)
+    below_4, above_4 = shift(below_2, "z", 2), shift(above_2, "z", -2)
+    below_6 = shift(jnp.concatenate([below_2[n:], below_4[: n + half]]), "z", 3)
+    above_6 = shift(
+        jnp.concatenate([above_2[n:], above_4[:n], above_4[n + half :]]), "z", -3
+    )
+    above = [down_t, above_1, above_2, above_4, above_6[: 2 * n]]
+    far = [below_6[2 * n :], above_6[2 * n :]]
+    below = []
+    for pair in (below_6, below_4, below_2):
+        below += [pair[n : 2 * n], pair[:n]]
+    return jnp.concatenate(above + far + below + [below_1])
 
 
 def gather_by_exchange(value, axes):

time: 245 us -> 226 us (0.922)
  starting transfers between devices: 88 us -> 58.3 us
  waiting for transfers between devices: 40.5 us -> 52.7 us
    ppermute x16 -> x8, starting transfers between devices: 59.3 us -> 38 us  [shift(): return lax.ppermute(value, axis, [(i, (i + by) % n) for i in range(n)])]
    ppermute x16 -> x8, waiting for transfers between devices: 5.55 us -> 19 us  [shift(): return lax.ppermute(value, axis, [(i, (i + by) % n) for i in range(n)])]
    ppermute x3, starting transfers between devices: 20.5 us -> 12.4 us  [swap(): return lax.ppermute(value, axis, [(0, 1), (1, 0)])]
  transfers between devices with their start and end apart: 21 -> 13, of which waited for: 6 -> 8; matrix products, arithmetic and copies ran while one was open for 2% -> 2% of each run, Pallas kernels for 0% -> 0%
where the time goes in v3:
time: 226 us; the launch traced here: 225 us
  blocking collectives  68.4 us (30%)
  starting transfers between devices  58.3 us (26%)
  waiting for transfers between devices  52.7 us (23%)
  Pallas kernels  17.9 us (8%)
  matrix products  16.6 us (7%)
  local copies, waits for them, and re-layouts  5.9 us (3%)
  other arithmetic  4.25 us (2%)
    ppermute x8, starting transfers between devices, shift(): return lax.ppermute(value, axis, [(i, (i + by) % n) for i in range(n)])  38 us
    all_to_all x2, blocking collectives, gather_by_exchange(): return lax.all_to_all(spread, axes, 0, 0, tiled=True)  36.3 us
    all_to_all x2, blocking collectives, sum_by_exchange(): lax.all_to_all(parts, axes, 0, 0, tiled=True).astype(f32)  32 us
    ppermute x8, waiting for transfers between devices, shift(): return lax.ppermute(value, axis, [(i, (i + by) % n) for i in range(n)])  19 us
    pallas_call x2, Pallas kernels, invert(): pl.pallas_call(invert_kernel, out_shape=jax.ShapeDtypeStruct(matrix.shape...  17.9 us
    dot_general x23, matrix products, dot(): lax.dot_general(a, b, (((ca,), (cb,)), ((), ())), precision=precision, pr...  16.6 us
    all_to_all x1, waiting for transfers between devices, sum_by_exchange(): lax.all_to_all(parts, axes, 0, 0, tiled=True).astype(f32)  15.7 us
    all_to_all x1, waiting for transfers between devices, on_device(): lax.all_to_all(spread.reshape(2 * nf, tokens // nf, rank // 2), plane, 0,...  14.9 us
  transfers between devices with their start and end apart: 13, of which 8 were waited for; matrix products, arithmetic and copies ran while one was open for 2% of the time, Pallas kernels for 0%

profile of v3, /device:TPU:1, one launch (start us, length us, event | category | flops | bytes accessed | tf_op | source)
XLA Modules:
  0.0 225.4 jit_solution(655707249255323351)
XLA Ops:
  0.6 12.0 %collective-permute-start = (bf16[16,2048]{1,0:T(8,128)(2,1)}, bf16[16,2048]{1,0:T(8,128)(2,1)S(1)}, u32[]{:S(2)}, u32[]{:S(2)}) collective-permute-start(bf16[16,2048]{1,0:T(8,128)(2,1)} %bitcast.109), channel_id=1, source_target_pairs={{0,240},{16,0},{32,16},{48,32},{64,48},{80,64},{96,80},{112,96},{1... | collective-permute-start | bytes 196616 | tf_op jit(solution)/shard_map/ppermute | solution.py:101
  12.6 1.9 collective-permute-start.4
  14.5 4.8 %collective-permute-start.9 = (bf16[512,2048]{1,0:T(8,128)(2,1)}, bf16[512,2048]{1,0:T(8,128)(2,1)S(1)}, u32[]{:S(2)}, u32[]{:S(2)}) collective-permute-start(bf16[512,2048]{1,0:T(8,128)(2,1)} %param.4), channel_id=1, source_target_pairs={{0,256},{256,0},{1,257},{257,1},{2,258},{258,2},{3,259},{259,3},{4... | collective-permute-start | bytes 6291464 | tf_op jit(solution)/shard_map/ppermute | solution.py:92
  21.1 3.8 %collective-permute-start.1 = (bf16[32,2048]{1,0:T(8,128)(2,1)S(1)}, bf16[32,2048]{1,0:T(8,128)(2,1)S(1)}, u32[]{:S(2)}, u32[]{:S(2)}) collective-permute-start(bf16[32,2048]{1,0:T(8,128)(2,1)S(1)} %get-tuple-element.35), channel_id=1, source_target_pairs={{0,224},{16,240},{32,0},{48,16},{64,32},{80,48},{96,64},{112,80},{... | collective-permute-start | bytes 393224 | tf_op jit(solution)/shard_map/ppermute | solution.py:101
  24.9 2.4 %collective-permute-start.5 = (bf16[32,2048]{1,0:T(8,128)(2,1)S(1)}, bf16[32,2048]{1,0:T(8,128)(2,1)S(1)}, u32[]{:S(2)}, u32[]{:S(2)}) collective-permute-start(bf16[32,2048]{1,0:T(8,128)(2,1)S(1)} %get-tuple-element.34), channel_id=1, source_target_pairs={{0,32},{16,48},{32,64},{48,80},{64,96},{80,112},{96,128},{112,144}... | collective-permute-start | bytes 393224 | tf_op jit(solution)/shard_map/ppermute | solution.py:101
  27.3 2.8 %collective-permute-done.1 = bf16[32,2048]{1,0:T(8,128)(2,1)S(1)} collective-permute-done((bf16[32,2048]{1,0:T(8,128)(2,1)S(1)}, bf16[32,2048]{1,0:T(8,128)(2,1)S(1)}, u32[]{:S(2)}, u32[]{:S(2)}) %collective-permute-start.1) | collective-permute-done | bytes 131104 | tf_op jit(solution)/shard_map/ppermute | solution.py:101
  30.1 4.0 %collective-permute-start.2 = (bf16[32,2048]{1,0:T(8,128)(2,1)S(1)}, bf16[32,2048]{1,0:T(8,128)(2,1)S(1)}, u32[]{:S(2)}, u32[]{:S(2)}) collective-permute-start(bf16[32,2048]{1,0:T(8,128)(2,1)S(1)} %collective-permute-done.1), channel_id=1, source_target_pairs={{0,224},{16,240},{32,0},{48,16},{64,32},{80,48},{96,64},{112,80},{... | collective-permute-start | bytes 393224 | tf_op jit(solution)/shard_map/ppermute | solution.py:101
  34.2 2.1 collective-permute-start.6
  37.0 9.9 %collective-permute-start.3 = (bf16[40,2048]{1,0:T(8,128)(2,1)S(1)}, bf16[40,2048]{1,0:T(8,128)(2,1)S(1)}, u32[]{:S(2)}, u32[]{:S(2)}) collective-permute-start(bf16[40,2048]{1,0:T(8,128)(2,1)S(1)} %pad_maximum_fusion.4), channel_id=1, source_target_pairs={{0,208},{16,224},{32,240},{48,0},{64,16},{80,32},{96,48},{112,64},... | collective-permute-start | bytes 491528 | tf_op jit(solution)/shard_map/ppermute | solution.py:101
  46.9 1.9 collective-permute-start.7
  48.9 3.5 %collective-permute-done.3 = bf16[40,2048]{1,0:T(8,128)(2,1)S(1)} collective-permute-done((bf16[40,2048]{1,0:T(8,128)(2,1)S(1)}, bf16[40,2048]{1,0:T(8,128)(2,1)S(1)}, u32[]{:S(2)}, u32[]{:S(2)}) %collective-permute-start.3) | collective-permute-done | bytes 163872 | tf_op jit(solution)/shard_map/ppermute | solution.py:101
  52.4 12.1 %collective-permute-done.7 = bf16[40,2048]{1,0:T(8,128)(2,1)S(1)} collective-permute-done((bf16[40,2048]{1,0:T(8,128)(2,1)S(1)}, bf16[40,2048]{1,0:T(8,128)(2,1)S(1)}, u32[]{:S(2)}, u32[]{:S(2)}) %collective-permute-start.7) | collective-permute-done | bytes 163872 | tf_op jit(solution)/shard_map/ppermute | solution.py:101
  64.7 2.4 %collective-permute-start.8 = (bf16[256,2048]{1,0:T(8,128)(2,1)S(1)}, bf16[256,2048]{1,0:T(8,128)(2,1)S(1)}, u32[]{:S(2)}, u32[]{:S(2)}) collective-permute-start(bf16[256,2048]{1,0:T(8,128)(2,1)S(1)} %get-tuple-element.28), channel_id=1, source_target_pairs={{0,8},{8,0},{1,9},{9,1},{2,10},{10,2},{3,11},{11,3},{4,12},{12,4},... | collective-permute-start | bytes 3145736 | tf_op jit(solution)/shard_map/ppermute | solution.py:92
  67.1 2.3 %collective-permute-done.8 = bf16[256,2048]{1,0:T(8,128)(2,1)S(1)} collective-permute-done((bf16[256,2048]{1,0:T(8,128)(2,1)S(1)}, bf16[256,2048]{1,0:T(8,128)(2,1)S(1)}, u32[]{:S(2)}, u32[]{:S(2)}) %collective-permute-start.8) | collective-permute-done | bytes 1048608 | tf_op jit(solution)/shard_map/ppermute | solution.py:92
  69.5 1.3 convolution_convert_fusion.2
  70.8 1.3 convolution_convert_fusion.1
  73.1 4.1 %all-to-all-start = ((bf16[8,128,512]{2,1,0:T(8,128)(2,1)}), bf16[8,128,512]{2,1,0:T(8,128)(2,1)S(1)}, u32[]{:S(2)}, u32[]{:S(2)}) async-start(bf16[8,128,512]{2,1,0:T(8,128)(2,1)} %bitcast.7), calls=%async_computation | async-start | bytes 2097152 | tf_op jit(solution)/shard_map/all_to_all | solution.py:142
  77.3 15.7 %all-to-all-done = bf16[8,128,512]{2,1,0:T(8,128)(2,1)S(1)} async-done(((bf16[8,128,512]{2,1,0:T(8,128)(2,1)}), bf16[8,128,512]{2,1,0:T(8,128)(2,1)S(1)}, u32[]{:S(2)}, u32[]{:S(2)}) %all-to-all-start) | async-done | bytes 1048608 | tf_op jit(solution)/shard_map/all_to_all | solution.py:142
  93.4 1.1 broadcast_in_dim.8
  94.5 3.8 %all-to-all-start.1 = ((bf16[16,64,512]{2,1,0:T(8,128)(2,1)}), bf16[16,64,512]{2,1,0:T(8,128)(2,1)S(1)}, u32[]{:S(2)}, u32[]{:S(2)}) async-start(bf16[16,64,512]{2,1,0:T(8,128)(2,1)} %bitcast.10), calls=%async_computation.1 | async-start | bytes 2097152 | tf_op jit(solution)/shard_map/all_to_all | solution.py:177
  98.3 14.9 %all-to-all-done.1 = bf16[16,64,512]{2,1,0:T(8,128)(2,1)S(1)} async-done(((bf16[16,64,512]{2,1,0:T(8,128)(2,1)}), bf16[16,64,512]{2,1,0:T(8,128)(2,1)S(1)}, u32[]{:S(2)}, u32[]{:S(2)}) %all-to-all-start.1) | async-done | bytes 1048608 | tf_op jit(solution)/shard_map/all_to_all | solution.py:177
  114.6 13.5 %all_to_all.30 = bf16[4,32,1280]{2,1,0:T(8,128)(2,1)S(1)} all-to-all(bf16[4,32,1280]{2,1,0:T(8,128)(2,1)S(1)} %bitcast.108), channel_id=1, replica_groups=mesh['yhi'=2,'z'=16,'core'=2,'x'=4,'ylo'=2] {'core','yhi'}, dimensions={0} | all-to-all | bytes 655360 | tf_op jit(solution)/shard_map/all_to_all | solution.py:142
  128.1 18.6 %all_to_all.31 = bf16[16,2,1280]{2,1,0:T(2,128)(2,1)S(1)} all-to-all(bf16[16,2,1280]{2,1,0:T(2,128)(2,1)S(1)} %reshape.49), channel_id=1, replica_groups=mesh['yhi'=2,'z'=16,'core'=2,'x'=4,'ylo'=2] {'z'}, dimensions={0} | all-to-all | bytes 163840 | tf_op jit(solution)/shard_map/all_to_all | solution.py:142
  146.8 15.8 %all_to_all.32 = bf16[16,2,1280]{2,1,0:T(2,128)(2,1)S(1)} all-to-all(bf16[16,2,1280]{2,1,0:T(2,128)(2,1)S(1)} %broadcast_in_dim.9), channel_id=1, replica_groups=mesh['yhi'=2,'z'=16,'core'=2,'x'=4,'ylo'=2] {'z'}, dimensions={0} | all-to-all | bytes 163840 | tf_op jit(solution)/shard_map/all_to_all | solution.py:136
  162.8 20.5 %all_to_all.33 = bf16[16,32,1280]{2,1,0:T(8,128)(2,1)S(1)} all-to-all(bf16[16,32,1280]{2,1,0:T(8,128)(2,1)S(1)} %broadcast_in_dim.22), channel_id=1, replica_groups=mesh['yhi'=2,'z'=16,'core'=2,'x'=4,'ylo'=2] {'x','ylo','yhi'}, dimensions={0} | all-to-all | bytes 2621440 | tf_op jit(solution)/shard_map/all_to_all | solution.py:136
  183.3 5.2 %collective-permute-start.10 = (bf16[8,64,1280]{2,1,0:T(8,128)(2,1)S(1)}, bf16[8,64,1280]{2,1,0:T(8,128)(2,1)}, u32[]{:S(2)}, u32[]{:S(2)}) collective-permute-start(bf16[8,64,1280]{2,1,0:T(8,128)(2,1)S(1)} %bitcast.94), channel_id=1, source_target_pairs={{0,8},{8,0},{1,9},{9,1},{2,10},{10,2},{3,11},{11,3},{4,12},{12,4},... | collective-permute-start | bytes 3932168 | tf_op jit(solution)/shard_map/ppermute | solution.py:92
  188.5 1.8 copy.30
  191.1 1.5 select_bitcast_fusion.1
  197.0 8.8 %shard_map.59 = f32[256,256]{1,0:T(8,128)S(1)} custom-call(f32[256,256]{1,0:T(8,128)S(1)} %fusion.20.matrix_ref), custom_call_target="tpu_custom_call" | custom-call | tf_op jit(solution)/shard_map/pallas_call | solution.py:82
  206.1 1.2 fusion.39
  212.9 9.1 %shard_map.60 = f32[256,256]{1,0:T(8,128)S(1)} custom-call(f32[256,256]{1,0:T(8,128)S(1)} %fusion.14.matrix_ref), custom_call_target="tpu_custom_call" | custom-call | tf_op jit(solution)/shard_map/pallas_call | solution.py:82
  223.4 1.2 convolution_subtract_fusion.2
  (81 shorter events, 18.8 us)
Async XLA Ops:
  0.6 19.6 %collective-permute-start = (bf16[16,2048]{1,0:T(8,128)(2,1)}, bf16[16,2048]{1,0:T(8,128)(2,1)S(1)}, u32[]{:S(2)}, u32[]{:S(2)}) collective-permute-start(bf16[16,2048]{1,0:T(8,128)(2,1)} %bitcast.109), channel_id=1, source_target_pairs={{0,240},{16,0},{32,16},{48,32},{64,48},{80,64},{96,80},{112,96},{1... | collective-permute-start | bytes 196616 | tf_op jit(solution)/shard_map/ppermute | solution.py:101
  12.6 7.6 %collective-permute-start.4 = (bf16[16,2048]{1,0:T(8,128)(2,1)}, bf16[16,2048]{1,0:T(8,128)(2,1)S(1)}, u32[]{:S(2)}, u32[]{:S(2)}) collective-permute-start(bf16[16,2048]{1,0:T(8,128)(2,1)} %bitcast.110), channel_id=1, source_target_pairs={{0,16},{16,32},{32,48},{48,64},{64,80},{80,96},{96,112},{112,128},... | collective-permute-start | bytes 196616 | tf_op jit(solution)/shard_map/ppermute | solution.py:101
  14.5 56.2 %collective-permute-start.9 = (bf16[512,2048]{1,0:T(8,128)(2,1)}, bf16[512,2048]{1,0:T(8,128)(2,1)S(1)}, u32[]{:S(2)}, u32[]{:S(2)}) collective-permute-start(bf16[512,2048]{1,0:T(8,128)(2,1)} %param.4), channel_id=1, source_target_pairs={{0,256},{256,0},{1,257},{257,1},{2,258},{258,2},{3,259},{259,3},{4... | collective-permute-start | bytes 6291464 | tf_op jit(solution)/shard_map/ppermute | solution.py:92
  21.1 9.0 %collective-permute-start.1 = (bf16[32,2048]{1,0:T(8,128)(2,1)S(1)}, bf16[32,2048]{1,0:T(8,128)(2,1)S(1)}, u32[]{:S(2)}, u32[]{:S(2)}) collective-permute-start(bf16[32,2048]{1,0:T(8,128)(2,1)S(1)} %get-tuple-element.35), channel_id=1, source_target_pairs={{0,224},{16,240},{32,0},{48,16},{64,32},{80,48},{96,64},{112,80},{... | collective-permute-start | bytes 393224 | tf_op jit(solution)/shard_map/ppermute | solution.py:101
  24.9 9.2 %collective-permute-start.5 = (bf16[32,2048]{1,0:T(8,128)(2,1)S(1)}, bf16[32,2048]{1,0:T(8,128)(2,1)S(1)}, u32[]{:S(2)}, u32[]{:S(2)}) collective-permute-start(bf16[32,2048]{1,0:T(8,128)(2,1)S(1)} %get-tuple-element.34), channel_id=1, source_target_pairs={{0,32},{16,48},{32,64},{48,80},{64,96},{80,112},{96,128},{112,144}... | collective-permute-start | bytes 393224 | tf_op jit(solution)/shard_map/ppermute | solution.py:101
  30.1 6.9 %collective-permute-start.2 = (bf16[32,2048]{1,0:T(8,128)(2,1)S(1)}, bf16[32,2048]{1,0:T(8,128)(2,1)S(1)}, u32[]{:S(2)}, u32[]{:S(2)}) collective-permute-start(bf16[32,2048]{1,0:T(8,128)(2,1)S(1)} %collective-permute-done.1), channel_id=1, source_target_pairs={{0,224},{16,240},{32,0},{48,16},{64,32},{80,48},{96,64},{112,80},{... | collective-permute-start | bytes 393224 | tf_op jit(solution)/shard_map/ppermute | solution.py:101
  34.2 12.7 %collective-permute-start.6 = (bf16[32,2048]{1,0:T(8,128)(2,1)S(1)}, bf16[32,2048]{1,0:T(8,128)(2,1)S(1)}, u32[]{:S(2)}, u32[]{:S(2)}) collective-permute-start(bf16[32,2048]{1,0:T(8,128)(2,1)S(1)} %collective-permute-done.5), channel_id=1, source_target_pairs={{0,32},{16,48},{32,64},{48,80},{64,96},{80,112},{96,128},{112,144}... | collective-permute-start | bytes 393224 | tf_op jit(solution)/shard_map/ppermute | solution.py:101
  37.0 15.4 %collective-permute-start.3 = (bf16[40,2048]{1,0:T(8,128)(2,1)S(1)}, bf16[40,2048]{1,0:T(8,128)(2,1)S(1)}, u32[]{:S(2)}, u32[]{:S(2)}) collective-permute-start(bf16[40,2048]{1,0:T(8,128)(2,1)S(1)} %pad_maximum_fusion.4), channel_id=1, source_target_pairs={{0,208},{16,224},{32,240},{48,0},{64,16},{80,32},{96,48},{112,64},... | collective-permute-start | bytes 491528 | tf_op jit(solution)/shard_map/ppermute | solution.py:101
  46.9 17.6 %collective-permute-start.7 = (bf16[40,2048]{1,0:T(8,128)(2,1)S(1)}, bf16[40,2048]{1,0:T(8,128)(2,1)S(1)}, u32[]{:S(2)}, u32[]{:S(2)}) collective-permute-start(bf16[40,2048]{1,0:T(8,128)(2,1)S(1)} %pad_maximum_fusion.5), channel_id=1, source_target_pairs={{0,48},{16,64},{32,80},{48,96},{64,112},{80,128},{96,144},{112,160... | collective-permute-start | bytes 491528 | tf_op jit(solution)/shard_map/ppermute | solution.py:101
  52.4 17.0 %copy-start.6 = (bf16[512,2048]{1,0:T(8,128)(2,1)S(1)}, bf16[512,2048]{1,0:T(8,128)(2,1)}, u32[]{:S(2)}) copy-start(bf16[512,2048]{1,0:T(8,128)(2,1)} %param.4) | copy-start | bytes 6291460
  64.7 4.7 %collective-permute-start.8 = (bf16[256,2048]{1,0:T(8,128)(2,1)S(1)}, bf16[256,2048]{1,0:T(8,128)(2,1)S(1)}, u32[]{:S(2)}, u32[]{:S(2)}) collective-permute-start(bf16[256,2048]{1,0:T(8,128)(2,1)S(1)} %get-tuple-element.28), channel_id=1, source_target_pairs={{0,8},{8,0},{1,9},{9,1},{2,10},{10,2},{3,11},{11,3},{4,12},{12,4},... | collective-permute-start | bytes 3145736 | tf_op jit(solution)/shard_map/ppermute | solution.py:92
  73.1 19.8 %all-to-all-start = ((bf16[8,128,512]{2,1,0:T(8,128)(2,1)}), bf16[8,128,512]{2,1,0:T(8,128)(2,1)S(1)}, u32[]{:S(2)}, u32[]{:S(2)}) async-start(bf16[8,128,512]{2,1,0:T(8,128)(2,1)} %bitcast.7), calls=%async_computation | async-start | bytes 2097152 | tf_op jit(solution)/shard_map/all_to_all | solution.py:142
  94.5 19.7 %copy-start.4 = (bf16[512,256]{1,0:T(8,128)(2,1)S(1)}, bf16[512,256]{1,0:T(8,128)(2,1)}, u32[]{:S(2)}) copy-start(bf16[512,256]{1,0:T(8,128)(2,1)} %param.7) | copy-start | bytes 786436
  94.5 18.7 %all-to-all-start.1 = ((bf16[16,64,512]{2,1,0:T(8,128)(2,1)}), bf16[16,64,512]{2,1,0:T(8,128)(2,1)S(1)}, u32[]{:S(2)}, u32[]{:S(2)}) async-start(bf16[16,64,512]{2,1,0:T(8,128)(2,1)} %bitcast.10), calls=%async_computation.1 | async-start | bytes 2097152 | tf_op jit(solution)/shard_map/all_to_all | solution.py:177
  113.3 0.8 copy-start
  113.4 1.2 copy-start.2
  183.3 7.8 %collective-permute-start.10 = (bf16[8,64,1280]{2,1,0:T(8,128)(2,1)S(1)}, bf16[8,64,1280]{2,1,0:T(8,128)(2,1)}, u32[]{:S(2)}, u32[]{:S(2)}) collective-permute-start(bf16[8,64,1280]{2,1,0:T(8,128)(2,1)S(1)} %bitcast.94), channel_id=1, source_target_pairs={{0,8},{8,0},{1,9},{9,1},{2,10},{10,2},{3,11},{11,3},{4,12},{12,4},... | collective-permute-start | bytes 3932168 | tf_op jit(solution)/shard_map/ppermute | solution.py:92
  222.0 1.3 copy-start.1
  222.0 1.3 copy-start.3
  222.1 1.3 copy-start.5

commit v4 on v3

--- a/solution.py
+++ b/solution.py
@@ -118,15 +118,12 @@
     below_2 = shift(jnp.concatenate([down_t, below_1]), "z", 2)
     above_2 = shift(jnp.concatenate([down_t, above_1]), "z", -2)
     below_4, above_4 = shift(below_2, "z", 2), shift(above_2, "z", -2)
-    below_6 = shift(jnp.concatenate([below_2[n:], below_4[: n + half]]), "z", 3)
-    above_6 = shift(
-        jnp.concatenate([above_2[n:], above_4[:n], above_4[n + half :]]), "z", -3
-    )
-    above = [down_t, above_1, above_2, above_4, above_6[: 2 * n]]
-    far = [below_6[2 * n :], above_6[2 * n :]]
+    below_6, above_6 = shift(below_4, "z", 2), shift(above_4, "z", -2)
+    far = [shift(below_4[n : n + half], "z", 3), shift(above_4[n + half :], "z", -3)]
+    above = [down_t, above_1, above_2, above_4, above_6]
     below = []
     for pair in (below_6, below_4, below_2):
-        below += [pair[n : 2 * n], pair[:n]]
+        below += [pair[n:], pair[:n]]
     return jnp.concatenate(above + far + below + [below_1])
 
 

time: 226 us -> 234 us (1.035)
  starting transfers between devices: 58.3 us -> 67.2 us
  waiting for transfers between devices: 52.7 us -> 49.7 us
    ppermute x8 -> x10, starting transfers between devices: 38 us -> 43 us  [shift(): return lax.ppermute(value, axis, [(i, (i + by) % n) for i in range(n)])]
    ppermute x8 -> x10, waiting for transfers between devices: 19 us -> 14.2 us  [shift(): return lax.ppermute(value, axis, [(i, (i + by) % n) for i in range(n)])]
    ppermute x3, starting transfers between devices: 12.4 us -> 15.8 us  [swap(): return lax.ppermute(value, axis, [(0, 1), (1, 0)])]
  transfers between devices with their start and end apart: 13 -> 15, of which waited for: 8 -> 8; matrix products, arithmetic and copies ran while one was open for 2% -> 2% of each run, Pallas kernels for 0% -> 0%
where the time goes in v4:
time: 234 us; the launch traced here: 233 us
  blocking collectives  70 us (30%)
  starting transfers between devices  67.2 us (29%)
  waiting for transfers between devices  49.7 us (21%)
  Pallas kernels  17.9 us (8%)
  matrix products  16.6 us (7%)
  local copies, waits for them, and re-layouts  5.87 us (3%)
  other arithmetic  4.22 us (2%)
    ppermute x10, starting transfers between devices, shift(): return lax.ppermute(value, axis, [(i, (i + by) % n) for i in range(n)])  43 us
    all_to_all x2, blocking collectives, gather_by_exchange(): return lax.all_to_all(spread, axes, 0, 0, tiled=True)  36.3 us
    all_to_all x2, blocking collectives, sum_by_exchange(): lax.all_to_all(parts, axes, 0, 0, tiled=True).astype(f32)  33.7 us
    pallas_call x2, Pallas kernels, invert(): pl.pallas_call(invert_kernel, out_shape=jax.ShapeDtypeStruct(matrix.shape...  17.9 us
    all_to_all x1, waiting for transfers between devices, on_device(): lax.all_to_all(spread.reshape(2 * nf, tokens // nf, rank // 2), plane, 0,...  16.7 us
    dot_general x23, matrix products, dot(): lax.dot_general(a, b, (((ca,), (cb,)), ((), ())), precision=precision, pr...  16.6 us
    ppermute x3, starting transfers between devices, swap(): return lax.ppermute(value, axis, [(0, 1), (1, 0)])  15.8 us
    all_to_all x1, waiting for transfers between devices, sum_by_exchange(): lax.all_to_all(parts, axes, 0, 0, tiled=True).astype(f32)  15.7 us
  transfers between devices with their start and end apart: 15, of which 8 were waited for; matrix products, arithmetic and copies ran while one was open for 2% of the time, Pallas kernels for 0%

profile of v4, /device:TPU:1, one launch (start us, length us, event | category | flops | bytes accessed | tf_op | source)
XLA Modules:
  0.0 232.7 jit_solution(16805282171562578178)
XLA Ops:
  0.6 12.0 %collective-permute-start = (bf16[16,2048]{1,0:T(8,128)(2,1)}, bf16[16,2048]{1,0:T(8,128)(2,1)S(1)}, u32[]{:S(2)}, u32[]{:S(2)}) collective-permute-start(bf16[16,2048]{1,0:T(8,128)(2,1)} %bitcast.109), channel_id=1, source_target_pairs={{0,240},{16,0},{32,16},{48,32},{64,48},{80,64},{96,80},{112,96},{1... | collective-permute-start | bytes 196616 | tf_op jit(solution)/shard_map/ppermute | solution.py:101
  12.6 1.9 collective-permute-start.4
  14.5 4.8 %collective-permute-start.11 = (bf16[512,2048]{1,0:T(8,128)(2,1)}, bf16[512,2048]{1,0:T(8,128)(2,1)S(1)}, u32[]{:S(2)}, u32[]{:S(2)}) collective-permute-start(bf16[512,2048]{1,0:T(8,128)(2,1)} %param.4), channel_id=1, source_target_pairs={{0,256},{256,0},{1,257},{257,1},{2,258},{258,2},{3,259},{259,3},{4... | collective-permute-start | bytes 6291464 | tf_op jit(solution)/shard_map/ppermute | solution.py:92
  21.1 3.8 %collective-permute-start.1 = (bf16[32,2048]{1,0:T(8,128)(2,1)S(1)}, bf16[32,2048]{1,0:T(8,128)(2,1)S(1)}, u32[]{:S(2)}, u32[]{:S(2)}) collective-permute-start(bf16[32,2048]{1,0:T(8,128)(2,1)S(1)} %get-tuple-element.31), channel_id=1, source_target_pairs={{0,224},{16,240},{32,0},{48,16},{64,32},{80,48},{96,64},{112,80},{... | collective-permute-start | bytes 393224 | tf_op jit(solution)/shard_map/ppermute | solution.py:101
  24.9 2.4 %collective-permute-start.5 = (bf16[32,2048]{1,0:T(8,128)(2,1)S(1)}, bf16[32,2048]{1,0:T(8,128)(2,1)S(1)}, u32[]{:S(2)}, u32[]{:S(2)}) collective-permute-start(bf16[32,2048]{1,0:T(8,128)(2,1)S(1)} %get-tuple-element.30), channel_id=1, source_target_pairs={{0,32},{16,48},{32,64},{48,80},{64,96},{80,112},{96,128},{112,144}... | collective-permute-start | bytes 393224 | tf_op jit(solution)/shard_map/ppermute | solution.py:101
  27.3 2.8 %collective-permute-done.1 = bf16[32,2048]{1,0:T(8,128)(2,1)S(1)} collective-permute-done((bf16[32,2048]{1,0:T(8,128)(2,1)S(1)}, bf16[32,2048]{1,0:T(8,128)(2,1)S(1)}, u32[]{:S(2)}, u32[]{:S(2)}) %collective-permute-start.1) | collective-permute-done | bytes 131104 | tf_op jit(solution)/shard_map/ppermute | solution.py:101
  30.1 4.0 %collective-permute-start.2 = (bf16[32,2048]{1,0:T(8,128)(2,1)S(1)}, bf16[32,2048]{1,0:T(8,128)(2,1)S(1)}, u32[]{:S(2)}, u32[]{:S(2)}) collective-permute-start(bf16[32,2048]{1,0:T(8,128)(2,1)S(1)} %collective-permute-done.1), channel_id=1, source_target_pairs={{0,224},{16,240},{32,0},{48,16},{64,32},{80,48},{96,64},{112,80},{... | collective-permute-start | bytes 393224 | tf_op jit(solution)/shard_map/ppermute | solution.py:101
  34.1 2.1 collective-permute-start.6
  36.3 6.0 %collective-permute-done.6 = bf16[32,2048]{1,0:T(8,128)(2,1)S(1)} collective-permute-done((bf16[32,2048]{1,0:T(8,128)(2,1)S(1)}, bf16[32,2048]{1,0:T(8,128)(2,1)S(1)}, u32[]{:S(2)}, u32[]{:S(2)}) %collective-permute-start.6) | collective-permute-done | bytes 131104 | tf_op jit(solution)/shard_map/ppermute | solution.py:101
  42.3 6.0 %collective-permute-start.7 = (bf16[8,2048]{1,0:T(8,128)(2,1)S(1)}, bf16[8,2048]{1,0:T(8,128)(2,1)S(1)}, u32[]{:S(2)}, u32[]{:S(2)}) collective-permute-start(bf16[8,2048]{1,0:T(8,128)(2,1)S(1)} %slice.64), channel_id=1, source_target_pairs={{0,48},{16,64},{32,80},{48,96},{64,112},{80,128},{96,144},{112,160... | collective-permute-start | bytes 98312 | tf_op jit(solution)/shard_map/ppermute | solution.py:101
  48.2 4.6 %collective-permute-start.8 = (bf16[8,2048]{1,0:T(8,128)(2,1)S(1)}, bf16[8,2048]{1,0:T(8,128)(2,1)S(1)}, u32[]{:S(2)}, u32[]{:S(2)}) collective-permute-start(bf16[8,2048]{1,0:T(8,128)(2,1)S(1)} %slice.65), channel_id=1, source_target_pairs={{0,208},{16,224},{32,240},{48,0},{64,16},{80,32},{96,48},{112,64},... | collective-permute-start | bytes 98312 | tf_op jit(solution)/shard_map/ppermute | solution.py:101
  52.9 3.7 %collective-permute-start.3 = (bf16[32,2048]{1,0:T(8,128)(2,1)S(1)}, bf16[32,2048]{1,0:T(8,128)(2,1)S(1)}, u32[]{:S(2)}, u32[]{:S(2)}) collective-permute-start(bf16[32,2048]{1,0:T(8,128)(2,1)S(1)} %collective-permute-done.2), channel_id=1, source_target_pairs={{0,224},{16,240},{32,0},{48,16},{64,32},{80,48},{96,64},{112,80},{... | collective-permute-start | bytes 393224 | tf_op jit(solution)/shard_map/ppermute | solution.py:101
  56.6 2.5 %collective-permute-start.9 = (bf16[32,2048]{1,0:T(8,128)(2,1)S(1)}, bf16[32,2048]{1,0:T(8,128)(2,1)S(1)}, u32[]{:S(2)}, u32[]{:S(2)}) collective-permute-start(bf16[32,2048]{1,0:T(8,128)(2,1)S(1)} %collective-permute-done.6), channel_id=1, source_target_pairs={{0,32},{16,48},{32,64},{48,80},{64,96},{80,112},{96,128},{112,144}... | collective-permute-start | bytes 393224 | tf_op jit(solution)/shard_map/ppermute | solution.py:101
  60.2 4.5 %collective-permute-done.9 = bf16[32,2048]{1,0:T(8,128)(2,1)S(1)} collective-permute-done((bf16[32,2048]{1,0:T(8,128)(2,1)S(1)}, bf16[32,2048]{1,0:T(8,128)(2,1)S(1)}, u32[]{:S(2)}, u32[]{:S(2)}) %collective-permute-start.9) | collective-permute-done | bytes 131104 | tf_op jit(solution)/shard_map/ppermute | solution.py:101
  64.8 5.8 %collective-permute-start.10 = (bf16[256,2048]{1,0:T(8,128)(2,1)S(1)}, bf16[256,2048]{1,0:T(8,128)(2,1)S(1)}, u32[]{:S(2)}, u32[]{:S(2)}) collective-permute-start(bf16[256,2048]{1,0:T(8,128)(2,1)S(1)} %get-tuple-element.24), channel_id=1, source_target_pairs={{0,8},{8,0},{1,9},{9,1},{2,10},{10,2},{3,11},{11,3},{4,12},{12,4},... | collective-permute-start | bytes 3145736 | tf_op jit(solution)/shard_map/ppermute | solution.py:92
  70.7 2.3 collective-permute-done.10
  73.0 1.3 convolution_convert_fusion.2
  74.3 1.3 convolution_convert_fusion.1
  76.7 4.1 %all-to-all-start = ((bf16[8,128,512]{2,1,0:T(8,128)(2,1)}), bf16[8,128,512]{2,1,0:T(8,128)(2,1)S(1)}, u32[]{:S(2)}, u32[]{:S(2)}) async-start(bf16[8,128,512]{2,1,0:T(8,128)(2,1)} %bitcast.7), calls=%async_computation | async-start | bytes 2097152 | tf_op jit(solution)/shard_map/all_to_all | solution.py:139
  80.8 15.7 %all-to-all-done = bf16[8,128,512]{2,1,0:T(8,128)(2,1)S(1)} async-done(((bf16[8,128,512]{2,1,0:T(8,128)(2,1)}), bf16[8,128,512]{2,1,0:T(8,128)(2,1)S(1)}, u32[]{:S(2)}, u32[]{:S(2)}) %all-to-all-start) | async-done | bytes 1048608 | tf_op jit(solution)/shard_map/all_to_all | solution.py:139
  98.1 4.2 %all-to-all-start.1 = ((bf16[16,64,512]{2,1,0:T(8,128)(2,1)}), bf16[16,64,512]{2,1,0:T(8,128)(2,1)S(1)}, u32[]{:S(2)}, u32[]{:S(2)}) async-start(bf16[16,64,512]{2,1,0:T(8,128)(2,1)} %bitcast.10), calls=%async_computation.1 | async-start | bytes 2097152 | tf_op jit(solution)/shard_map/all_to_all | solution.py:174
  102.3 16.7 %all-to-all-done.1 = bf16[16,64,512]{2,1,0:T(8,128)(2,1)S(1)} async-done(((bf16[16,64,512]{2,1,0:T(8,128)(2,1)}), bf16[16,64,512]{2,1,0:T(8,128)(2,1)S(1)}, u32[]{:S(2)}, u32[]{:S(2)}) %all-to-all-start.1) | async-done | bytes 1048608 | tf_op jit(solution)/shard_map/all_to_all | solution.py:174
  120.3 13.7 %all_to_all.30 = bf16[4,32,1280]{2,1,0:T(8,128)(2,1)S(1)} all-to-all(bf16[4,32,1280]{2,1,0:T(8,128)(2,1)S(1)} %bitcast.108), channel_id=1, replica_groups=mesh['yhi'=2,'z'=16,'core'=2,'x'=4,'ylo'=2] {'core','yhi'}, dimensions={0} | all-to-all | bytes 655360 | tf_op jit(solution)/shard_map/all_to_all | solution.py:139
  134.1 19.9 %all_to_all.31 = bf16[16,2,1280]{2,1,0:T(2,128)(2,1)S(1)} all-to-all(bf16[16,2,1280]{2,1,0:T(2,128)(2,1)S(1)} %reshape.49), channel_id=1, replica_groups=mesh['yhi'=2,'z'=16,'core'=2,'x'=4,'ylo'=2] {'z'}, dimensions={0} | all-to-all | bytes 163840 | tf_op jit(solution)/shard_map/all_to_all | solution.py:139
  154.2 15.8 %all_to_all.32 = bf16[16,2,1280]{2,1,0:T(2,128)(2,1)S(1)} all-to-all(bf16[16,2,1280]{2,1,0:T(2,128)(2,1)S(1)} %broadcast_in_dim.9), channel_id=1, replica_groups=mesh['yhi'=2,'z'=16,'core'=2,'x'=4,'ylo'=2] {'z'}, dimensions={0} | all-to-all | bytes 163840 | tf_op jit(solution)/shard_map/all_to_all | solution.py:133
  170.1 20.5 %all_to_all.33 = bf16[16,32,1280]{2,1,0:T(8,128)(2,1)S(1)} all-to-all(bf16[16,32,1280]{2,1,0:T(8,128)(2,1)S(1)} %broadcast_in_dim.22), channel_id=1, replica_groups=mesh['yhi'=2,'z'=16,'core'=2,'x'=4,'ylo'=2] {'x','ylo','yhi'}, dimensions={0} | all-to-all | bytes 2621440 | tf_op jit(solution)/shard_map/all_to_all | solution.py:133
  190.7 5.2 %collective-permute-start.12 = (bf16[8,64,1280]{2,1,0:T(8,128)(2,1)S(1)}, bf16[8,64,1280]{2,1,0:T(8,128)(2,1)}, u32[]{:S(2)}, u32[]{:S(2)}) collective-permute-start(bf16[8,64,1280]{2,1,0:T(8,128)(2,1)S(1)} %bitcast.94), channel_id=1, source_target_pairs={{0,8},{8,0},{1,9},{9,1},{2,10},{10,2},{3,11},{11,3},{4,12},{12,4},... | collective-permute-start | bytes 3932168 | tf_op jit(solution)/shard_map/ppermute | solution.py:92
  195.8 1.8 copy.30
  198.4 1.5 select_bitcast_fusion.1
  204.3 8.8 %shard_map.59 = f32[256,256]{1,0:T(8,128)S(1)} custom-call(f32[256,256]{1,0:T(8,128)S(1)} %fusion.20.matrix_ref), custom_call_target="tpu_custom_call" | custom-call | tf_op jit(solution)/shard_map/pallas_call | solution.py:82
  213.5 1.2 fusion.39
  220.3 9.1 %shard_map.60 = f32[256,256]{1,0:T(8,128)S(1)} custom-call(f32[256,256]{1,0:T(8,128)S(1)} %fusion.14.matrix_ref), custom_call_target="tpu_custom_call" | custom-call | tf_op jit(solution)/shard_map/pallas_call | solution.py:82
  (80 shorter events, 21.5 us)
Async XLA Ops:
  0.6 19.6 %collective-permute-start = (bf16[16,2048]{1,0:T(8,128)(2,1)}, bf16[16,2048]{1,0:T(8,128)(2,1)S(1)}, u32[]{:S(2)}, u32[]{:S(2)}) collective-permute-start(bf16[16,2048]{1,0:T(8,128)(2,1)} %bitcast.109), channel_id=1, source_target_pairs={{0,240},{16,0},{32,16},{48,32},{64,48},{80,64},{96,80},{112,96},{1... | collective-permute-start | bytes 196616 | tf_op jit(solution)/shard_map/ppermute | solution.py:101
  12.6 7.6 %collective-permute-start.4 = (bf16[16,2048]{1,0:T(8,128)(2,1)}, bf16[16,2048]{1,0:T(8,128)(2,1)S(1)}, u32[]{:S(2)}, u32[]{:S(2)}) collective-permute-start(bf16[16,2048]{1,0:T(8,128)(2,1)} %bitcast.110), channel_id=1, source_target_pairs={{0,16},{16,32},{32,48},{48,64},{64,80},{80,96},{96,112},{112,128},... | collective-permute-start | bytes 196616 | tf_op jit(solution)/shard_map/ppermute | solution.py:101
  14.5 59.8 %collective-permute-start.11 = (bf16[512,2048]{1,0:T(8,128)(2,1)}, bf16[512,2048]{1,0:T(8,128)(2,1)S(1)}, u32[]{:S(2)}, u32[]{:S(2)}) collective-permute-start(bf16[512,2048]{1,0:T(8,128)(2,1)} %param.4), channel_id=1, source_target_pairs={{0,256},{256,0},{1,257},{257,1},{2,258},{258,2},{3,259},{259,3},{4... | collective-permute-start | bytes 6291464 | tf_op jit(solution)/shard_map/ppermute | solution.py:92
  21.1 9.0 %collective-permute-start.1 = (bf16[32,2048]{1,0:T(8,128)(2,1)S(1)}, bf16[32,2048]{1,0:T(8,128)(2,1)S(1)}, u32[]{:S(2)}, u32[]{:S(2)}) collective-permute-start(bf16[32,2048]{1,0:T(8,128)(2,1)S(1)} %get-tuple-element.31), channel_id=1, source_target_pairs={{0,224},{16,240},{32,0},{48,16},{64,32},{80,48},{96,64},{112,80},{... | collective-permute-start | bytes 393224 | tf_op jit(solution)/shard_map/ppermute | solution.py:101
  24.9 9.2 %collective-permute-start.5 = (bf16[32,2048]{1,0:T(8,128)(2,1)S(1)}, bf16[32,2048]{1,0:T(8,128)(2,1)S(1)}, u32[]{:S(2)}, u32[]{:S(2)}) collective-permute-start(bf16[32,2048]{1,0:T(8,128)(2,1)S(1)} %get-tuple-element.30), channel_id=1, source_target_pairs={{0,32},{16,48},{32,64},{48,80},{64,96},{80,112},{96,128},{112,144}... | collective-permute-start | bytes 393224 | tf_op jit(solution)/shard_map/ppermute | solution.py:101
  30.1 18.1 %collective-permute-start.2 = (bf16[32,2048]{1,0:T(8,128)(2,1)S(1)}, bf16[32,2048]{1,0:T(8,128)(2,1)S(1)}, u32[]{:S(2)}, u32[]{:S(2)}) collective-permute-start(bf16[32,2048]{1,0:T(8,128)(2,1)S(1)} %collective-permute-done.1), channel_id=1, source_target_pairs={{0,224},{16,240},{32,0},{48,16},{64,32},{80,48},{96,64},{112,80},{... | collective-permute-start | bytes 393224 | tf_op jit(solution)/shard_map/ppermute | solution.py:101
  34.1 8.1 %collective-permute-start.6 = (bf16[32,2048]{1,0:T(8,128)(2,1)S(1)}, bf16[32,2048]{1,0:T(8,128)(2,1)S(1)}, u32[]{:S(2)}, u32[]{:S(2)}) collective-permute-start(bf16[32,2048]{1,0:T(8,128)(2,1)S(1)} %collective-permute-done.5), channel_id=1, source_target_pairs={{0,32},{16,48},{32,64},{48,80},{64,96},{80,112},{96,128},{112,144}... | collective-permute-start | bytes 393224 | tf_op jit(solution)/shard_map/ppermute | solution.py:101
  42.3 17.9 %collective-permute-start.7 = (bf16[8,2048]{1,0:T(8,128)(2,1)S(1)}, bf16[8,2048]{1,0:T(8,128)(2,1)S(1)}, u32[]{:S(2)}, u32[]{:S(2)}) collective-permute-start(bf16[8,2048]{1,0:T(8,128)(2,1)S(1)} %slice.64), channel_id=1, source_target_pairs={{0,48},{16,64},{32,80},{48,96},{64,112},{80,128},{96,144},{112,160... | collective-permute-start | bytes 98312 | tf_op jit(solution)/shard_map/ppermute | solution.py:101
  48.2 11.9 %collective-permute-start.8 = (bf16[8,2048]{1,0:T(8,128)(2,1)S(1)}, bf16[8,2048]{1,0:T(8,128)(2,1)S(1)}, u32[]{:S(2)}, u32[]{:S(2)}) collective-permute-start(bf16[8,2048]{1,0:T(8,128)(2,1)S(1)} %slice.65), channel_id=1, source_target_pairs={{0,208},{16,224},{32,240},{48,0},{64,16},{80,32},{96,48},{112,64},... | collective-permute-start | bytes 98312 | tf_op jit(solution)/shard_map/ppermute | solution.py:101
  52.9 7.3 %collective-permute-start.3 = (bf16[32,2048]{1,0:T(8,128)(2,1)S(1)}, bf16[32,2048]{1,0:T(8,128)(2,1)S(1)}, u32[]{:S(2)}, u32[]{:S(2)}) collective-permute-start(bf16[32,2048]{1,0:T(8,128)(2,1)S(1)} %collective-permute-done.2), channel_id=1, source_target_pairs={{0,224},{16,240},{32,0},{48,16},{64,32},{80,48},{96,64},{112,80},{... | collective-permute-start | bytes 393224 | tf_op jit(solution)/shard_map/ppermute | solution.py:101
  56.6 8.1 %collective-permute-start.9 = (bf16[32,2048]{1,0:T(8,128)(2,1)S(1)}, bf16[32,2048]{1,0:T(8,128)(2,1)S(1)}, u32[]{:S(2)}, u32[]{:S(2)}) collective-permute-start(bf16[32,2048]{1,0:T(8,128)(2,1)S(1)} %collective-permute-done.6), channel_id=1, source_target_pairs={{0,32},{16,48},{32,64},{48,80},{64,96},{80,112},{96,128},{112,144}... | collective-permute-start | bytes 393224 | tf_op jit(solution)/shard_map/ppermute | solution.py:101
  60.1 12.9 %copy-start.6 = (bf16[512,2048]{1,0:T(8,128)(2,1)S(1)}, bf16[512,2048]{1,0:T(8,128)(2,1)}, u32[]{:S(2)}) copy-start(bf16[512,2048]{1,0:T(8,128)(2,1)} %param.4) | copy-start | bytes 6291460
  64.8 8.1 %collective-permute-start.10 = (bf16[256,2048]{1,0:T(8,128)(2,1)S(1)}, bf16[256,2048]{1,0:T(8,128)(2,1)S(1)}, u32[]{:S(2)}, u32[]{:S(2)}) collective-permute-start(bf16[256,2048]{1,0:T(8,128)(2,1)S(1)} %get-tuple-element.24), channel_id=1, source_target_pairs={{0,8},{8,0},{1,9},{9,1},{2,10},{10,2},{3,11},{11,3},{4,12},{12,4},... | collective-permute-start | bytes 3145736 | tf_op jit(solution)/shard_map/ppermute | solution.py:92
  76.7 19.9 %all-to-all-start = ((bf16[8,128,512]{2,1,0:T(8,128)(2,1)}), bf16[8,128,512]{2,1,0:T(8,128)(2,1)S(1)}, u32[]{:S(2)}, u32[]{:S(2)}) async-start(bf16[8,128,512]{2,1,0:T(8,128)(2,1)} %bitcast.7), calls=%async_computation | async-start | bytes 2097152 | tf_op jit(solution)/shard_map/all_to_all | solution.py:139
  98.0 21.8 %copy-start.4 = (bf16[512,256]{1,0:T(8,128)(2,1)S(1)}, bf16[512,256]{1,0:T(8,128)(2,1)}, u32[]{:S(2)}) copy-start(bf16[512,256]{1,0:T(8,128)(2,1)} %param.7) | copy-start | bytes 786436
  98.1 20.9 %all-to-all-start.1 = ((bf16[16,64,512]{2,1,0:T(8,128)(2,1)}), bf16[16,64,512]{2,1,0:T(8,128)(2,1)S(1)}, u32[]{:S(2)}, u32[]{:S(2)}) async-start(bf16[16,64,512]{2,1,0:T(8,128)(2,1)} %bitcast.10), calls=%async_computation.1 | async-start | bytes 2097152 | tf_op jit(solution)/shard_map/all_to_all | solution.py:174
  119.1 0.8 copy-start
  119.1 1.2 copy-start.2
  190.7 7.8 %collective-permute-start.12 = (bf16[8,64,1280]{2,1,0:T(8,128)(2,1)S(1)}, bf16[8,64,1280]{2,1,0:T(8,128)(2,1)}, u32[]{:S(2)}, u32[]{:S(2)}) collective-permute-start(bf16[8,64,1280]{2,1,0:T(8,128)(2,1)S(1)} %bitcast.94), channel_id=1, source_target_pairs={{0,8},{8,0},{1,9},{9,1},{2,10},{10,2},{3,11},{11,3},{4,12},{12,4},... | collective-permute-start | bytes 3932168 | tf_op jit(solution)/shard_map/ppermute | solution.py:92
  229.4 1.3 copy-start.1
  229.4 1.3 copy-start.3
  229.4 1.3 copy-start.5

commit v5 on v4

--- a/solution.py
+++ b/solution.py
@@ -119,7 +119,7 @@
     above_2 = shift(jnp.concatenate([down_t, above_1]), "z", -2)
     below_4, above_4 = shift(below_2, "z", 2), shift(above_2, "z", -2)
     below_6, above_6 = shift(below_4, "z", 2), shift(above_4, "z", -2)
-    far = [shift(below_4[n : n + half], "z", 3), shift(above_4[n + half :], "z", -3)]
+    far = [shift(below_6[n : n + half], "z", 1), shift(above_6[n + half :], "z", -1)]
     above = [down_t, above_1, above_2, above_4, above_6]
     below = []
     for pair in (below_6, below_4, below_2):
@@ -198,9 +198,7 @@
     inverse = invert(curvature)
     step = dot(inverse, gram_now, 1, 0, three)
 
-    coarse = image_back.astype(bf16)
-    fine = (image_back - coarse.astype(f32)).astype(bf16)
-    curved = dot(rows, coarse, 0, 0) + dot(rows, fine, 0, 0)
+    curved = dot(rows, image_back.astype(bf16), 0, 0)
     descent_next = descent - dot(curved, step, 1, 0, three)
     gram_next = dot(descent_next, descent_next, 0, 0, three)
     mixing = dot(inverse, dot(curved, descent_next, 0, 0, three), 1, 0, three)

time: 234 us -> 230 us (0.983)
    dot_general x23 -> x22, matrix products: 16.6 us -> 15.9 us  [dot(): lax.dot_general(a, b, (((ca,), (cb,)), ((), ())), precision=precision, pr...]
where the time goes in v5:
time: 230 us
  starting transfers between devices  68.5 us (30%)
  blocking collectives  67.7 us (29%)
  waiting for transfers between devices  48.5 us (21%)
  Pallas kernels  17.6 us (8%)
  matrix products  15.9 us (7%)
  local copies, waits for them, and re-layouts  5.87 us (3%)
  other arithmetic  4.22 us (2%)
    ppermute x10, starting transfers between devices, shift(): return lax.ppermute(value, axis, [(i, (i + by) % n) for i in range(n)])  42.5 us
    all_to_all x2, blocking collectives, gather_by_exchange(): return lax.all_to_all(spread, axes, 0, 0, tiled=True)  35.8 us
    all_to_all x2, blocking collectives, sum_by_exchange(): lax.all_to_all(parts, axes, 0, 0, tiled=True).astype(f32)  31.9 us
    pallas_call x2, Pallas kernels, invert(): pl.pallas_call(invert_kernel, out_shape=jax.ShapeDtypeStruct(matrix.shape...  17.6 us
    ppermute x3, starting transfers between devices, swap(): return lax.ppermute(value, axis, [(0, 1), (1, 0)])  17.2 us
    all_to_all x1, waiting for transfers between devices, on_device(): lax.all_to_all(spread.reshape(2 * nf, tokens // nf, rank // 2), plane, 0,...  17.1 us
    dot_general x22, matrix products, dot(): lax.dot_general(a, b, (((ca,), (cb,)), ((), ())), precision=precision, pr...  15.9 us
    all_to_all x1, waiting for transfers between devices, sum_by_exchange(): lax.all_to_all(parts, axes, 0, 0, tiled=True).astype(f32)  15.7 us
  transfers between devices with their start and end apart: 15, of which 8 were waited for; matrix products, arithmetic and copies ran while one was open for 2% of the time, Pallas kernels for 0%

profile of v5, /device:TPU:1, one launch (start us, length us, event | category | flops | bytes accessed | tf_op | source)
XLA Modules:
  0.0 229.6 jit_solution(7122507382276952880)
XLA Ops:
  0.6 12.0 %collective-permute-start = (bf16[16,2048]{1,0:T(8,128)(2,1)}, bf16[16,2048]{1,0:T(8,128)(2,1)S(1)}, u32[]{:S(2)}, u32[]{:S(2)}) collective-permute-start(bf16[16,2048]{1,0:T(8,128)(2,1)} %bitcast.107), channel_id=1, source_target_pairs={{0,240},{16,0},{32,16},{48,32},{64,48},{80,64},{96,80},{112,96},{1... | collective-permute-start | bytes 196616 | tf_op jit(solution)/shard_map/ppermute | solution.py:101
  12.6 1.9 collective-permute-start.4
  14.5 4.8 %collective-permute-start.11 = (bf16[512,2048]{1,0:T(8,128)(2,1)}, bf16[512,2048]{1,0:T(8,128)(2,1)S(1)}, u32[]{:S(2)}, u32[]{:S(2)}) collective-permute-start(bf16[512,2048]{1,0:T(8,128)(2,1)} %param.4), channel_id=1, source_target_pairs={{0,256},{256,0},{1,257},{257,1},{2,258},{258,2},{3,259},{259,3},{4... | collective-permute-start | bytes 6291464 | tf_op jit(solution)/shard_map/ppermute | solution.py:92
  21.1 3.8 %collective-permute-start.1 = (bf16[32,2048]{1,0:T(8,128)(2,1)S(1)}, bf16[32,2048]{1,0:T(8,128)(2,1)S(1)}, u32[]{:S(2)}, u32[]{:S(2)}) collective-permute-start(bf16[32,2048]{1,0:T(8,128)(2,1)S(1)} %get-tuple-element.31), channel_id=1, source_target_pairs={{0,224},{16,240},{32,0},{48,16},{64,32},{80,48},{96,64},{112,80},{... | collective-permute-start | bytes 393224 | tf_op jit(solution)/shard_map/ppermute | solution.py:101
  24.9 2.4 %collective-permute-start.5 = (bf16[32,2048]{1,0:T(8,128)(2,1)S(1)}, bf16[32,2048]{1,0:T(8,128)(2,1)S(1)}, u32[]{:S(2)}, u32[]{:S(2)}) collective-permute-start(bf16[32,2048]{1,0:T(8,128)(2,1)S(1)} %get-tuple-element.30), channel_id=1, source_target_pairs={{0,32},{16,48},{32,64},{48,80},{64,96},{80,112},{96,128},{112,144}... | collective-permute-start | bytes 393224 | tf_op jit(solution)/shard_map/ppermute | solution.py:101
  27.3 2.8 %collective-permute-done.1 = bf16[32,2048]{1,0:T(8,128)(2,1)S(1)} collective-permute-done((bf16[32,2048]{1,0:T(8,128)(2,1)S(1)}, bf16[32,2048]{1,0:T(8,128)(2,1)S(1)}, u32[]{:S(2)}, u32[]{:S(2)}) %collective-permute-start.1) | collective-permute-done | bytes 131104 | tf_op jit(solution)/shard_map/ppermute | solution.py:101
  30.1 4.0 %collective-permute-start.2 = (bf16[32,2048]{1,0:T(8,128)(2,1)S(1)}, bf16[32,2048]{1,0:T(8,128)(2,1)S(1)}, u32[]{:S(2)}, u32[]{:S(2)}) collective-permute-start(bf16[32,2048]{1,0:T(8,128)(2,1)S(1)} %collective-permute-done.1), channel_id=1, source_target_pairs={{0,224},{16,240},{32,0},{48,16},{64,32},{80,48},{96,64},{112,80},{... | collective-permute-start | bytes 393224 | tf_op jit(solution)/shard_map/ppermute | solution.py:101
  34.1 2.1 collective-permute-start.6
  37.0 5.3 %collective-permute-start.3 = (bf16[32,2048]{1,0:T(8,128)(2,1)S(1)}, bf16[32,2048]{1,0:T(8,128)(2,1)S(1)}, u32[]{:S(2)}, u32[]{:S(2)}) collective-permute-start(bf16[32,2048]{1,0:T(8,128)(2,1)S(1)} %collective-permute-done.2), channel_id=1, source_target_pairs={{0,224},{16,240},{32,0},{48,16},{64,32},{80,48},{96,64},{112,80},{... | collective-permute-start | bytes 393224 | tf_op jit(solution)/shard_map/ppermute | solution.py:101
  42.3 1.9 collective-permute-start.7
  44.2 6.2 %collective-permute-done.7 = bf16[32,2048]{1,0:T(8,128)(2,1)S(1)} collective-permute-done((bf16[32,2048]{1,0:T(8,128)(2,1)S(1)}, bf16[32,2048]{1,0:T(8,128)(2,1)S(1)}, u32[]{:S(2)}, u32[]{:S(2)}) %collective-permute-start.7) | collective-permute-done | bytes 131104 | tf_op jit(solution)/shard_map/ppermute | solution.py:101
  50.4 7.1 %collective-permute-start.8 = (bf16[8,2048]{1,0:T(8,128)(2,1)S(1)}, bf16[8,2048]{1,0:T(8,128)(2,1)S(1)}, u32[]{:S(2)}, u32[]{:S(2)}) collective-permute-start(bf16[8,2048]{1,0:T(8,128)(2,1)S(1)} %slice.64), channel_id=1, source_target_pairs={{0,16},{16,32},{32,48},{48,64},{64,80},{80,96},{96,112},{112,128},... | collective-permute-start | bytes 98312 | tf_op jit(solution)/shard_map/ppermute | solution.py:101
  57.5 2.0 collective-permute-start.9
  59.6 2.8 %collective-permute-done.9 = bf16[8,2048]{1,0:T(8,128)(2,1)S(1)} collective-permute-done((bf16[8,2048]{1,0:T(8,128)(2,1)S(1)}, bf16[8,2048]{1,0:T(8,128)(2,1)S(1)}, u32[]{:S(2)}, u32[]{:S(2)}) %collective-permute-start.9) | collective-permute-done | bytes 32800 | tf_op jit(solution)/shard_map/ppermute | solution.py:101
  62.6 6.8 %collective-permute-start.10 = (bf16[256,2048]{1,0:T(8,128)(2,1)S(1)}, bf16[256,2048]{1,0:T(8,128)(2,1)S(1)}, u32[]{:S(2)}, u32[]{:S(2)}) collective-permute-start(bf16[256,2048]{1,0:T(8,128)(2,1)S(1)} %get-tuple-element.24), channel_id=1, source_target_pairs={{0,8},{8,0},{1,9},{9,1},{2,10},{10,2},{3,11},{11,3},{4,12},{12,4},... | collective-permute-start | bytes 3145736 | tf_op jit(solution)/shard_map/ppermute | solution.py:92
  69.4 2.3 collective-permute-done.10
  71.8 1.3 convolution_convert_fusion.2
  73.1 1.3 convolution_convert_fusion.1
  75.4 4.0 %all-to-all-start = ((bf16[8,128,512]{2,1,0:T(8,128)(2,1)}), bf16[8,128,512]{2,1,0:T(8,128)(2,1)S(1)}, u32[]{:S(2)}, u32[]{:S(2)}) async-start(bf16[8,128,512]{2,1,0:T(8,128)(2,1)} %bitcast.7), calls=%async_computation | async-start | bytes 2097152 | tf_op jit(solution)/shard_map/all_to_all | solution.py:139
  79.4 15.7 %all-to-all-done = bf16[8,128,512]{2,1,0:T(8,128)(2,1)S(1)} async-done(((bf16[8,128,512]{2,1,0:T(8,128)(2,1)}), bf16[8,128,512]{2,1,0:T(8,128)(2,1)S(1)}, u32[]{:S(2)}, u32[]{:S(2)}) %all-to-all-start) | async-done | bytes 1048608 | tf_op jit(solution)/shard_map/all_to_all | solution.py:139
  96.7 4.7 %all-to-all-start.1 = ((bf16[16,64,512]{2,1,0:T(8,128)(2,1)}), bf16[16,64,512]{2,1,0:T(8,128)(2,1)S(1)}, u32[]{:S(2)}, u32[]{:S(2)}) async-start(bf16[16,64,512]{2,1,0:T(8,128)(2,1)} %bitcast.10), calls=%async_computation.1 | async-start | bytes 2097152 | tf_op jit(solution)/shard_map/all_to_all | solution.py:174
  101.5 17.1 %all-to-all-done.1 = bf16[16,64,512]{2,1,0:T(8,128)(2,1)S(1)} async-done(((bf16[16,64,512]{2,1,0:T(8,128)(2,1)}), bf16[16,64,512]{2,1,0:T(8,128)(2,1)S(1)}, u32[]{:S(2)}, u32[]{:S(2)}) %all-to-all-start.1) | async-done | bytes 1048608 | tf_op jit(solution)/shard_map/all_to_all | solution.py:174
  119.9 13.9 %all_to_all.30 = bf16[4,32,1280]{2,1,0:T(8,128)(2,1)S(1)} all-to-all(bf16[4,32,1280]{2,1,0:T(8,128)(2,1)S(1)} %bitcast.106), channel_id=1, replica_groups=mesh['yhi'=2,'z'=16,'core'=2,'x'=4,'ylo'=2] {'core','yhi'}, dimensions={0} | all-to-all | bytes 655360 | tf_op jit(solution)/shard_map/all_to_all | solution.py:139
  133.9 18.0 %all_to_all.31 = bf16[16,2,1280]{2,1,0:T(2,128)(2,1)S(1)} all-to-all(bf16[16,2,1280]{2,1,0:T(2,128)(2,1)S(1)} %reshape.49), channel_id=1, replica_groups=mesh['yhi'=2,'z'=16,'core'=2,'x'=4,'ylo'=2] {'z'}, dimensions={0} | all-to-all | bytes 163840 | tf_op jit(solution)/shard_map/all_to_all | solution.py:139
  152.0 15.8 %all_to_all.32 = bf16[16,2,1280]{2,1,0:T(2,128)(2,1)S(1)} all-to-all(bf16[16,2,1280]{2,1,0:T(2,128)(2,1)S(1)} %broadcast_in_dim.9), channel_id=1, replica_groups=mesh['yhi'=2,'z'=16,'core'=2,'x'=4,'ylo'=2] {'z'}, dimensions={0} | all-to-all | bytes 163840 | tf_op jit(solution)/shard_map/all_to_all | solution.py:133
  168.0 20.0 %all_to_all.33 = bf16[16,32,1280]{2,1,0:T(8,128)(2,1)S(1)} all-to-all(bf16[16,32,1280]{2,1,0:T(8,128)(2,1)S(1)} %broadcast_in_dim.22), channel_id=1, replica_groups=mesh['yhi'=2,'z'=16,'core'=2,'x'=4,'ylo'=2] {'x','ylo','yhi'}, dimensions={0} | all-to-all | bytes 2621440 | tf_op jit(solution)/shard_map/all_to_all | solution.py:133
  188.0 5.6 %collective-permute-start.12 = (bf16[8,64,1280]{2,1,0:T(8,128)(2,1)S(1)}, bf16[8,64,1280]{2,1,0:T(8,128)(2,1)}, u32[]{:S(2)}, u32[]{:S(2)}) collective-permute-start(bf16[8,64,1280]{2,1,0:T(8,128)(2,1)S(1)} %bitcast.92), channel_id=1, source_target_pairs={{0,8},{8,0},{1,9},{9,1},{2,10},{10,2},{3,11},{11,3},{4,12},{12,4},... | collective-permute-start | bytes 3932168 | tf_op jit(solution)/shard_map/ppermute | solution.py:92
  193.7 1.8 copy.30
  196.2 1.5 select_bitcast_fusion.1
  202.2 8.8 %shard_map.59 = f32[256,256]{1,0:T(8,128)S(1)} custom-call(f32[256,256]{1,0:T(8,128)S(1)} %fusion.19.matrix_ref), custom_call_target="tpu_custom_call" | custom-call | tf_op jit(solution)/shard_map/pallas_call | solution.py:82
  211.3 1.2 fusion.38
  217.4 8.8 %shard_map.60 = f32[256,256]{1,0:T(8,128)S(1)} custom-call(f32[256,256]{1,0:T(8,128)S(1)} %fusion.16.matrix_ref), custom_call_target="tpu_custom_call" | custom-call | tf_op jit(solution)/shard_map/pallas_call | solution.py:82
  (79 shorter events, 20.4 us)
Async XLA Ops:
  0.6 19.6 %collective-permute-start = (bf16[16,2048]{1,0:T(8,128)(2,1)}, bf16[16,2048]{1,0:T(8,128)(2,1)S(1)}, u32[]{:S(2)}, u32[]{:S(2)}) collective-permute-start(bf16[16,2048]{1,0:T(8,128)(2,1)} %bitcast.107), channel_id=1, source_target_pairs={{0,240},{16,0},{32,16},{48,32},{64,48},{80,64},{96,80},{112,96},{1... | collective-permute-start | bytes 196616 | tf_op jit(solution)/shard_map/ppermute | solution.py:101
  12.6 7.6 %collective-permute-start.4 = (bf16[16,2048]{1,0:T(8,128)(2,1)}, bf16[16,2048]{1,0:T(8,128)(2,1)S(1)}, u32[]{:S(2)}, u32[]{:S(2)}) collective-permute-start(bf16[16,2048]{1,0:T(8,128)(2,1)} %bitcast.108), channel_id=1, source_target_pairs={{0,16},{16,32},{32,48},{48,64},{64,80},{80,96},{96,112},{112,128},... | collective-permute-start | bytes 196616 | tf_op jit(solution)/shard_map/ppermute | solution.py:101
  14.5 58.5 %collective-permute-start.11 = (bf16[512,2048]{1,0:T(8,128)(2,1)}, bf16[512,2048]{1,0:T(8,128)(2,1)S(1)}, u32[]{:S(2)}, u32[]{:S(2)}) collective-permute-start(bf16[512,2048]{1,0:T(8,128)(2,1)} %param.4), channel_id=1, source_target_pairs={{0,256},{256,0},{1,257},{257,1},{2,258},{258,2},{3,259},{259,3},{4... | collective-permute-start | bytes 6291464 | tf_op jit(solution)/shard_map/ppermute | solution.py:92
  21.1 9.0 %collective-permute-start.1 = (bf16[32,2048]{1,0:T(8,128)(2,1)S(1)}, bf16[32,2048]{1,0:T(8,128)(2,1)S(1)}, u32[]{:S(2)}, u32[]{:S(2)}) collective-permute-start(bf16[32,2048]{1,0:T(8,128)(2,1)S(1)} %get-tuple-element.31), channel_id=1, source_target_pairs={{0,224},{16,240},{32,0},{48,16},{64,32},{80,48},{96,64},{112,80},{... | collective-permute-start | bytes 393224 | tf_op jit(solution)/shard_map/ppermute | solution.py:101
  24.9 9.2 %collective-permute-start.5 = (bf16[32,2048]{1,0:T(8,128)(2,1)S(1)}, bf16[32,2048]{1,0:T(8,128)(2,1)S(1)}, u32[]{:S(2)}, u32[]{:S(2)}) collective-permute-start(bf16[32,2048]{1,0:T(8,128)(2,1)S(1)} %get-tuple-element.30), channel_id=1, source_target_pairs={{0,32},{16,48},{32,64},{48,80},{64,96},{80,112},{96,128},{112,144}... | collective-permute-start | bytes 393224 | tf_op jit(solution)/shard_map/ppermute | solution.py:101
  30.1 6.9 %collective-permute-start.2 = (bf16[32,2048]{1,0:T(8,128)(2,1)S(1)}, bf16[32,2048]{1,0:T(8,128)(2,1)S(1)}, u32[]{:S(2)}, u32[]{:S(2)}) collective-permute-start(bf16[32,2048]{1,0:T(8,128)(2,1)S(1)} %collective-permute-done.1), channel_id=1, source_target_pairs={{0,224},{16,240},{32,0},{48,16},{64,32},{80,48},{96,64},{112,80},{... | collective-permute-start | bytes 393224 | tf_op jit(solution)/shard_map/ppermute | solution.py:101
  34.1 8.1 %collective-permute-start.6 = (bf16[32,2048]{1,0:T(8,128)(2,1)S(1)}, bf16[32,2048]{1,0:T(8,128)(2,1)S(1)}, u32[]{:S(2)}, u32[]{:S(2)}) collective-permute-start(bf16[32,2048]{1,0:T(8,128)(2,1)S(1)} %collective-permute-done.5), channel_id=1, source_target_pairs={{0,32},{16,48},{32,64},{48,80},{64,96},{80,112},{96,128},{112,144}... | collective-permute-start | bytes 393224 | tf_op jit(solution)/shard_map/ppermute | solution.py:101
  37.0 20.5 %collective-permute-start.3 = (bf16[32,2048]{1,0:T(8,128)(2,1)S(1)}, bf16[32,2048]{1,0:T(8,128)(2,1)S(1)}, u32[]{:S(2)}, u32[]{:S(2)}) collective-permute-start(bf16[32,2048]{1,0:T(8,128)(2,1)S(1)} %collective-permute-done.2), channel_id=1, source_target_pairs={{0,224},{16,240},{32,0},{48,16},{64,32},{80,48},{96,64},{112,80},{... | collective-permute-start | bytes 393224 | tf_op jit(solution)/shard_map/ppermute | solution.py:101
  42.3 8.2 %collective-permute-start.7 = (bf16[32,2048]{1,0:T(8,128)(2,1)S(1)}, bf16[32,2048]{1,0:T(8,128)(2,1)S(1)}, u32[]{:S(2)}, u32[]{:S(2)}) collective-permute-start(bf16[32,2048]{1,0:T(8,128)(2,1)S(1)} %collective-permute-done.6), channel_id=1, source_target_pairs={{0,32},{16,48},{32,64},{48,80},{64,96},{80,112},{96,128},{112,144}... | collective-permute-start | bytes 393224 | tf_op jit(solution)/shard_map/ppermute | solution.py:101
  50.4 9.2 %collective-permute-start.8 = (bf16[8,2048]{1,0:T(8,128)(2,1)S(1)}, bf16[8,2048]{1,0:T(8,128)(2,1)S(1)}, u32[]{:S(2)}, u32[]{:S(2)}) collective-permute-start(bf16[8,2048]{1,0:T(8,128)(2,1)S(1)} %slice.64), channel_id=1, source_target_pairs={{0,16},{16,32},{32,48},{48,64},{64,80},{80,96},{96,112},{112,128},... | collective-permute-start | bytes 98312 | tf_op jit(solution)/shard_map/ppermute | solution.py:101
  57.5 5.0 %collective-permute-start.9 = (bf16[8,2048]{1,0:T(8,128)(2,1)S(1)}, bf16[8,2048]{1,0:T(8,128)(2,1)S(1)}, u32[]{:S(2)}, u32[]{:S(2)}) collective-permute-start(bf16[8,2048]{1,0:T(8,128)(2,1)S(1)} %slice.65), channel_id=1, source_target_pairs={{0,240},{16,0},{32,16},{48,32},{64,48},{80,64},{96,80},{112,96},{1... | collective-permute-start | bytes 98312 | tf_op jit(solution)/shard_map/ppermute | solution.py:101
  59.6 12.2 %copy-start.6 = (bf16[512,2048]{1,0:T(8,128)(2,1)S(1)}, bf16[512,2048]{1,0:T(8,128)(2,1)}, u32[]{:S(2)}) copy-start(bf16[512,2048]{1,0:T(8,128)(2,1)} %param.4) | copy-start | bytes 6291460
  62.6 9.0 %collective-permute-start.10 = (bf16[256,2048]{1,0:T(8,128)(2,1)S(1)}, bf16[256,2048]{1,0:T(8,128)(2,1)S(1)}, u32[]{:S(2)}, u32[]{:S(2)}) collective-permute-start(bf16[256,2048]{1,0:T(8,128)(2,1)S(1)} %get-tuple-element.24), channel_id=1, source_target_pairs={{0,8},{8,0},{1,9},{9,1},{2,10},{10,2},{3,11},{11,3},{4,12},{12,4},... | collective-permute-start | bytes 3145736 | tf_op jit(solution)/shard_map/ppermute | solution.py:92
  75.4 19.7 %all-to-all-start = ((bf16[8,128,512]{2,1,0:T(8,128)(2,1)}), bf16[8,128,512]{2,1,0:T(8,128)(2,1)S(1)}, u32[]{:S(2)}, u32[]{:S(2)}) async-start(bf16[8,128,512]{2,1,0:T(8,128)(2,1)} %bitcast.7), calls=%async_computation | async-start | bytes 2097152 | tf_op jit(solution)/shard_map/all_to_all | solution.py:139
  96.7 22.8 %copy-start.4 = (bf16[512,256]{1,0:T(8,128)(2,1)S(1)}, bf16[512,256]{1,0:T(8,128)(2,1)}, u32[]{:S(2)}) copy-start(bf16[512,256]{1,0:T(8,128)(2,1)} %param.7) | copy-start | bytes 786436
  96.7 21.9 %all-to-all-start.1 = ((bf16[16,64,512]{2,1,0:T(8,128)(2,1)}), bf16[16,64,512]{2,1,0:T(8,128)(2,1)S(1)}, u32[]{:S(2)}, u32[]{:S(2)}) async-start(bf16[16,64,512]{2,1,0:T(8,128)(2,1)} %bitcast.10), calls=%async_computation.1 | async-start | bytes 2097152 | tf_op jit(solution)/shard_map/all_to_all | solution.py:174
  118.7 0.8 copy-start
  118.7 1.2 copy-start.2
  188.0 8.2 %collective-permute-start.12 = (bf16[8,64,1280]{2,1,0:T(8,128)(2,1)S(1)}, bf16[8,64,1280]{2,1,0:T(8,128)(2,1)}, u32[]{:S(2)}, u32[]{:S(2)}) collective-permute-start(bf16[8,64,1280]{2,1,0:T(8,128)(2,1)S(1)} %bitcast.92), channel_id=1, source_target_pairs={{0,8},{8,0},{1,9},{9,1},{2,10},{10,2},{3,11},{11,3},{4,12},{12,4},... | collective-permute-start | bytes 3932168 | tf_op jit(solution)/shard_map/ppermute | solution.py:92
  226.2 1.3 copy-start.1
  226.2 1.3 copy-start.3
  226.2 1.3 copy-start.5

commit v6 on v3

--- a/solution.py
+++ b/solution.py
@@ -88,6 +88,33 @@
     )(matrix)
 
 
+def join_blocks_kernel(low_ref, high_ref, gram_ref):
+    count, half, _ = low_ref.shape
+    size = 2 * half
+    for i in range(count):
+        top = i * size
+        for k in range(count // 2 + 1):
+            left = (i + k) % count * size
+            low = low_ref[i, :, k * size : (k + 1) * size]
+            high = high_ref[i, :, k * size : (k + 1) * size]
+            gram_ref[top : top + half, left : left + size] = low
+            gram_ref[top + half : top + size, left : left + size] = high
+            if 0 < k < count // 2:
+                block = jnp.concatenate([low.astype(f32), high.astype(f32)])
+                gram_ref[left : left + size, top : top + size] = block.T.astype(bf16)
+
+
+def join_blocks(low, high):
+    rank = 2 * low.shape[0] * low.shape[1]
+    return pl.pallas_call(
+        join_blocks_kernel,
+        out_shape=jax.ShapeDtypeStruct((rank, rank), bf16),
+        in_specs=[pl.BlockSpec(memory_space=pltpu.VMEM)] * 2,
+        out_specs=pl.BlockSpec(memory_space=pltpu.VMEM),
+        compiler_params=pltpu.CompilerParams(vmem_limit_bytes=16 * 1024 * 1024),
+    )(low, high)
+
+
 def swap(value, axis):
     return lax.ppermute(value, axis, [(0, 1), (1, 0)])
 
@@ -181,16 +208,17 @@
 
     rows = precond.reshape(2, nz, 2, narrow, rank).transpose(0, 2, 1, 3, 4).reshape(rank, rank)
 
-    joined_slice = lax.dynamic_slice_in_dim(joined, feat * share, share, 1)
-    total = dot(joined_slice, jnp.concatenate([joined, target], axis=1), 0, 0)
+    count = (nf // 2 + 1) * share
+    wrapped = jnp.concatenate([joined, joined[:, : count - share]], axis=1)
+    window = lax.dynamic_slice_in_dim(wrapped, feat * share, count, 1)
+    total = dot(window[:, :share], jnp.concatenate([window, target], axis=1), 0, 0)
     width = total.shape[1]
     summed = sum_by_exchange(sum_by_exchange(total, ("core", "yhi")), "z").astype(bf16)
     summed = gather_by_exchange(summed, "z").reshape(share // 4, width)
     summed = gather_by_exchange(summed, plane).reshape(nf, share // 2, width)
     low, high = ordered(core == 0, summed, swap(summed, "core"))
-    summed = jnp.stack([low, high], axis=1).reshape(rank, width)
-    gram = summed[:, :rank]
-    back = summed[:, rank:]
+    gram = join_blocks(low, high)
+    back = jnp.stack([low[:, :, count:], high[:, :, count:]], axis=1).reshape(rank, -1)
 
     descent = dot(rows, back, 0, 0)
     gram_now = dot(descent, descent, 0, 0, three)
@@ -201,9 +229,7 @@
     inverse = invert(curvature)
     step = dot(inverse, gram_now, 1, 0, three)
 
-    coarse = image_back.astype(bf16)
-    fine = (image_back - coarse.astype(f32)).astype(bf16)
-    curved = dot(rows, coarse, 0, 0) + dot(rows, fine, 0, 0)
+    curved = dot(rows, image_back.astype(bf16), 0, 0)
     descent_next = descent - dot(curved, step, 1, 0, three)
     gram_next = dot(descent_next, descent_next, 0, 0, three)
     mixing = dot(inverse, dot(curved, descent_next, 0, 0, three), 1, 0, three)

time: 226 us -> 218 us (0.965)
  blocking collectives: 68.4 us -> 60.4 us
    all_to_all x2, blocking collectives: 36.3 us -> 29.8 us  [gather_by_exchange(): return lax.all_to_all(spread, axes, 0, 0, tiled=True)]
    dot_general x23 -> x22, matrix products: 16.6 us -> 15.9 us  [dot(): lax.dot_general(a, b, (((ca,), (cb,)), ((), ())), precision=precision, pr...]
where the time goes in v6:
time: 218 us; the launch traced here: 217 us
  blocking collectives  60.4 us (28%)
  starting transfers between devices  59.5 us (27%)
  waiting for transfers between devices  52.4 us (24%)
  Pallas kernels  18.3 us (8%)
  matrix products  15.9 us (7%)
  local copies, waits for them, and re-layouts  5.11 us (2%)
  other arithmetic  4.57 us (2%)
    ppermute x8, starting transfers between devices, shift(): return lax.ppermute(value, axis, [(i, (i + by) % n) for i in range(n)])  38 us
    all_to_all x2, blocking collectives, sum_by_exchange(): lax.all_to_all(parts, axes, 0, 0, tiled=True).astype(f32)  30.7 us
    all_to_all x2, blocking collectives, gather_by_exchange(): return lax.all_to_all(spread, axes, 0, 0, tiled=True)  29.8 us
    ppermute x8, waiting for transfers between devices, shift(): return lax.ppermute(value, axis, [(i, (i + by) % n) for i in range(n)])  19 us
    pallas_call x2, Pallas kernels, invert(): pl.pallas_call(invert_kernel, out_shape=jax.ShapeDtypeStruct(matrix.shape...  17.9 us
    dot_general x22, matrix products, dot(): lax.dot_general(a, b, (((ca,), (cb,)), ((), ())), precision=precision, pr...  15.9 us
    all_to_all x1, waiting for transfers between devices, sum_by_exchange(): lax.all_to_all(parts, axes, 0, 0, tiled=True).astype(f32)  15.7 us
    all_to_all x1, waiting for transfers between devices, on_device(): lax.all_to_all(spread.reshape(2 * nf, tokens // nf, rank // 2), plane, 0,...  14.9 us
  transfers between devices with their start and end apart: 13, of which 8 were waited for; matrix products, arithmetic and copies ran while one was open for 2% of the time, Pallas kernels for 0%

profile of v6, /device:TPU:1, one launch (start us, length us, event | category | flops | bytes accessed | tf_op | source)
XLA Modules:
  0.0 217.4 jit_solution(13353669893600750971)
XLA Ops:
  0.6 12.0 %collective-permute-start = (bf16[16,2048]{1,0:T(8,128)(2,1)}, bf16[16,2048]{1,0:T(8,128)(2,1)S(1)}, u32[]{:S(2)}, u32[]{:S(2)}) collective-permute-start(bf16[16,2048]{1,0:T(8,128)(2,1)} %bitcast.103), channel_id=1, source_target_pairs={{0,240},{16,0},{32,16},{48,32},{64,48},{80,64},{96,80},{112,96},{1... | collective-permute-start | bytes 196616 | tf_op jit(solution)/shard_map/ppermute | solution.py:128
  12.6 1.9 collective-permute-start.4
  14.5 4.8 %collective-permute-start.9 = (bf16[512,2048]{1,0:T(8,128)(2,1)}, bf16[512,2048]{1,0:T(8,128)(2,1)S(1)}, u32[]{:S(2)}, u32[]{:S(2)}) collective-permute-start(bf16[512,2048]{1,0:T(8,128)(2,1)} %param.4), channel_id=1, source_target_pairs={{0,256},{256,0},{1,257},{257,1},{2,258},{258,2},{3,259},{259,3},{4... | collective-permute-start | bytes 6291464 | tf_op jit(solution)/shard_map/ppermute | solution.py:119
  21.1 3.8 %collective-permute-start.1 = (bf16[32,2048]{1,0:T(8,128)(2,1)S(1)}, bf16[32,2048]{1,0:T(8,128)(2,1)S(1)}, u32[]{:S(2)}, u32[]{:S(2)}) collective-permute-start(bf16[32,2048]{1,0:T(8,128)(2,1)S(1)} %get-tuple-element.35), channel_id=1, source_target_pairs={{0,224},{16,240},{32,0},{48,16},{64,32},{80,48},{96,64},{112,80},{... | collective-permute-start | bytes 393224 | tf_op jit(solution)/shard_map/ppermute | solution.py:128
  24.9 2.4 %collective-permute-start.5 = (bf16[32,2048]{1,0:T(8,128)(2,1)S(1)}, bf16[32,2048]{1,0:T(8,128)(2,1)S(1)}, u32[]{:S(2)}, u32[]{:S(2)}) collective-permute-start(bf16[32,2048]{1,0:T(8,128)(2,1)S(1)} %get-tuple-element.34), channel_id=1, source_target_pairs={{0,32},{16,48},{32,64},{48,80},{64,96},{80,112},{96,128},{112,144}... | collective-permute-start | bytes 393224 | tf_op jit(solution)/shard_map/ppermute | solution.py:128
  27.3 2.8 %collective-permute-done.1 = bf16[32,2048]{1,0:T(8,128)(2,1)S(1)} collective-permute-done((bf16[32,2048]{1,0:T(8,128)(2,1)S(1)}, bf16[32,2048]{1,0:T(8,128)(2,1)S(1)}, u32[]{:S(2)}, u32[]{:S(2)}) %collective-permute-start.1) | collective-permute-done | bytes 131104 | tf_op jit(solution)/shard_map/ppermute | solution.py:128
  30.1 4.0 %collective-permute-start.2 = (bf16[32,2048]{1,0:T(8,128)(2,1)S(1)}, bf16[32,2048]{1,0:T(8,128)(2,1)S(1)}, u32[]{:S(2)}, u32[]{:S(2)}) collective-permute-start(bf16[32,2048]{1,0:T(8,128)(2,1)S(1)} %collective-permute-done.1), channel_id=1, source_target_pairs={{0,224},{16,240},{32,0},{48,16},{64,32},{80,48},{96,64},{112,80},{... | collective-permute-start | bytes 393224 | tf_op jit(solution)/shard_map/ppermute | solution.py:128
  34.2 2.1 collective-permute-start.6
  37.0 9.9 %collective-permute-start.3 = (bf16[40,2048]{1,0:T(8,128)(2,1)S(1)}, bf16[40,2048]{1,0:T(8,128)(2,1)S(1)}, u32[]{:S(2)}, u32[]{:S(2)}) collective-permute-start(bf16[40,2048]{1,0:T(8,128)(2,1)S(1)} %pad_maximum_fusion.2), channel_id=1, source_target_pairs={{0,208},{16,224},{32,240},{48,0},{64,16},{80,32},{96,48},{112,64},... | collective-permute-start | bytes 491528 | tf_op jit(solution)/shard_map/ppermute | solution.py:128
  46.9 1.9 collective-permute-start.7
  48.9 3.5 %collective-permute-done.3 = bf16[40,2048]{1,0:T(8,128)(2,1)S(1)} collective-permute-done((bf16[40,2048]{1,0:T(8,128)(2,1)S(1)}, bf16[40,2048]{1,0:T(8,128)(2,1)S(1)}, u32[]{:S(2)}, u32[]{:S(2)}) %collective-permute-start.3) | collective-permute-done | bytes 163872 | tf_op jit(solution)/shard_map/ppermute | solution.py:128
  52.4 12.1 %collective-permute-done.7 = bf16[40,2048]{1,0:T(8,128)(2,1)S(1)} collective-permute-done((bf16[40,2048]{1,0:T(8,128)(2,1)S(1)}, bf16[40,2048]{1,0:T(8,128)(2,1)S(1)}, u32[]{:S(2)}, u32[]{:S(2)}) %collective-permute-start.7) | collective-permute-done | bytes 163872 | tf_op jit(solution)/shard_map/ppermute | solution.py:128
  64.7 2.4 %collective-permute-start.8 = (bf16[256,2048]{1,0:T(8,128)(2,1)S(1)}, bf16[256,2048]{1,0:T(8,128)(2,1)S(1)}, u32[]{:S(2)}, u32[]{:S(2)}) collective-permute-start(bf16[256,2048]{1,0:T(8,128)(2,1)S(1)} %get-tuple-element.28), channel_id=1, source_target_pairs={{0,8},{8,0},{1,9},{9,1},{2,10},{10,2},{3,11},{11,3},{4,12},{12,4},... | collective-permute-start | bytes 3145736 | tf_op jit(solution)/shard_map/ppermute | solution.py:119
  67.1 2.3 %collective-permute-done.8 = bf16[256,2048]{1,0:T(8,128)(2,1)S(1)} collective-permute-done((bf16[256,2048]{1,0:T(8,128)(2,1)S(1)}, bf16[256,2048]{1,0:T(8,128)(2,1)S(1)}, u32[]{:S(2)}, u32[]{:S(2)}) %collective-permute-start.8) | collective-permute-done | bytes 1048608 | tf_op jit(solution)/shard_map/ppermute | solution.py:119
  69.5 1.3 convolution_convert_fusion.1
  70.8 1.3 convolution_convert_fusion
  72.0 1.1 pad_maximum_fusion
  73.2 4.1 %all-to-all-start = ((bf16[8,128,512]{2,1,0:T(8,128)(2,1)}), bf16[8,128,512]{2,1,0:T(8,128)(2,1)S(1)}, u32[]{:S(2)}, u32[]{:S(2)}) async-start(bf16[8,128,512]{2,1,0:T(8,128)(2,1)} %bitcast.7), calls=%async_computation | async-start | bytes 2097152 | tf_op jit(solution)/shard_map/all_to_all | solution.py:169
  77.3 15.7 %all-to-all-done = bf16[8,128,512]{2,1,0:T(8,128)(2,1)S(1)} async-done(((bf16[8,128,512]{2,1,0:T(8,128)(2,1)}), bf16[8,128,512]{2,1,0:T(8,128)(2,1)S(1)}, u32[]{:S(2)}, u32[]{:S(2)}) %all-to-all-start) | async-done | bytes 1048608 | tf_op jit(solution)/shard_map/all_to_all | solution.py:169
  93.5 1.1 broadcast_in_dim.8
  94.6 3.7 %all-to-all-start.1 = ((bf16[16,64,512]{2,1,0:T(8,128)(2,1)}), bf16[16,64,512]{2,1,0:T(8,128)(2,1)S(1)}, u32[]{:S(2)}, u32[]{:S(2)}) async-start(bf16[16,64,512]{2,1,0:T(8,128)(2,1)} %bitcast.10), calls=%async_computation.1 | async-start | bytes 2097152 | tf_op jit(solution)/shard_map/all_to_all | solution.py:204
  98.2 14.9 %all-to-all-done.1 = bf16[16,64,512]{2,1,0:T(8,128)(2,1)S(1)} async-done(((bf16[16,64,512]{2,1,0:T(8,128)(2,1)}), bf16[16,64,512]{2,1,0:T(8,128)(2,1)S(1)}, u32[]{:S(2)}, u32[]{:S(2)}) %all-to-all-start.1) | async-done | bytes 1048608 | tf_op jit(solution)/shard_map/all_to_all | solution.py:204
  114.0 12.2 %all_to_all.30 = bf16[4,32,896]{2,1,0:T(8,128)(2,1)S(1)} all-to-all(bf16[4,32,896]{2,1,0:T(8,128)(2,1)S(1)} %bitcast.106), channel_id=1, replica_groups=mesh['yhi'=2,'z'=16,'core'=2,'x'=4,'ylo'=2] {'core','yhi'}, dimensions={0} | all-to-all | bytes 458752 | tf_op jit(solution)/shard_map/all_to_all | solution.py:169
  126.3 18.4 %all_to_all.31 = bf16[16,2,896]{2,1,0:T(2,128)(2,1)S(1)} all-to-all(bf16[16,2,896]{2,1,0:T(2,128)(2,1)S(1)} %reshape.49), channel_id=1, replica_groups=mesh['yhi'=2,'z'=16,'core'=2,'x'=4,'ylo'=2] {'z'}, dimensions={0} | all-to-all | bytes 114688 | tf_op jit(solution)/shard_map/all_to_all | solution.py:169
  144.8 14.2 %all_to_all.32 = bf16[16,2,896]{2,1,0:T(2,128)(2,1)S(1)} all-to-all(bf16[16,2,896]{2,1,0:T(2,128)(2,1)S(1)} %broadcast_in_dim.9), channel_id=1, replica_groups=mesh['yhi'=2,'z'=16,'core'=2,'x'=4,'ylo'=2] {'z'}, dimensions={0} | all-to-all | bytes 114688 | tf_op jit(solution)/shard_map/all_to_all | solution.py:163
  159.1 15.6 %all_to_all.33 = bf16[16,32,896]{2,1,0:T(8,128)(2,1)} all-to-all(bf16[16,32,896]{2,1,0:T(8,128)(2,1)S(1)} %broadcast_in_dim.22), channel_id=1, replica_groups=mesh['yhi'=2,'z'=16,'core'=2,'x'=4,'ylo'=2] {'x','ylo','yhi'}, dimensions={0} | all-to-all | bytes 1835008 | tf_op jit(solution)/shard_map/all_to_all | solution.py:163
  174.7 6.4 %collective-permute-start.10 = (bf16[8,64,896]{2,1,0:T(8,128)(2,1)}, bf16[8,64,896]{2,1,0:T(8,128)(2,1)}, u32[]{:S(2)}, u32[]{:S(2)}) collective-permute-start(bf16[8,64,896]{2,1,0:T(8,128)(2,1)} %bitcast.15), channel_id=1, source_target_pairs={{0,8},{8,0},{1,9},{9,1},{2,10},{10,2},{3,11},{11,3},{4,12},{12,4},... | collective-permute-start | bytes 2752520 | tf_op jit(solution)/shard_map/ppermute | solution.py:119
  181.2 1.8 copy.30
  183.4 1.6 broadcast_select_fusion.1
  189.8 8.8 %shard_map.60 = f32[256,256]{1,0:T(8,128)S(1)} custom-call(f32[256,256]{1,0:T(8,128)S(1)} %fusion.17.matrix_ref), custom_call_target="tpu_custom_call" | custom-call | tf_op jit(solution)/shard_map/pallas_call | solution.py:82
  205.0 9.1 %shard_map.61 = f32[256,256]{1,0:T(8,128)S(1)} custom-call(f32[256,256]{1,0:T(8,128)S(1)} %fusion.13.matrix_ref), custom_call_target="tpu_custom_call" | custom-call | tf_op jit(solution)/shard_map/pallas_call | solution.py:82
  215.4 1.2 convolution_subtract_fusion.2
  (75 shorter events, 17.6 us)
Async XLA Ops:
  0.6 19.6 %collective-permute-start = (bf16[16,2048]{1,0:T(8,128)(2,1)}, bf16[16,2048]{1,0:T(8,128)(2,1)S(1)}, u32[]{:S(2)}, u32[]{:S(2)}) collective-permute-start(bf16[16,2048]{1,0:T(8,128)(2,1)} %bitcast.103), channel_id=1, source_target_pairs={{0,240},{16,0},{32,16},{48,32},{64,48},{80,64},{96,80},{112,96},{1... | collective-permute-start | bytes 196616 | tf_op jit(solution)/shard_map/ppermute | solution.py:128
  12.6 7.6 %collective-permute-start.4 = (bf16[16,2048]{1,0:T(8,128)(2,1)}, bf16[16,2048]{1,0:T(8,128)(2,1)S(1)}, u32[]{:S(2)}, u32[]{:S(2)}) collective-permute-start(bf16[16,2048]{1,0:T(8,128)(2,1)} %bitcast.104), channel_id=1, source_target_pairs={{0,16},{16,32},{32,48},{48,64},{64,80},{80,96},{96,112},{112,128},... | collective-permute-start | bytes 196616 | tf_op jit(solution)/shard_map/ppermute | solution.py:128
  14.5 56.2 %collective-permute-start.9 = (bf16[512,2048]{1,0:T(8,128)(2,1)}, bf16[512,2048]{1,0:T(8,128)(2,1)S(1)}, u32[]{:S(2)}, u32[]{:S(2)}) collective-permute-start(bf16[512,2048]{1,0:T(8,128)(2,1)} %param.4), channel_id=1, source_target_pairs={{0,256},{256,0},{1,257},{257,1},{2,258},{258,2},{3,259},{259,3},{4... | collective-permute-start | bytes 6291464 | tf_op jit(solution)/shard_map/ppermute | solution.py:119
  21.1 9.0 %collective-permute-start.1 = (bf16[32,2048]{1,0:T(8,128)(2,1)S(1)}, bf16[32,2048]{1,0:T(8,128)(2,1)S(1)}, u32[]{:S(2)}, u32[]{:S(2)}) collective-permute-start(bf16[32,2048]{1,0:T(8,128)(2,1)S(1)} %get-tuple-element.35), channel_id=1, source_target_pairs={{0,224},{16,240},{32,0},{48,16},{64,32},{80,48},{96,64},{112,80},{... | collective-permute-start | bytes 393224 | tf_op jit(solution)/shard_map/ppermute | solution.py:128
  24.9 9.2 %collective-permute-start.5 = (bf16[32,2048]{1,0:T(8,128)(2,1)S(1)}, bf16[32,2048]{1,0:T(8,128)(2,1)S(1)}, u32[]{:S(2)}, u32[]{:S(2)}) collective-permute-start(bf16[32,2048]{1,0:T(8,128)(2,1)S(1)} %get-tuple-element.34), channel_id=1, source_target_pairs={{0,32},{16,48},{32,64},{48,80},{64,96},{80,112},{96,128},{112,144}... | collective-permute-start | bytes 393224 | tf_op jit(solution)/shard_map/ppermute | solution.py:128
  30.1 6.9 %collective-permute-start.2 = (bf16[32,2048]{1,0:T(8,128)(2,1)S(1)}, bf16[32,2048]{1,0:T(8,128)(2,1)S(1)}, u32[]{:S(2)}, u32[]{:S(2)}) collective-permute-start(bf16[32,2048]{1,0:T(8,128)(2,1)S(1)} %collective-permute-done.1), channel_id=1, source_target_pairs={{0,224},{16,240},{32,0},{48,16},{64,32},{80,48},{96,64},{112,80},{... | collective-permute-start | bytes 393224 | tf_op jit(solution)/shard_map/ppermute | solution.py:128
  34.2 12.7 %collective-permute-start.6 = (bf16[32,2048]{1,0:T(8,128)(2,1)S(1)}, bf16[32,2048]{1,0:T(8,128)(2,1)S(1)}, u32[]{:S(2)}, u32[]{:S(2)}) collective-permute-start(bf16[32,2048]{1,0:T(8,128)(2,1)S(1)} %collective-permute-done.5), channel_id=1, source_target_pairs={{0,32},{16,48},{32,64},{48,80},{64,96},{80,112},{96,128},{112,144}... | collective-permute-start | bytes 393224 | tf_op jit(solution)/shard_map/ppermute | solution.py:128
  37.0 15.4 %collective-permute-start.3 = (bf16[40,2048]{1,0:T(8,128)(2,1)S(1)}, bf16[40,2048]{1,0:T(8,128)(2,1)S(1)}, u32[]{:S(2)}, u32[]{:S(2)}) collective-permute-start(bf16[40,2048]{1,0:T(8,128)(2,1)S(1)} %pad_maximum_fusion.2), channel_id=1, source_target_pairs={{0,208},{16,224},{32,240},{48,0},{64,16},{80,32},{96,48},{112,64},... | collective-permute-start | bytes 491528 | tf_op jit(solution)/shard_map/ppermute | solution.py:128
  46.9 17.6 %collective-permute-start.7 = (bf16[40,2048]{1,0:T(8,128)(2,1)S(1)}, bf16[40,2048]{1,0:T(8,128)(2,1)S(1)}, u32[]{:S(2)}, u32[]{:S(2)}) collective-permute-start(bf16[40,2048]{1,0:T(8,128)(2,1)S(1)} %pad_maximum_fusion.3), channel_id=1, source_target_pairs={{0,48},{16,64},{32,80},{48,96},{64,112},{80,128},{96,144},{112,160... | collective-permute-start | bytes 491528 | tf_op jit(solution)/shard_map/ppermute | solution.py:128
  52.4 17.0 %copy-start.1 = (bf16[512,2048]{1,0:T(8,128)(2,1)S(1)}, bf16[512,2048]{1,0:T(8,128)(2,1)}, u32[]{:S(2)}) copy-start(bf16[512,2048]{1,0:T(8,128)(2,1)} %param.4) | copy-start | bytes 6291460
  64.7 4.7 %collective-permute-start.8 = (bf16[256,2048]{1,0:T(8,128)(2,1)S(1)}, bf16[256,2048]{1,0:T(8,128)(2,1)S(1)}, u32[]{:S(2)}, u32[]{:S(2)}) collective-permute-start(bf16[256,2048]{1,0:T(8,128)(2,1)S(1)} %get-tuple-element.28), channel_id=1, source_target_pairs={{0,8},{8,0},{1,9},{9,1},{2,10},{10,2},{3,11},{11,3},{4,12},{12,4},... | collective-permute-start | bytes 3145736 | tf_op jit(solution)/shard_map/ppermute | solution.py:119
  73.2 19.8 %all-to-all-start = ((bf16[8,128,512]{2,1,0:T(8,128)(2,1)}), bf16[8,128,512]{2,1,0:T(8,128)(2,1)S(1)}, u32[]{:S(2)}, u32[]{:S(2)}) async-start(bf16[8,128,512]{2,1,0:T(8,128)(2,1)} %bitcast.7), calls=%async_computation | async-start | bytes 2097152 | tf_op jit(solution)/shard_map/all_to_all | solution.py:169
  94.6 18.6 %all-to-all-start.1 = ((bf16[16,64,512]{2,1,0:T(8,128)(2,1)}), bf16[16,64,512]{2,1,0:T(8,128)(2,1)S(1)}, u32[]{:S(2)}, u32[]{:S(2)}) async-start(bf16[16,64,512]{2,1,0:T(8,128)(2,1)} %bitcast.10), calls=%async_computation.1 | async-start | bytes 2097152 | tf_op jit(solution)/shard_map/all_to_all | solution.py:204
  98.2 15.4 %copy-start = (bf16[512,256]{1,0:T(8,128)(2,1)S(1)}, bf16[512,256]{1,0:T(8,128)(2,1)}, u32[]{:S(2)}) copy-start(bf16[512,256]{1,0:T(8,128)(2,1)} %param.7) | copy-start | bytes 786436
  174.7 8.7 %collective-permute-start.10 = (bf16[8,64,896]{2,1,0:T(8,128)(2,1)}, bf16[8,64,896]{2,1,0:T(8,128)(2,1)}, u32[]{:S(2)}, u32[]{:S(2)}) collective-permute-start(bf16[8,64,896]{2,1,0:T(8,128)(2,1)} %bitcast.15), channel_id=1, source_target_pairs={{0,8},{8,0},{1,9},{9,1},{2,10},{10,2},{3,11},{11,3},{4,12},{12,4},... | collective-permute-start | bytes 2752520 | tf_op jit(solution)/shard_map/ppermute | solution.py:119

commit v7 on v3

--- a/solution.py
+++ b/solution.py
@@ -88,6 +88,50 @@
     )(matrix)
 
 
+def join_blocks_kernel(core_ref, mine_ref, other_ref, gram_ref, back_ref):
+    count, half, _ = mine_ref.shape
+    size = 2 * half
+    width = (count // 2 + 1) * size
+
+    def join(low_ref, high_ref):
+        for i in range(count):
+            top = i * size
+            back_ref[top : top + half, :] = low_ref[i, :, width:]
+            back_ref[top + half : top + size, :] = high_ref[i, :, width:]
+            for k in range(count // 2 + 1):
+                left = (i + k) % count * size
+                low = low_ref[i, :, k * size : (k + 1) * size]
+                high = high_ref[i, :, k * size : (k + 1) * size]
+                gram_ref[top : top + half, left : left + size] = low
+                gram_ref[top + half : top + size, left : left + size] = high
+                if 0 < k < count // 2:
+                    block = jnp.concatenate([low.astype(f32), high.astype(f32)])
+                    gram_ref[left : left + size, top : top + size] = block.T.astype(bf16)
+
+    @pl.when(core_ref[0] == 0)
+    def _():
+        join(mine_ref, other_ref)
+
+    @pl.when(core_ref[0] != 0)
+    def _():
+        join(other_ref, mine_ref)
+
+
+def join_blocks(core, mine, other, columns):
+    rank = 2 * mine.shape[0] * mine.shape[1]
+    vmem = pl.BlockSpec(memory_space=pltpu.VMEM)
+    return pl.pallas_call(
+        join_blocks_kernel,
+        out_shape=[
+            jax.ShapeDtypeStruct((rank, rank), bf16),
+            jax.ShapeDtypeStruct((rank, columns), bf16),
+        ],
+        in_specs=[pl.BlockSpec(memory_space=pltpu.SMEM), vmem, vmem],
+        out_specs=[vmem, vmem],
+        compiler_params=pltpu.CompilerParams(vmem_limit_bytes=16 * 1024 * 1024),
+    )(core.reshape(1), mine, other)
+
+
 def swap(value, axis):
     return lax.ppermute(value, axis, [(0, 1), (1, 0)])
 
@@ -181,16 +225,15 @@
 
     rows = precond.reshape(2, nz, 2, narrow, rank).transpose(0, 2, 1, 3, 4).reshape(rank, rank)
 
-    joined_slice = lax.dynamic_slice_in_dim(joined, feat * share, share, 1)
-    total = dot(joined_slice, jnp.concatenate([joined, target], axis=1), 0, 0)
+    count = (nf // 2 + 1) * share
+    wrapped = jnp.concatenate([joined, joined[:, : count - share]], axis=1)
+    window = lax.dynamic_slice_in_dim(wrapped, feat * share, count, 1)
+    total = dot(window[:, :share], jnp.concatenate([window, target], axis=1), 0, 0)
     width = total.shape[1]
     summed = sum_by_exchange(sum_by_exchange(total, ("core", "yhi")), "z").astype(bf16)
     summed = gather_by_exchange(summed, "z").reshape(share // 4, width)
     summed = gather_by_exchange(summed, plane).reshape(nf, share // 2, width)
-    low, high = ordered(core == 0, summed, swap(summed, "core"))
-    summed = jnp.stack([low, high], axis=1).reshape(rank, width)
-    gram = summed[:, :rank]
-    back = summed[:, rank:]
+    gram, back = join_blocks(core, summed, swap(summed, "core"), target.shape[1])
 
     descent = dot(rows, back, 0, 0)
     gram_now = dot(descent, descent, 0, 0, three)
@@ -201,9 +244,7 @@
     inverse = invert(curvature)
     step = dot(inverse, gram_now, 1, 0, three)
 
-    coarse = image_back.astype(bf16)
-    fine = (image_back - coarse.astype(f32)).astype(bf16)
-    curved = dot(rows, coarse, 0, 0) + dot(rows, fine, 0, 0)
+    curved = dot(rows, image_back.astype(bf16), 0, 0)
     descent_next = descent - dot(curved, step, 1, 0, three)
     gram_next = dot(descent_next, descent_next, 0, 0, three)
     mixing = dot(inverse, dot(curved, descent_next, 0, 0, three), 1, 0, three)

time: 226 us -> 218 us (0.965)
  blocking collectives: 68.4 us -> 59.8 us
    all_to_all x2, blocking collectives: 36.3 us -> 29.1 us  [gather_by_exchange(): return lax.all_to_all(spread, axes, 0, 0, tiled=True)]
    dot_general x23 -> x22, matrix products: 16.6 us -> 17.5 us  [dot(): lax.dot_general(a, b, (((ca,), (cb,)), ((), ())), precision=precision, pr...]
  transfers between devices with their start and end apart: 13 -> 13, of which waited for: 8 -> 7; matrix products, arithmetic and copies ran while one was open for 2% -> 3% of each run, Pallas kernels for 0% -> 0%
where the time goes in v7:
time: 218 us; the launch traced here: 217 us
  blocking collectives  59.8 us (27%)
  starting transfers between devices  59.3 us (27%)
  waiting for transfers between devices  51.9 us (24%)
  Pallas kernels  18.3 us (8%)
  matrix products  17.5 us (8%)
  local copies, waits for them, and re-layouts  6.5 us (3%)
  other arithmetic  2.88 us (1%)
    ppermute x8, starting transfers between devices, shift(): return lax.ppermute(value, axis, [(i, (i + by) % n) for i in range(n)])  38 us
    all_to_all x2, blocking collectives, sum_by_exchange(): lax.all_to_all(parts, axes, 0, 0, tiled=True).astype(f32)  30.7 us
    all_to_all x2, blocking collectives, gather_by_exchange(): return lax.all_to_all(spread, axes, 0, 0, tiled=True)  29.1 us
    ppermute x8, waiting for transfers between devices, shift(): return lax.ppermute(value, axis, [(i, (i + by) % n) for i in range(n)])  19 us
    pallas_call x2, Pallas kernels, invert(): pl.pallas_call(invert_kernel, out_shape=jax.ShapeDtypeStruct(matrix.shape...  17.6 us
    dot_general x22, matrix products, dot(): lax.dot_general(a, b, (((ca,), (cb,)), ((), ())), precision=precision, pr...  17.5 us
    all_to_all x1, waiting for transfers between devices, sum_by_exchange(): lax.all_to_all(parts, axes, 0, 0, tiled=True).astype(f32)  15.7 us
    all_to_all x1, waiting for transfers between devices, on_device(): lax.all_to_all(spread.reshape(2 * nf, tokens // nf, rank // 2), plane, 0,...  14.9 us
  transfers between devices with their start and end apart: 13, of which 7 were waited for; matrix products, arithmetic and copies ran while one was open for 3% of the time, Pallas kernels for 0%

profile of v7, /device:TPU:1, one launch (start us, length us, event | category | flops | bytes accessed | tf_op | source)
XLA Modules:
  0.0 217.4 jit_solution(10460592434890922641)
XLA Ops:
  0.6 12.0 %collective-permute-start = (bf16[16,2048]{1,0:T(8,128)(2,1)}, bf16[16,2048]{1,0:T(8,128)(2,1)S(1)}, u32[]{:S(2)}, u32[]{:S(2)}) collective-permute-start(bf16[16,2048]{1,0:T(8,128)(2,1)} %bitcast.97), channel_id=1, source_target_pairs={{0,240},{16,0},{32,16},{48,32},{64,48},{80,64},{96,80},{112,96},{1... | collective-permute-start | bytes 196616 | tf_op jit(solution)/shard_map/ppermute | solution.py:145
  12.6 1.9 collective-permute-start.4
  14.5 4.8 %collective-permute-start.9 = (bf16[512,2048]{1,0:T(8,128)(2,1)}, bf16[512,2048]{1,0:T(8,128)(2,1)S(1)}, u32[]{:S(2)}, u32[]{:S(2)}) collective-permute-start(bf16[512,2048]{1,0:T(8,128)(2,1)} %param.4), channel_id=1, source_target_pairs={{0,256},{256,0},{1,257},{257,1},{2,258},{258,2},{3,259},{259,3},{4... | collective-permute-start | bytes 6291464 | tf_op jit(solution)/shard_map/ppermute | solution.py:136
  21.1 3.8 %collective-permute-start.1 = (bf16[32,2048]{1,0:T(8,128)(2,1)S(1)}, bf16[32,2048]{1,0:T(8,128)(2,1)S(1)}, u32[]{:S(2)}, u32[]{:S(2)}) collective-permute-start(bf16[32,2048]{1,0:T(8,128)(2,1)S(1)} %get-tuple-element.37), channel_id=1, source_target_pairs={{0,224},{16,240},{32,0},{48,16},{64,32},{80,48},{96,64},{112,80},{... | collective-permute-start | bytes 393224 | tf_op jit(solution)/shard_map/ppermute | solution.py:145
  24.9 2.4 %collective-permute-start.5 = (bf16[32,2048]{1,0:T(8,128)(2,1)S(1)}, bf16[32,2048]{1,0:T(8,128)(2,1)S(1)}, u32[]{:S(2)}, u32[]{:S(2)}) collective-permute-start(bf16[32,2048]{1,0:T(8,128)(2,1)S(1)} %get-tuple-element.36), channel_id=1, source_target_pairs={{0,32},{16,48},{32,64},{48,80},{64,96},{80,112},{96,128},{112,144}... | collective-permute-start | bytes 393224 | tf_op jit(solution)/shard_map/ppermute | solution.py:145
  27.3 2.8 %collective-permute-done.1 = bf16[32,2048]{1,0:T(8,128)(2,1)S(1)} collective-permute-done((bf16[32,2048]{1,0:T(8,128)(2,1)S(1)}, bf16[32,2048]{1,0:T(8,128)(2,1)S(1)}, u32[]{:S(2)}, u32[]{:S(2)}) %collective-permute-start.1) | collective-permute-done | bytes 131104 | tf_op jit(solution)/shard_map/ppermute | solution.py:145
  30.1 4.0 %collective-permute-start.2 = (bf16[32,2048]{1,0:T(8,128)(2,1)S(1)}, bf16[32,2048]{1,0:T(8,128)(2,1)S(1)}, u32[]{:S(2)}, u32[]{:S(2)}) collective-permute-start(bf16[32,2048]{1,0:T(8,128)(2,1)S(1)} %collective-permute-done.1), channel_id=1, source_target_pairs={{0,224},{16,240},{32,0},{48,16},{64,32},{80,48},{96,64},{112,80},{... | collective-permute-start | bytes 393224 | tf_op jit(solution)/shard_map/ppermute | solution.py:145
  34.2 2.1 collective-permute-start.6
  37.0 9.9 %collective-permute-start.3 = (bf16[40,2048]{1,0:T(8,128)(2,1)S(1)}, bf16[40,2048]{1,0:T(8,128)(2,1)S(1)}, u32[]{:S(2)}, u32[]{:S(2)}) collective-permute-start(bf16[40,2048]{1,0:T(8,128)(2,1)S(1)} %pad_maximum_fusion.1), channel_id=1, source_target_pairs={{0,208},{16,224},{32,240},{48,0},{64,16},{80,32},{96,48},{112,64},... | collective-permute-start | bytes 491528 | tf_op jit(solution)/shard_map/ppermute | solution.py:145
  46.9 1.9 collective-permute-start.7
  48.9 3.5 %collective-permute-done.3 = bf16[40,2048]{1,0:T(8,128)(2,1)S(1)} collective-permute-done((bf16[40,2048]{1,0:T(8,128)(2,1)S(1)}, bf16[40,2048]{1,0:T(8,128)(2,1)S(1)}, u32[]{:S(2)}, u32[]{:S(2)}) %collective-permute-start.3) | collective-permute-done | bytes 163872 | tf_op jit(solution)/shard_map/ppermute | solution.py:145
  52.4 12.1 %collective-permute-done.7 = bf16[40,2048]{1,0:T(8,128)(2,1)S(1)} collective-permute-done((bf16[40,2048]{1,0:T(8,128)(2,1)S(1)}, bf16[40,2048]{1,0:T(8,128)(2,1)S(1)}, u32[]{:S(2)}, u32[]{:S(2)}) %collective-permute-start.7) | collective-permute-done | bytes 163872 | tf_op jit(solution)/shard_map/ppermute | solution.py:145
  64.7 2.4 %collective-permute-start.8 = (bf16[256,2048]{1,0:T(8,128)(2,1)S(1)}, bf16[256,2048]{1,0:T(8,128)(2,1)S(1)}, u32[]{:S(2)}, u32[]{:S(2)}) collective-permute-start(bf16[256,2048]{1,0:T(8,128)(2,1)S(1)} %get-tuple-element.30), channel_id=1, source_target_pairs={{0,8},{8,0},{1,9},{9,1},{2,10},{10,2},{3,11},{11,3},{4,12},{12,4},... | collective-permute-start | bytes 3145736 | tf_op jit(solution)/shard_map/ppermute | solution.py:136
  67.1 2.3 %collective-permute-done.8 = bf16[256,2048]{1,0:T(8,128)(2,1)S(1)} collective-permute-done((bf16[256,2048]{1,0:T(8,128)(2,1)S(1)}, bf16[256,2048]{1,0:T(8,128)(2,1)S(1)}, u32[]{:S(2)}, u32[]{:S(2)}) %collective-permute-start.8) | collective-permute-done | bytes 1048608 | tf_op jit(solution)/shard_map/ppermute | solution.py:136
  69.5 1.3 convolution_convert_fusion.1
  70.8 1.3 convolution_convert_fusion
  73.1 4.1 %all-to-all-start = ((bf16[8,128,512]{2,1,0:T(8,128)(2,1)}), bf16[8,128,512]{2,1,0:T(8,128)(2,1)S(1)}, u32[]{:S(2)}, u32[]{:S(2)}) async-start(bf16[8,128,512]{2,1,0:T(8,128)(2,1)} %bitcast.8), calls=%async_computation | async-start | bytes 2097152 | tf_op jit(solution)/shard_map/all_to_all | solution.py:186
  77.3 15.7 %all-to-all-done = bf16[8,128,512]{2,1,0:T(8,128)(2,1)S(1)} async-done(((bf16[8,128,512]{2,1,0:T(8,128)(2,1)}), bf16[8,128,512]{2,1,0:T(8,128)(2,1)S(1)}, u32[]{:S(2)}, u32[]{:S(2)}) %all-to-all-start) | async-done | bytes 1048608 | tf_op jit(solution)/shard_map/all_to_all | solution.py:186
  93.4 1.1 broadcast_in_dim.8
  94.6 3.7 %all-to-all-start.1 = ((bf16[16,64,512]{2,1,0:T(8,128)(2,1)}), bf16[16,64,512]{2,1,0:T(8,128)(2,1)S(1)}, u32[]{:S(2)}, u32[]{:S(2)}) async-start(bf16[16,64,512]{2,1,0:T(8,128)(2,1)} %bitcast.11), calls=%async_computation.1 | async-start | bytes 2097152 | tf_op jit(solution)/shard_map/all_to_all | solution.py:221
  98.2 14.9 %all-to-all-done.1 = bf16[16,64,512]{2,1,0:T(8,128)(2,1)S(1)} async-done(((bf16[16,64,512]{2,1,0:T(8,128)(2,1)}), bf16[16,64,512]{2,1,0:T(8,128)(2,1)S(1)}, u32[]{:S(2)}, u32[]{:S(2)}) %all-to-all-start.1) | async-done | bytes 1048608 | tf_op jit(solution)/shard_map/all_to_all | solution.py:221
  114.0 12.2 %all_to_all.30 = bf16[4,32,896]{2,1,0:T(8,128)(2,1)S(1)} all-to-all(bf16[4,32,896]{2,1,0:T(8,128)(2,1)S(1)} %bitcast.100), channel_id=1, replica_groups=mesh['yhi'=2,'z'=16,'core'=2,'x'=4,'ylo'=2] {'core','yhi'}, dimensions={0} | all-to-all | bytes 458752 | tf_op jit(solution)/shard_map/all_to_all | solution.py:186
  126.3 18.4 %all_to_all.31 = bf16[16,2,896]{2,1,0:T(2,128)(2,1)S(1)} all-to-all(bf16[16,2,896]{2,1,0:T(2,128)(2,1)S(1)} %reshape.50), channel_id=1, replica_groups=mesh['yhi'=2,'z'=16,'core'=2,'x'=4,'ylo'=2] {'z'}, dimensions={0} | all-to-all | bytes 114688 | tf_op jit(solution)/shard_map/all_to_all | solution.py:186
  144.8 14.2 %all_to_all.32 = bf16[16,2,896]{2,1,0:T(2,128)(2,1)S(1)} all-to-all(bf16[16,2,896]{2,1,0:T(2,128)(2,1)S(1)} %broadcast_in_dim.9), channel_id=1, replica_groups=mesh['yhi'=2,'z'=16,'core'=2,'x'=4,'ylo'=2] {'z'}, dimensions={0} | all-to-all | bytes 114688 | tf_op jit(solution)/shard_map/all_to_all | solution.py:180
  159.1 14.9 %all_to_all.33 = bf16[16,32,896]{2,1,0:T(8,128)(2,1)S(1)} all-to-all(bf16[16,32,896]{2,1,0:T(8,128)(2,1)S(1)} %broadcast_in_dim.22), channel_id=1, replica_groups=mesh['yhi'=2,'z'=16,'core'=2,'x'=4,'ylo'=2] {'x','ylo','yhi'}, dimensions={0} | all-to-all | bytes 1835008 | tf_op jit(solution)/shard_map/all_to_all | solution.py:180
  174.0 6.2 %collective-permute-start.10 = (bf16[8,64,896]{2,1,0:T(8,128)(2,1)S(1)}, bf16[8,64,896]{2,1,0:T(8,128)(2,1)S(1)}, u32[]{:S(2)}, u32[]{:S(2)}) collective-permute-start(bf16[8,64,896]{2,1,0:T(8,128)(2,1)S(1)} %bitcast.81), channel_id=1, source_target_pairs={{0,8},{8,0},{1,9},{9,1},{2,10},{10,2},{3,11},{11,3},{4,12},{12,4},... | collective-permute-start | bytes 2752520 | tf_op jit(solution)/shard_map/ppermute | solution.py:136
  180.3 3.2 %copy.26 = bf16[2,2,16,16,1024]{4,3,2,1,0:T(8,128)(2,1)} copy(bf16[2,2,16,16,1024]{4,3,1,2,0:T(8,128)(2,1)} %bitcast.93) | data formatting | bytes 4194304 | tf_op jit(solution)/shard_map/transpose | solution.py:226
  184.2 2.5 %fusion.33 = f32[256,1024]{1,0:T(8,128)S(1)} fusion(bf16[1024,256]{1,0:T(8,128)(2,1)S(1)} %get-tuple-element.4, bf16[1024,1024]{1,0:T(8,128)(2,1)} %bitcast.83), kind=kOutput, calls=%fused_computation.89 | convolution fusion | flops 536870912 | bytes 3670016 | tf_op jit(solution)/shard_map/dot_general | solution.py:18
  190.0 8.8 %shard_map.60 = f32[256,256]{1,0:T(8,128)S(1)} custom-call(f32[256,256]{1,0:T(8,128)S(1)} %fusion.17.matrix_ref), custom_call_target="tpu_custom_call" | custom-call | tf_op jit(solution)/shard_map/pallas_call | solution.py:82
  199.1 1.2 fusion.36
  205.2 8.8 %shard_map.61 = f32[256,256]{1,0:T(8,128)S(1)} custom-call(f32[256,256]{1,0:T(8,128)S(1)} %fusion.13.matrix_ref), custom_call_target="tpu_custom_call" | custom-call | tf_op jit(solution)/shard_map/pallas_call | solution.py:82
  215.4 1.2 convolution_subtract_fusion.2
  (72 shorter events, 16.3 us)
Async XLA Ops:
  0.6 19.6 %collective-permute-start = (bf16[16,2048]{1,0:T(8,128)(2,1)}, bf16[16,2048]{1,0:T(8,128)(2,1)S(1)}, u32[]{:S(2)}, u32[]{:S(2)}) collective-permute-start(bf16[16,2048]{1,0:T(8,128)(2,1)} %bitcast.97), channel_id=1, source_target_pairs={{0,240},{16,0},{32,16},{48,32},{64,48},{80,64},{96,80},{112,96},{1... | collective-permute-start | bytes 196616 | tf_op jit(solution)/shard_map/ppermute | solution.py:145
  12.6 7.6 %collective-permute-start.4 = (bf16[16,2048]{1,0:T(8,128)(2,1)}, bf16[16,2048]{1,0:T(8,128)(2,1)S(1)}, u32[]{:S(2)}, u32[]{:S(2)}) collective-permute-start(bf16[16,2048]{1,0:T(8,128)(2,1)} %bitcast.98), channel_id=1, source_target_pairs={{0,16},{16,32},{32,48},{48,64},{64,80},{80,96},{96,112},{112,128},... | collective-permute-start | bytes 196616 | tf_op jit(solution)/shard_map/ppermute | solution.py:145
  14.5 56.2 %collective-permute-start.9 = (bf16[512,2048]{1,0:T(8,128)(2,1)}, bf16[512,2048]{1,0:T(8,128)(2,1)S(1)}, u32[]{:S(2)}, u32[]{:S(2)}) collective-permute-start(bf16[512,2048]{1,0:T(8,128)(2,1)} %param.4), channel_id=1, source_target_pairs={{0,256},{256,0},{1,257},{257,1},{2,258},{258,2},{3,259},{259,3},{4... | collective-permute-start | bytes 6291464 | tf_op jit(solution)/shard_map/ppermute | solution.py:136
  21.1 9.0 %collective-permute-start.1 = (bf16[32,2048]{1,0:T(8,128)(2,1)S(1)}, bf16[32,2048]{1,0:T(8,128)(2,1)S(1)}, u32[]{:S(2)}, u32[]{:S(2)}) collective-permute-start(bf16[32,2048]{1,0:T(8,128)(2,1)S(1)} %get-tuple-element.37), channel_id=1, source_target_pairs={{0,224},{16,240},{32,0},{48,16},{64,32},{80,48},{96,64},{112,80},{... | collective-permute-start | bytes 393224 | tf_op jit(solution)/shard_map/ppermute | solution.py:145
  24.9 9.2 %collective-permute-start.5 = (bf16[32,2048]{1,0:T(8,128)(2,1)S(1)}, bf16[32,2048]{1,0:T(8,128)(2,1)S(1)}, u32[]{:S(2)}, u32[]{:S(2)}) collective-permute-start(bf16[32,2048]{1,0:T(8,128)(2,1)S(1)} %get-tuple-element.36), channel_id=1, source_target_pairs={{0,32},{16,48},{32,64},{48,80},{64,96},{80,112},{96,128},{112,144}... | collective-permute-start | bytes 393224 | tf_op jit(solution)/shard_map/ppermute | solution.py:145
  30.1 6.9 %collective-permute-start.2 = (bf16[32,2048]{1,0:T(8,128)(2,1)S(1)}, bf16[32,2048]{1,0:T(8,128)(2,1)S(1)}, u32[]{:S(2)}, u32[]{:S(2)}) collective-permute-start(bf16[32,2048]{1,0:T(8,128)(2,1)S(1)} %collective-permute-done.1), channel_id=1, source_target_pairs={{0,224},{16,240},{32,0},{48,16},{64,32},{80,48},{96,64},{112,80},{... | collective-permute-start | bytes 393224 | tf_op jit(solution)/shard_map/ppermute | solution.py:145
  34.2 12.7 %collective-permute-start.6 = (bf16[32,2048]{1,0:T(8,128)(2,1)S(1)}, bf16[32,2048]{1,0:T(8,128)(2,1)S(1)}, u32[]{:S(2)}, u32[]{:S(2)}) collective-permute-start(bf16[32,2048]{1,0:T(8,128)(2,1)S(1)} %collective-permute-done.5), channel_id=1, source_target_pairs={{0,32},{16,48},{32,64},{48,80},{64,96},{80,112},{96,128},{112,144}... | collective-permute-start | bytes 393224 | tf_op jit(solution)/shard_map/ppermute | solution.py:145
  37.0 15.4 %collective-permute-start.3 = (bf16[40,2048]{1,0:T(8,128)(2,1)S(1)}, bf16[40,2048]{1,0:T(8,128)(2,1)S(1)}, u32[]{:S(2)}, u32[]{:S(2)}) collective-permute-start(bf16[40,2048]{1,0:T(8,128)(2,1)S(1)} %pad_maximum_fusion.1), channel_id=1, source_target_pairs={{0,208},{16,224},{32,240},{48,0},{64,16},{80,32},{96,48},{112,64},... | collective-permute-start | bytes 491528 | tf_op jit(solution)/shard_map/ppermute | solution.py:145
  46.9 17.6 %collective-permute-start.7 = (bf16[40,2048]{1,0:T(8,128)(2,1)S(1)}, bf16[40,2048]{1,0:T(8,128)(2,1)S(1)}, u32[]{:S(2)}, u32[]{:S(2)}) collective-permute-start(bf16[40,2048]{1,0:T(8,128)(2,1)S(1)} %pad_maximum_fusion.2), channel_id=1, source_target_pairs={{0,48},{16,64},{32,80},{48,96},{64,112},{80,128},{96,144},{112,160... | collective-permute-start | bytes 491528 | tf_op jit(solution)/shard_map/ppermute | solution.py:145
  52.4 17.0 %copy-start.2 = (bf16[512,2048]{1,0:T(8,128)(2,1)S(1)}, bf16[512,2048]{1,0:T(8,128)(2,1)}, u32[]{:S(2)}) copy-start(bf16[512,2048]{1,0:T(8,128)(2,1)} %param.4) | copy-start | bytes 6291460
  64.7 4.7 %collective-permute-start.8 = (bf16[256,2048]{1,0:T(8,128)(2,1)S(1)}, bf16[256,2048]{1,0:T(8,128)(2,1)S(1)}, u32[]{:S(2)}, u32[]{:S(2)}) collective-permute-start(bf16[256,2048]{1,0:T(8,128)(2,1)S(1)} %get-tuple-element.30), channel_id=1, source_target_pairs={{0,8},{8,0},{1,9},{9,1},{2,10},{10,2},{3,11},{11,3},{4,12},{12,4},... | collective-permute-start | bytes 3145736 | tf_op jit(solution)/shard_map/ppermute | solution.py:136
  73.1 19.8 %all-to-all-start = ((bf16[8,128,512]{2,1,0:T(8,128)(2,1)}), bf16[8,128,512]{2,1,0:T(8,128)(2,1)S(1)}, u32[]{:S(2)}, u32[]{:S(2)}) async-start(bf16[8,128,512]{2,1,0:T(8,128)(2,1)} %bitcast.8), calls=%async_computation | async-start | bytes 2097152 | tf_op jit(solution)/shard_map/all_to_all | solution.py:186
  94.6 18.6 %all-to-all-start.1 = ((bf16[16,64,512]{2,1,0:T(8,128)(2,1)}), bf16[16,64,512]{2,1,0:T(8,128)(2,1)S(1)}, u32[]{:S(2)}, u32[]{:S(2)}) async-start(bf16[16,64,512]{2,1,0:T(8,128)(2,1)} %bitcast.11), calls=%async_computation.1 | async-start | bytes 2097152 | tf_op jit(solution)/shard_map/all_to_all | solution.py:221
  98.2 15.4 %copy-start.1 = (bf16[512,256]{1,0:T(8,128)(2,1)S(1)}, bf16[512,256]{1,0:T(8,128)(2,1)}, u32[]{:S(2)}) copy-start(bf16[512,256]{1,0:T(8,128)(2,1)} %param.7) | copy-start | bytes 786436
  174.0 9.5 %collective-permute-start.10 = (bf16[8,64,896]{2,1,0:T(8,128)(2,1)S(1)}, bf16[8,64,896]{2,1,0:T(8,128)(2,1)S(1)}, u32[]{:S(2)}, u32[]{:S(2)}) collective-permute-start(bf16[8,64,896]{2,1,0:T(8,128)(2,1)S(1)} %bitcast.81), channel_id=1, source_target_pairs={{0,8},{8,0},{1,9},{9,1},{2,10},{10,2},{3,11},{11,3},{4,12},{12,4},... | collective-permute-start | bytes 2752520 | tf_op jit(solution)/shard_map/ppermute | solution.py:136
  184.1 2.5 %copy-start = (bf16[2,2,16,16,1024]{4,3,2,1,0:T(8,128)(2,1)S(1)}, bf16[2,2,16,16,1024]{4,3,2,1,0:T(8,128)(2,1)}, u32[]{:S(2)}) copy-start(bf16[2,2,16,16,1024]{4,3,2,1,0:T(8,128)(2,1)} %copy.26) | copy-start | bytes 6291460
